TPU v7x, 32 devices: a whole 2x2x4 slice. The times are simulated.
32 devices in a mesh: section: 4 (over y, core), blk: 8 (over z, x).
Axes of the slice: x: 2, y: 2, z: 4, core: 2. Of those that a mesh axis runs over, the one named last changes fastest.
Arguments:
- residual: float32 [1536, 32, 128], P(('section', 'blk')), may hold values from -6 to 6
- kin_inverse: float32 [1536, 32, 32], P(('section', 'blk'))
- cell_weight: float32 [1536, 128], P(('section', 'blk')), may hold values from 0.5 to 1
- upwind_frac: float32 [1536, 4, 128], P(('section', 'blk')), may hold values from 0.2 to 0.7
- block_level: int32 [1536], P(('section', 'blk')), may hold values from 0 to 5, as said below
- send_in: int32 [32, 5, 8], P(('section', 'blk')), may hold values from 0 to 48, as said below
- send_down: int32 [32, 5, 8], P(('section', 'blk')), may hold values from 0 to 48, as said below
- upwind_slot: int32 [1536, 4], P(('section', 'blk')), may hold values from 0 to 128, as said below
Outputs:
- newton_step: float32 [1536, 32, 128], P(('section', 'blk'))
Inputs may be any that keep to these rules, and one draw needn't show every extreme that they name: `block_level`: on each device the blocks of levels 0 to 5 number 48 * 8 / 24, 6 / 24, 4 / 24, 3 / 24, 2 / 24 and 1 / 24 in some cyclic order of the levels, so one level holds 16 blocks of every device. `send_in`: an entry other than 48 names a block of level l on the sending device, for entry [d, l, i]. About half of the entries are none; for every section and level some device receives a block from every device of its section. `send_down`: as send_in, for the owner i of the next section. The last section sends none; for every other section and level some device of the next section receives a block from every device of the sending section. `upwind_slot`: every source of a block has a lower level than the block (a slot of send level l counts as level l), and a slot that is named holds a block; blocks of level 0 have none.
All inputs are finite; a program needn't handle non-finite values.
Results may differ from a plain program's by a relative error of at most 0.0001.
Values sent between devices are 32-bit elements; how exact they have to be, the bound alone decides.
No kernel may reach another device: no remote copies, remote signals or barrier semaphores. Data moves between devices by JAX's collectives and lax.ppermute only.
A program may use at most 64 MiB of HBM per device.

v0:
```python
import functools

import jax
import jax.numpy as jnp
from jax import lax
from jax.experimental import pallas as pl
from jax.experimental.pallas import tpu as pltpu
from jax.sharding import PartitionSpec as P


def split_of(groups):
    columns = max(c for c in range(1, groups + 1) if groups % c == 0 and c * c <= groups)
    return groups // columns, columns


def stepped(row, step, rows, back=False):
    if rows & (rows - 1) == 0:
        return row ^ step
    return (row + (rows - step if back else step)) % rows


def moved(value, sections, rows, columns, steps):
    groups = rows * columns
    pairs = []
    for section in range(sections):
        for row in range(rows):
            for column in range(columns):
                target = stepped(row, steps[1], rows) * columns + (column + steps[2]) % columns
                below = (section + steps[0]) % sections
                pairs.append((section * groups + row * columns + column, below * groups + target))
    return lax.ppermute(value, ("section", "blk"), pairs)


def halves_of(rows):
    return rows // 2 if rows > 1 and rows & (rows - 1) == 0 else rows


def last_steps(rows, columns):
    half = halves_of(rows)
    across = [(row, 0) for row in range(rows - 1, half - 1, -1)]
    aside = [(row, column) for row in range(half - 1, -1, -1) for column in range(1, columns)]
    return across + aside + [(row, 0) for row in range(half - 1, 0, -1)]


def wrapped(value, count):
    return jnp.where(value >= count, value - count, value)


def sort_blocks(blocks, levels, plan):
    stride = blocks + 1
    for level in range(plan.shape[0] // stride):
        plan[level * stride + blocks] = 0

    def place(block, carry):
        first = levels[block] * stride
        count = plan[first + blocks]
        plan[first + count] = block
        plan[first + blocks] = count + 1
        return carry

    lax.fori_loop(0, blocks, place, 0)


def solve_blocks(level, blocks, plan, inflow_of, kin, weight, pool):
    first = level * (blocks + 1)
    count = plan[first + blocks]
    ids = [plan[first + jnp.minimum(i, count - 1)] for i in range(blocks * 8 // 24)]
    solved = []
    for block in ids:
        mixed = jnp.dot(
            kin[block], inflow_of(block), precision=lax.Precision.HIGHEST, preferred_element_type=jnp.float32
        )
        solved.append(weight[pl.ds(block, 1), :] * mixed)
    for block, value in zip(ids, solved):
        pool[block] = value


def fill_sends(level, rows, columns, blocks, peers, downs, pool, outs):
    here = lax.axis_index("blk")
    row, column = here // columns, lax.rem(here, columns)
    ends = lax.axis_index("section") == lax.axis_size("section") - 1
    half = halves_of(rows)
    for row_step in range(rows):
        to_row = stepped(row, row_step, rows)
        for column_step in range(columns):
            target = to_row * columns + wrapped(column + column_step, columns)
            outs[column_step][row_step] = pool[jnp.where(ends, blocks, downs[level, 0, target])]
            part = outs[columns + row_step // half]
            part[row_step % half * columns + column_step] = pool[peers[level, 0, target]]


def first_level(rows, columns, *refs):
    refs = list(refs)
    levels_in, kin_in, residual_in, weight_in, peers_in, downs_in, slots_in, frac_in = (refs.pop(0) for _ in range(8))
    pool, kin, plan, peers_out, downs_out, slots_out, residual, weight, frac = (refs.pop(0) for _ in range(9))
    outs = [refs.pop(0) for _ in range(columns + rows // halves_of(rows))]
    levels, kin_here, peers, downs, sems = refs
    pairs = [(levels_in, levels), (kin_in, kin_here), (residual_in, residual), (weight_in, weight)]
    pairs += [(peers_in, peers), (downs_in, downs)]
    pairs += [(peers_in, peers_out), (downs_in, downs_out), (slots_in, slots_out), (frac_in, frac)]
    copies = [pltpu.make_async_copy(source, target, sems.at[i]) for i, (source, target) in enumerate(pairs)]
    for copy in copies:
        copy.start()
    blocks = residual.shape[0]
    pool[blocks] = jnp.zeros(pool.shape[1:], pool.dtype)
    copies[0].wait()
    sort_blocks(blocks, levels, plan)
    copies[1].wait()
    for i in range(kin.shape[1]):
        kin[:, i, :] = jnp.transpose(kin_here[i])
    for copy in copies[2:6]:
        copy.wait()

    solve_blocks(0, blocks, plan, lambda block: residual[block], kin, weight, pool)
    fill_sends(0, rows, columns, blocks, peers, downs, pool, outs)
    for copy in copies[6:]:
        copy.wait()


def later_level(level, rows, columns, plan, peers, downs, slots, residual, weight, frac, kin, *refs):
    refs = list(refs)
    half, steps = halves_of(rows), last_steps(rows, columns)
    arrived = {step: refs.pop(0) for step in steps}
    from_above = [refs.pop(0) for _ in range(columns)]
    from_halves = [refs.pop(0) for _ in range(rows // half)]
    refs.pop(0)
    pool = refs.pop(0)
    outs = refs
    blocks, upw = residual.shape[0], slots.shape[0]
    rounds, groups = peers.shape[0], rows * columns
    here = lax.axis_index("blk")
    row, column = here // columns, lax.rem(here, columns)
    peers_first = blocks + 1 + (level - 1) * groups
    downs_first = peers_first + rounds * groups
    for row_step in range(rows):
        from_row = stepped(row, row_step, rows, back=True)
        for column_step in range(columns):
            source = from_row * columns + wrapped(column + columns - column_step, columns)
            down = arrived[row_step, 0].at[column_step] if row_step else from_above[column_step].at[0]
            at_half, rest = row_step // half, row_step % half
            if rest or column_step:
                peer = arrived[rest, column_step].at[at_half if column_step else columns + at_half]
            else:
                peer = from_halves[at_half].at[0]
            pool[downs_first + source] = down[...]
            pool[peers_first + source] = peer[...]

    def inflow_of(block):
        inflow = residual[block]
        parts = frac[block]
        for k in range(upw):
            inflow = inflow + parts[k : k + 1, :] * pool[slots[k, block]]
        return inflow

    solve_blocks(level, blocks, plan, inflow_of, kin, weight, pool)
    if level < rounds:
        fill_sends(level, rows, columns, blocks, peers, downs, pool, outs)
    else:
        outs[0][...] = pool[pl.ds(0, blocks)]


def shards(
    residual, kin_inverse, cell_weight, upwind_frac, block_level, send_in, send_down, upwind_slot
):
    blocks, species, cells = residual.shape
    sections, groups = lax.axis_size("section"), lax.axis_size("blk")
    rows, columns = split_of(groups)
    rounds = send_in.shape[1]
    peers = send_in.transpose(1, 0, 2)
    downs = send_down.transpose(1, 0, 2)
    slots = upwind_slot.transpose(1, 0)
    kin_turned = kin_inverse.transpose(1, 2, 0)
    smem = pl.BlockSpec(memory_space=pltpu.SMEM)
    vmem = pl.BlockSpec(memory_space=pltpu.VMEM)
    hbm = pl.BlockSpec(memory_space=pltpu.HBM)
    params = pltpu.CompilerParams(vmem_limit_bytes=40 * 1024 * 1024)
    pool_shape = jax.ShapeDtypeStruct((blocks + 1 + 2 * rounds * groups, species, cells), jnp.float32)
    kin_shape = jax.ShapeDtypeStruct((blocks, species, species), jnp.float32)
    half = halves_of(rows)
    send_shapes = [jax.ShapeDtypeStruct((rows, species, cells), jnp.float32)] * columns
    send_shapes += [jax.ShapeDtypeStruct((half * columns, species, cells), jnp.float32)] * (rows // half)
    to_first = (block_level, kin_turned, residual, cell_weight, peers, downs, slots, upwind_frac)
    held = (peers, downs, slots, residual, cell_weight, upwind_frac)
    held_shapes = [jax.ShapeDtypeStruct(((rounds + 1) * (blocks + 1),), jnp.int32)]
    held_shapes += [jax.ShapeDtypeStruct(x.shape, x.dtype) for x in held]
    pool, kin, *outs = pl.pallas_call(
        functools.partial(first_level, rows, columns),
        in_specs=[hbm] * len(to_first),
        out_specs=[vmem, vmem, smem] + [vmem] * (len(held) + len(send_shapes)),
        out_shape=[pool_shape, kin_shape] + held_shapes + send_shapes,
        scratch_shapes=[
            pltpu.SMEM(block_level.shape, jnp.int32),
            pltpu.VMEM(kin_turned.shape, jnp.float32),
            pltpu.SMEM(peers.shape, jnp.int32),
            pltpu.SMEM(downs.shape, jnp.int32),
            pltpu.SemaphoreType.DMA((10,)),
        ],
        compiler_params=params,
        name="first_level",
    )(*(pltpu.with_memory_space_constraint(x, pltpu.HBM) for x in to_first))
    held, outs = outs[: len(held_shapes)], outs[len(held_shapes) :]
    for level in range(1, rounds + 1):
        from_halves = outs[columns:]
        if half < rows:
            from_halves[1] = moved(from_halves[1], sections, rows, columns, (0, half, 0))
        from_above = [moved(outs[c], sections, rows, columns, (1, 0, c)) for c in range(columns)]
        arrived = []
        for row, column in last_steps(rows, columns):
            part = [] if column else [value[row] for value in from_above]
            if row < half:
                part += [value[row * columns + column] for value in from_halves]
            arrived.append(moved(jnp.stack(part), sections, rows, columns, (0, row, column)))
        if level < rounds:
            out_shapes = send_shapes
        else:
            out_shapes = [jax.ShapeDtypeStruct(residual.shape, residual.dtype)]
        operands = held + [kin] + arrived + from_above + from_halves + [pool]
        pool, *outs = pl.pallas_call(
            functools.partial(later_level, level, rows, columns),
            in_specs=[smem] * 4 + [vmem] * (len(operands) - 4),
            out_specs=[vmem] * (1 + len(out_shapes)),
            out_shape=[pool_shape] + out_shapes,
            input_output_aliases={len(operands) - 1: 0},
            compiler_params=params,
            name="later_level",
        )(*operands)
    return outs[0]


def solution(mesh):
    return jax.shard_map(
        shards,
        mesh=mesh,
        in_specs=(
            P(("section", "blk"), None, None),
            P(("section", "blk"), None, None),
            P(("section", "blk"), None),
            P(("section", "blk"), None, None),
            P(("section", "blk")),
            P(("section", "blk"), None, None),
            P(("section", "blk"), None, None),
            P(("section", "blk"), None),
        ),
        out_specs=P(("section", "blk"), None, None),
        check_vma=False,
    )
```

profile of v0, /device:TPU:0, one launch (start us, length us, event | category | flops | bytes accessed | tf_op | source)
XLA Modules:
  0.0 85.8 jit_solution(17062245441557426047)
XLA Ops:
  0.0 3.1 %first_level.1 = (f32[129,32,128]{2,1,0:T(8,128)S(1)}, f32[48,32,32]{2,1,0:T(8,128)S(1)}, s32[294]{0:T(512)S(1)}, s32[5,1,8]{2,1,0:T(1,128)S(1)}, s32[5,1,8]{2,1...) custom-call(s32[48]{0:T(128)} %refs_0_.1, ...), custom_call_target="tpu_custom_call" | custom-call | tf_op jit(solution)/shard_map/first_level/pallas_call | solution.py:186
  3.6 3.7 %collective-permute-start.1 = (f32[4,32,128]{2,1,0:T(8,128)S(1)}, f32[4,32,128]{2,1,0:T(8,128)S(1)}, u32[]{:S(2)}, u32[]{:S(2)}) collective-permute-start(f32[4,32,128]{2,1,0:T(8,128)S(1)} %get-tuple-element.48), channel_id=1, source_target_pairs={{0,9},{1,8},{2,11},{3,10},{4,13},{5,12},{6,15},{7,14},{8,17},{9,16... | collective-permute-start | bytes 196616 | tf_op jit(solution)/shard_map/ppermute | solution.py:31
  7.4 2.6 %collective-permute-start.4 = (f32[4,32,128]{2,1,0:T(8,128)S(1)}, f32[4,32,128]{2,1,0:T(8,128)S(1)}, u32[]{:S(2)}, u32[]{:S(2)}) collective-permute-start(f32[4,32,128]{2,1,0:T(8,128)S(1)} %get-tuple-element.50), channel_id=1, source_target_pairs={{0,4},{1,5},{2,6},{3,7},{4,0},{5,1},{6,2},{7,3},{8,12},{9,13},{10,... | collective-permute-start | bytes 196616 | tf_op jit(solution)/shard_map/ppermute | solution.py:31
  10.0 3.0 %collective-permute-start.2 = (f32[2,32,128]{2,1,0:T(8,128)S(1)}, f32[2,32,128]{2,1,0:T(8,128)S(1)}, u32[]{:S(2)}, u32[]{:S(2)}) collective-permute-start(f32[2,32,128]{2,1,0:T(8,128)S(1)} %pad_maximum_fusion.5), channel_id=1, source_target_pairs={{0,6},{1,7},{2,4},{3,5},{4,2},{5,3},{6,0},{7,1},{8,14},{9,15},{10,... | collective-permute-start | bytes 98312 | tf_op jit(solution)/shard_map/ppermute | solution.py:31
  14.8 1.3 %collective-permute-start.7 = (f32[4,32,128]{2,1,0:T(8,128)S(1)}, f32[4,32,128]{2,1,0:T(8,128)S(1)}, u32[]{:S(2)}, u32[]{:S(2)}) collective-permute-start(f32[4,32,128]{2,1,0:T(8,128)S(1)} %pad_maximum_fusion), channel_id=1, source_target_pairs={{0,2},{1,3},{2,0},{3,1},{4,6},{5,7},{6,4},{7,5},{8,10},{9,11},{10,... | collective-permute-start | bytes 196616 | tf_op jit(solution)/shard_map/ppermute | solution.py:31
  16.1 1.5 %collective-permute-start.6 = (f32[2,32,128]{2,1,0:T(8,128)S(1)}, f32[2,32,128]{2,1,0:T(8,128)S(1)}, u32[]{:S(2)}, u32[]{:S(2)}) collective-permute-start(f32[2,32,128]{2,1,0:T(8,128)S(1)} %pad_maximum_fusion.8), channel_id=1, source_target_pairs={{0,1},{1,0},{2,3},{3,2},{4,5},{5,4},{6,7},{7,6},{8,9},{9,8},{10,11... | collective-permute-start | bytes 98312 | tf_op jit(solution)/shard_map/ppermute | solution.py:31
  17.8 1.4 %collective-permute-done.5.refs_2_ = f32[2,32,128]{2,1,0:T(8,128)S(1)} collective-permute-done((f32[2,32,128]{2,1,0:T(8,128)S(1)}, f32[2,32,128]{2,1,0:T(8,128)S(1)}, u32[]{:S(2)}, u32[]{:S(2)}) %collective-permute-start.5) | collective-permute-done | bytes 32800 | tf_op jit(solution)/shard_map/ppermute | solution.py:31
  20.0 1.2 %later_level.5 = (f32[129,32,128]{2,1,0:T(8,128)S(1)}, f32[4,32,128]{2,1,0:T(8,128)S(1)}, f32[4,32,128]{2,1,0:T(8,128)S(1)}, f32[4,32,128]{2,1,0:T(8,128)S(1)}, f32[4,32,128]{2,1,0:T(8,128)S(1)}) custom-call(s32[294]{0:T(512)S(1)} %get-tuple-element.39.plan, s32[5,1,8]{2,1,0:T(1,128)S(1)} %get-tuple-element.40.peers, ...), custom_call_target="tpu_custom_call", output_to_operand_aliasing={{0}: (17, {})} | custom-call | tf_op jit(solution)/shard_map/later_level/pallas_call | solution.py:218
  21.3 1.7 %collective-permute-start.9 = (f32[4,32,128]{2,1,0:T(8,128)S(1)}, f32[4,32,128]{2,1,0:T(8,128)S(1)}, u32[]{:S(2)}, u32[]{:S(2)}) collective-permute-start(f32[4,32,128]{2,1,0:T(8,128)S(1)} %get-tuple-element.53), channel_id=1, source_target_pairs={{0,9},{1,8},{2,11},{3,10},{4,13},{5,12},{6,15},{7,14},{8,17},{9,16... | collective-permute-start | bytes 196616 | tf_op jit(solution)/shard_map/ppermute | solution.py:31
  23.0 2.9 %collective-permute-start.12 = (f32[4,32,128]{2,1,0:T(8,128)S(1)}, f32[4,32,128]{2,1,0:T(8,128)S(1)}, u32[]{:S(2)}, u32[]{:S(2)}) collective-permute-start(f32[4,32,128]{2,1,0:T(8,128)S(1)} %get-tuple-element.55), channel_id=1, source_target_pairs={{0,4},{1,5},{2,6},{3,7},{4,0},{5,1},{6,2},{7,3},{8,12},{9,13},{10,... | collective-permute-start | bytes 196616 | tf_op jit(solution)/shard_map/ppermute | solution.py:31
  26.0 3.8 %collective-permute-start.10 = (f32[2,32,128]{2,1,0:T(8,128)S(1)}, f32[2,32,128]{2,1,0:T(8,128)S(1)}, u32[]{:S(2)}, u32[]{:S(2)}) collective-permute-start(f32[2,32,128]{2,1,0:T(8,128)S(1)} %pad_maximum_fusion.9), channel_id=1, source_target_pairs={{0,6},{1,7},{2,4},{3,5},{4,2},{5,3},{6,0},{7,1},{8,14},{9,15},{10,... | collective-permute-start | bytes 98312 | tf_op jit(solution)/shard_map/ppermute | solution.py:31
  29.8 1.7 %collective-permute-start.13 = (f32[2,32,128]{2,1,0:T(8,128)S(1)}, f32[2,32,128]{2,1,0:T(8,128)S(1)}, u32[]{:S(2)}, u32[]{:S(2)}) collective-permute-start(f32[2,32,128]{2,1,0:T(8,128)S(1)} %pad_maximum_fusion.11), channel_id=1, source_target_pairs={{0,3},{1,2},{2,1},{3,0},{4,7},{5,6},{6,5},{7,4},{8,11},{9,10},{10,... | collective-permute-start | bytes 98312 | tf_op jit(solution)/shard_map/ppermute | solution.py:31
  33.4 1.2 %collective-permute-done.11.refs_1_ = f32[2,32,128]{2,1,0:T(8,128)S(1)} collective-permute-done((f32[2,32,128]{2,1,0:T(8,128)S(1)}, f32[2,32,128]{2,1,0:T(8,128)S(1)}, u32[]{:S(2)}, u32[]{:S(2)}) %collective-permute-start.11) | collective-permute-done | bytes 32800 | tf_op jit(solution)/shard_map/ppermute | solution.py:31
  35.0 1.5 %collective-permute-done.14.refs_3_ = f32[2,32,128]{2,1,0:T(8,128)S(1)} collective-permute-done((f32[2,32,128]{2,1,0:T(8,128)S(1)}, f32[2,32,128]{2,1,0:T(8,128)S(1)}, u32[]{:S(2)}, u32[]{:S(2)}) %collective-permute-start.14) | collective-permute-done | bytes 32800 | tf_op jit(solution)/shard_map/ppermute | solution.py:31
  36.5 1.2 %later_level.6 = (f32[129,32,128]{2,1,0:T(8,128)S(1)}, f32[4,32,128]{2,1,0:T(8,128)S(1)}, f32[4,32,128]{2,1,0:T(8,128)S(1)}, f32[4,32,128]{2,1,0:T(8,128)S(1)}, f32[4,32,128]{2,1,0:T(8,128)S(1)}) custom-call(s32[294]{0:T(512)S(1)} %get-tuple-element.39.plan, s32[5,1,8]{2,1,0:T(1,128)S(1)} %get-tuple-element.40.peers, ...), custom_call_target="tpu_custom_call", output_to_operand_aliasing={{0}: (17, {})} | custom-call | tf_op jit(solution)/shard_map/later_level/pallas_call | solution.py:218
  37.8 1.6 %collective-permute-start.17 = (f32[4,32,128]{2,1,0:T(8,128)S(1)}, f32[4,32,128]{2,1,0:T(8,128)S(1)}, u32[]{:S(2)}, u32[]{:S(2)}) collective-permute-start(f32[4,32,128]{2,1,0:T(8,128)S(1)} %get-tuple-element.58), channel_id=1, source_target_pairs={{0,9},{1,8},{2,11},{3,10},{4,13},{5,12},{6,15},{7,14},{8,17},{9,16... | collective-permute-start | bytes 196616 | tf_op jit(solution)/shard_map/ppermute | solution.py:31
  39.4 2.3 %collective-permute-start.20 = (f32[4,32,128]{2,1,0:T(8,128)S(1)}, f32[4,32,128]{2,1,0:T(8,128)S(1)}, u32[]{:S(2)}, u32[]{:S(2)}) collective-permute-start(f32[4,32,128]{2,1,0:T(8,128)S(1)} %get-tuple-element.60), channel_id=1, source_target_pairs={{0,4},{1,5},{2,6},{3,7},{4,0},{5,1},{6,2},{7,3},{8,12},{9,13},{10,... | collective-permute-start | bytes 196616 | tf_op jit(solution)/shard_map/ppermute | solution.py:31
  42.4 3.0 %collective-permute-start.18 = (f32[2,32,128]{2,1,0:T(8,128)S(1)}, f32[2,32,128]{2,1,0:T(8,128)S(1)}, u32[]{:S(2)}, u32[]{:S(2)}) collective-permute-start(f32[2,32,128]{2,1,0:T(8,128)S(1)} %pad_maximum_fusion.13), channel_id=1, source_target_pairs={{0,6},{1,7},{2,4},{3,5},{4,2},{5,3},{6,0},{7,1},{8,14},{9,15},{10,... | collective-permute-start | bytes 98312 | tf_op jit(solution)/shard_map/ppermute | solution.py:31
  45.6 1.7 %collective-permute-start.21 = (f32[2,32,128]{2,1,0:T(8,128)S(1)}, f32[2,32,128]{2,1,0:T(8,128)S(1)}, u32[]{:S(2)}, u32[]{:S(2)}) collective-permute-start(f32[2,32,128]{2,1,0:T(8,128)S(1)} %pad_maximum_fusion.15), channel_id=1, source_target_pairs={{0,3},{1,2},{2,1},{3,0},{4,7},{5,6},{6,5},{7,4},{8,11},{9,10},{10,... | collective-permute-start | bytes 98312 | tf_op jit(solution)/shard_map/ppermute | solution.py:31
  49.1 1.4 %collective-permute-done.19.refs_1_ = f32[2,32,128]{2,1,0:T(8,128)S(1)} collective-permute-done((f32[2,32,128]{2,1,0:T(8,128)S(1)}, f32[2,32,128]{2,1,0:T(8,128)S(1)}, u32[]{:S(2)}, u32[]{:S(2)}) %collective-permute-start.19) | collective-permute-done | bytes 32800 | tf_op jit(solution)/shard_map/ppermute | solution.py:31
  51.9 1.2 %later_level.7 = (f32[129,32,128]{2,1,0:T(8,128)S(1)}, f32[4,32,128]{2,1,0:T(8,128)S(1)}, f32[4,32,128]{2,1,0:T(8,128)S(1)}, f32[4,32,128]{2,1,0:T(8,128)S(1)}, f32[4,32,128]{2,1,0:T(8,128)S(1)}) custom-call(s32[294]{0:T(512)S(1)} %get-tuple-element.39.plan, s32[5,1,8]{2,1,0:T(1,128)S(1)} %get-tuple-element.40.peers, ...), custom_call_target="tpu_custom_call", output_to_operand_aliasing={{0}: (17, {})} | custom-call | tf_op jit(solution)/shard_map/later_level/pallas_call | solution.py:218
  53.3 2.0 %collective-permute-start.25 = (f32[4,32,128]{2,1,0:T(8,128)S(1)}, f32[4,32,128]{2,1,0:T(8,128)S(1)}, u32[]{:S(2)}, u32[]{:S(2)}) collective-permute-start(f32[4,32,128]{2,1,0:T(8,128)S(1)} %get-tuple-element.63), channel_id=1, source_target_pairs={{0,9},{1,8},{2,11},{3,10},{4,13},{5,12},{6,15},{7,14},{8,17},{9,16... | collective-permute-start | bytes 196616 | tf_op jit(solution)/shard_map/ppermute | solution.py:31
  55.3 2.5 %collective-permute-start.28 = (f32[4,32,128]{2,1,0:T(8,128)S(1)}, f32[4,32,128]{2,1,0:T(8,128)S(1)}, u32[]{:S(2)}, u32[]{:S(2)}) collective-permute-start(f32[4,32,128]{2,1,0:T(8,128)S(1)} %get-tuple-element.65), channel_id=1, source_target_pairs={{0,4},{1,5},{2,6},{3,7},{4,0},{5,1},{6,2},{7,3},{8,12},{9,13},{10,... | collective-permute-start | bytes 196616 | tf_op jit(solution)/shard_map/ppermute | solution.py:31
  57.9 3.1 %collective-permute-start.26 = (f32[2,32,128]{2,1,0:T(8,128)S(1)}, f32[2,32,128]{2,1,0:T(8,128)S(1)}, u32[]{:S(2)}, u32[]{:S(2)}) collective-permute-start(f32[2,32,128]{2,1,0:T(8,128)S(1)} %pad_maximum_fusion.17), channel_id=1, source_target_pairs={{0,6},{1,7},{2,4},{3,5},{4,2},{5,3},{6,0},{7,1},{8,14},{9,15},{10,... | collective-permute-start | bytes 98312 | tf_op jit(solution)/shard_map/ppermute | solution.py:31
  61.5 1.5 %collective-permute-start.29 = (f32[2,32,128]{2,1,0:T(8,128)S(1)}, f32[2,32,128]{2,1,0:T(8,128)S(1)}, u32[]{:S(2)}, u32[]{:S(2)}) collective-permute-start(f32[2,32,128]{2,1,0:T(8,128)S(1)} %pad_maximum_fusion.19), channel_id=1, source_target_pairs={{0,3},{1,2},{2,1},{3,0},{4,7},{5,6},{6,5},{7,4},{8,11},{9,10},{10,... | collective-permute-start | bytes 98312 | tf_op jit(solution)/shard_map/ppermute | solution.py:31
  63.0 1.3 %collective-permute-start.31 = (f32[4,32,128]{2,1,0:T(8,128)S(1)}, f32[4,32,128]{2,1,0:T(8,128)S(1)}, u32[]{:S(2)}, u32[]{:S(2)}) collective-permute-start(f32[4,32,128]{2,1,0:T(8,128)S(1)} %pad_maximum_fusion.3), channel_id=1, source_target_pairs={{0,2},{1,3},{2,0},{3,1},{4,6},{5,7},{6,4},{7,5},{8,10},{9,11},{10,... | collective-permute-start | bytes 196616 | tf_op jit(solution)/shard_map/ppermute | solution.py:31
  68.2 1.2 %later_level.8 = (f32[129,32,128]{2,1,0:T(8,128)S(1)}, f32[4,32,128]{2,1,0:T(8,128)S(1)}, f32[4,32,128]{2,1,0:T(8,128)S(1)}, f32[4,32,128]{2,1,0:T(8,128)S(1)}, f32[4,32,128]{2,1,0:T(8,128)S(1)}) custom-call(s32[294]{0:T(512)S(1)} %get-tuple-element.39.plan, s32[5,1,8]{2,1,0:T(1,128)S(1)} %get-tuple-element.40.peers, ...), custom_call_target="tpu_custom_call", output_to_operand_aliasing={{0}: (17, {})} | custom-call | tf_op jit(solution)/shard_map/later_level/pallas_call | solution.py:218
  69.5 1.4 %collective-permute-start.33 = (f32[4,32,128]{2,1,0:T(8,128)S(1)}, f32[4,32,128]{2,1,0:T(8,128)S(1)}, u32[]{:S(2)}, u32[]{:S(2)}) collective-permute-start(f32[4,32,128]{2,1,0:T(8,128)S(1)} %get-tuple-element.68), channel_id=1, source_target_pairs={{0,9},{1,8},{2,11},{3,10},{4,13},{5,12},{6,15},{7,14},{8,17},{9,16... | collective-permute-start | bytes 196616 | tf_op jit(solution)/shard_map/ppermute | solution.py:31
  71.0 2.9 %collective-permute-start.36 = (f32[4,32,128]{2,1,0:T(8,128)S(1)}, f32[4,32,128]{2,1,0:T(8,128)S(1)}, u32[]{:S(2)}, u32[]{:S(2)}) collective-permute-start(f32[4,32,128]{2,1,0:T(8,128)S(1)} %get-tuple-element.70), channel_id=1, source_target_pairs={{0,4},{1,5},{2,6},{3,7},{4,0},{5,1},{6,2},{7,3},{8,12},{9,13},{10,... | collective-permute-start | bytes 196616 | tf_op jit(solution)/shard_map/ppermute | solution.py:31
  74.2 3.0 %collective-permute-start.34 = (f32[2,32,128]{2,1,0:T(8,128)S(1)}, f32[2,32,128]{2,1,0:T(8,128)S(1)}, u32[]{:S(2)}, u32[]{:S(2)}) collective-permute-start(f32[2,32,128]{2,1,0:T(8,128)S(1)} %pad_maximum_fusion.21), channel_id=1, source_target_pairs={{0,6},{1,7},{2,4},{3,5},{4,2},{5,3},{6,0},{7,1},{8,14},{9,15},{10,... | collective-permute-start | bytes 98312 | tf_op jit(solution)/shard_map/ppermute | solution.py:31
  77.4 1.5 %collective-permute-start.37 = (f32[2,32,128]{2,1,0:T(8,128)S(1)}, f32[2,32,128]{2,1,0:T(8,128)S(1)}, u32[]{:S(2)}, u32[]{:S(2)}) collective-permute-start(f32[2,32,128]{2,1,0:T(8,128)S(1)} %pad_maximum_fusion.23), channel_id=1, source_target_pairs={{0,3},{1,2},{2,1},{3,0},{4,7},{5,6},{6,5},{7,4},{8,11},{9,10},{10,... | collective-permute-start | bytes 98312 | tf_op jit(solution)/shard_map/ppermute | solution.py:31
  83.7 2.1 %later_level.9 = (f32[129,32,128]{2,1,0:T(8,128)S(1)}, f32[48,32,128]{2,1,0:T(8,128)}) custom-call(s32[294]{0:T(512)S(1)} %get-tuple-element.39.plan, s32[5,1,8]{2,1,0:T(1,128)S(1)} %get-tuple-element.40.peers, s32[5,1,8]{2,1,0:T(1,128)S(1)} %get-tuple-element.41.downs, s32[4,48]{1,0:T(4,128)S(1)} %get-tuple-element.42.slots, ...), custom_call_target="tpu_custom_call", output_to_operand_aliasing={{0}: (17, {})} | custom-call | tf_op jit(solution)/shard_map/later_level/pallas_call | solution.py:218
  (99 shorter events, 19.9 us)
Async XLA Ops:
  3.1 6.8 %collective-permute-start = (f32[4,32,128]{2,1,0:T(8,128)S(1)}, f32[4,32,128]{2,1,0:T(8,128)S(1)}, u32[]{:S(2)}, u32[]{:S(2)}) collective-permute-start(f32[4,32,128]{2,1,0:T(8,128)S(1)} %get-tuple-element.47), channel_id=1, source_target_pairs={{0,8},{1,9},{2,10},{3,11},{4,12},{5,13},{6,14},{7,15},{8,16},{9,17... | collective-permute-start | bytes 196616 | tf_op jit(solution)/shard_map/ppermute | solution.py:31
  3.6 6.3 %collective-permute-start.1 = (f32[4,32,128]{2,1,0:T(8,128)S(1)}, f32[4,32,128]{2,1,0:T(8,128)S(1)}, u32[]{:S(2)}, u32[]{:S(2)}) collective-permute-start(f32[4,32,128]{2,1,0:T(8,128)S(1)} %get-tuple-element.48), channel_id=1, source_target_pairs={{0,9},{1,8},{2,11},{3,10},{4,13},{5,12},{6,15},{7,14},{8,17},{9,16... | collective-permute-start | bytes 196616 | tf_op jit(solution)/shard_map/ppermute | solution.py:31
  7.4 6.7 %collective-permute-start.4 = (f32[4,32,128]{2,1,0:T(8,128)S(1)}, f32[4,32,128]{2,1,0:T(8,128)S(1)}, u32[]{:S(2)}, u32[]{:S(2)}) collective-permute-start(f32[4,32,128]{2,1,0:T(8,128)S(1)} %get-tuple-element.50), channel_id=1, source_target_pairs={{0,4},{1,5},{2,6},{3,7},{4,0},{5,1},{6,2},{7,3},{8,12},{9,13},{10,... | collective-permute-start | bytes 196616 | tf_op jit(solution)/shard_map/ppermute | solution.py:31
  10.0 7.6 %collective-permute-start.2 = (f32[2,32,128]{2,1,0:T(8,128)S(1)}, f32[2,32,128]{2,1,0:T(8,128)S(1)}, u32[]{:S(2)}, u32[]{:S(2)}) collective-permute-start(f32[2,32,128]{2,1,0:T(8,128)S(1)} %pad_maximum_fusion.5), channel_id=1, source_target_pairs={{0,6},{1,7},{2,4},{3,5},{4,2},{5,3},{6,0},{7,1},{8,14},{9,15},{10,... | collective-permute-start | bytes 98312 | tf_op jit(solution)/shard_map/ppermute | solution.py:31
  13.0 4.8 %collective-permute-start.3 = (f32[2,32,128]{2,1,0:T(8,128)S(1)}, f32[2,32,128]{2,1,0:T(8,128)S(1)}, u32[]{:S(2)}, u32[]{:S(2)}) collective-permute-start(f32[2,32,128]{2,1,0:T(8,128)S(1)} %pad_maximum_fusion.6), channel_id=1, source_target_pairs={{0,4},{1,5},{2,6},{3,7},{4,0},{5,1},{6,2},{7,3},{8,12},{9,13},{10,... | collective-permute-start | bytes 98312 | tf_op jit(solution)/shard_map/ppermute | solution.py:31
  14.1 5.1 %collective-permute-start.5 = (f32[2,32,128]{2,1,0:T(8,128)S(1)}, f32[2,32,128]{2,1,0:T(8,128)S(1)}, u32[]{:S(2)}, u32[]{:S(2)}) collective-permute-start(f32[2,32,128]{2,1,0:T(8,128)S(1)} %pad_maximum_fusion.7), channel_id=1, source_target_pairs={{0,3},{1,2},{2,1},{3,0},{4,7},{5,6},{6,5},{7,4},{8,11},{9,10},{10,... | collective-permute-start | bytes 98312 | tf_op jit(solution)/shard_map/ppermute | solution.py:31
  14.8 5.2 %collective-permute-start.7 = (f32[4,32,128]{2,1,0:T(8,128)S(1)}, f32[4,32,128]{2,1,0:T(8,128)S(1)}, u32[]{:S(2)}, u32[]{:S(2)}) collective-permute-start(f32[4,32,128]{2,1,0:T(8,128)S(1)} %pad_maximum_fusion), channel_id=1, source_target_pairs={{0,2},{1,3},{2,0},{3,1},{4,6},{5,7},{6,4},{7,5},{8,10},{9,11},{10,... | collective-permute-start | bytes 196616 | tf_op jit(solution)/shard_map/ppermute | solution.py:31
  21.2 4.7 %collective-permute-start.8 = (f32[4,32,128]{2,1,0:T(8,128)S(1)}, f32[4,32,128]{2,1,0:T(8,128)S(1)}, u32[]{:S(2)}, u32[]{:S(2)}) collective-permute-start(f32[4,32,128]{2,1,0:T(8,128)S(1)} %get-tuple-element.52), channel_id=1, source_target_pairs={{0,8},{1,9},{2,10},{3,11},{4,12},{5,13},{6,14},{7,15},{8,16},{9,17... | collective-permute-start | bytes 196616 | tf_op jit(solution)/shard_map/ppermute | solution.py:31
  21.3 4.6 %collective-permute-start.9 = (f32[4,32,128]{2,1,0:T(8,128)S(1)}, f32[4,32,128]{2,1,0:T(8,128)S(1)}, u32[]{:S(2)}, u32[]{:S(2)}) collective-permute-start(f32[4,32,128]{2,1,0:T(8,128)S(1)} %get-tuple-element.53), channel_id=1, source_target_pairs={{0,9},{1,8},{2,11},{3,10},{4,13},{5,12},{6,15},{7,14},{8,17},{9,16... | collective-permute-start | bytes 196616 | tf_op jit(solution)/shard_map/ppermute | solution.py:31
  23.0 6.7 %collective-permute-start.12 = (f32[4,32,128]{2,1,0:T(8,128)S(1)}, f32[4,32,128]{2,1,0:T(8,128)S(1)}, u32[]{:S(2)}, u32[]{:S(2)}) collective-permute-start(f32[4,32,128]{2,1,0:T(8,128)S(1)} %get-tuple-element.55), channel_id=1, source_target_pairs={{0,4},{1,5},{2,6},{3,7},{4,0},{5,1},{6,2},{7,3},{8,12},{9,13},{10,... | collective-permute-start | bytes 196616 | tf_op jit(solution)/shard_map/ppermute | solution.py:31
  26.0 7.4 %collective-permute-start.10 = (f32[2,32,128]{2,1,0:T(8,128)S(1)}, f32[2,32,128]{2,1,0:T(8,128)S(1)}, u32[]{:S(2)}, u32[]{:S(2)}) collective-permute-start(f32[2,32,128]{2,1,0:T(8,128)S(1)} %pad_maximum_fusion.9), channel_id=1, source_target_pairs={{0,6},{1,7},{2,4},{3,5},{4,2},{5,3},{6,0},{7,1},{8,14},{9,15},{10,... | collective-permute-start | bytes 98312 | tf_op jit(solution)/shard_map/ppermute | solution.py:31
  29.8 4.8 %collective-permute-start.11 = (f32[2,32,128]{2,1,0:T(8,128)S(1)}, f32[2,32,128]{2,1,0:T(8,128)S(1)}, u32[]{:S(2)}, u32[]{:S(2)}) collective-permute-start(f32[2,32,128]{2,1,0:T(8,128)S(1)} %pad_maximum_fusion.10), channel_id=1, source_target_pairs={{0,4},{1,5},{2,6},{3,7},{4,0},{5,1},{6,2},{7,3},{8,12},{9,13},{10,... | collective-permute-start | bytes 98312 | tf_op jit(solution)/shard_map/ppermute | solution.py:31
  29.8 5.2 %collective-permute-start.13 = (f32[2,32,128]{2,1,0:T(8,128)S(1)}, f32[2,32,128]{2,1,0:T(8,128)S(1)}, u32[]{:S(2)}, u32[]{:S(2)}) collective-permute-start(f32[2,32,128]{2,1,0:T(8,128)S(1)} %pad_maximum_fusion.11), channel_id=1, source_target_pairs={{0,3},{1,2},{2,1},{3,0},{4,7},{5,6},{6,5},{7,4},{8,11},{9,10},{10,... | collective-permute-start | bytes 98312 | tf_op jit(solution)/shard_map/ppermute | solution.py:31
  31.5 5.0 %collective-permute-start.15 = (f32[4,32,128]{2,1,0:T(8,128)S(1)}, f32[4,32,128]{2,1,0:T(8,128)S(1)}, u32[]{:S(2)}, u32[]{:S(2)}) collective-permute-start(f32[4,32,128]{2,1,0:T(8,128)S(1)} %pad_maximum_fusion.1), channel_id=1, source_target_pairs={{0,2},{1,3},{2,0},{3,1},{4,6},{5,7},{6,4},{7,5},{8,10},{9,11},{10,... | collective-permute-start | bytes 196616 | tf_op jit(solution)/shard_map/ppermute | solution.py:31
  37.8 4.6 %collective-permute-start.17 = (f32[4,32,128]{2,1,0:T(8,128)S(1)}, f32[4,32,128]{2,1,0:T(8,128)S(1)}, u32[]{:S(2)}, u32[]{:S(2)}) collective-permute-start(f32[4,32,128]{2,1,0:T(8,128)S(1)} %get-tuple-element.58), channel_id=1, source_target_pairs={{0,9},{1,8},{2,11},{3,10},{4,13},{5,12},{6,15},{7,14},{8,17},{9,16... | collective-permute-start | bytes 196616 | tf_op jit(solution)/shard_map/ppermute | solution.py:31
  39.4 6.2 %collective-permute-start.20 = (f32[4,32,128]{2,1,0:T(8,128)S(1)}, f32[4,32,128]{2,1,0:T(8,128)S(1)}, u32[]{:S(2)}, u32[]{:S(2)}) collective-permute-start(f32[4,32,128]{2,1,0:T(8,128)S(1)} %get-tuple-element.60), channel_id=1, source_target_pairs={{0,4},{1,5},{2,6},{3,7},{4,0},{5,1},{6,2},{7,3},{8,12},{9,13},{10,... | collective-permute-start | bytes 196616 | tf_op jit(solution)/shard_map/ppermute | solution.py:31
  42.4 6.7 %collective-permute-start.18 = (f32[2,32,128]{2,1,0:T(8,128)S(1)}, f32[2,32,128]{2,1,0:T(8,128)S(1)}, u32[]{:S(2)}, u32[]{:S(2)}) collective-permute-start(f32[2,32,128]{2,1,0:T(8,128)S(1)} %pad_maximum_fusion.13), channel_id=1, source_target_pairs={{0,6},{1,7},{2,4},{3,5},{4,2},{5,3},{6,0},{7,1},{8,14},{9,15},{10,... | collective-permute-start | bytes 98312 | tf_op jit(solution)/shard_map/ppermute | solution.py:31
  45.4 5.2 %collective-permute-start.19 = (f32[2,32,128]{2,1,0:T(8,128)S(1)}, f32[2,32,128]{2,1,0:T(8,128)S(1)}, u32[]{:S(2)}, u32[]{:S(2)}) collective-permute-start(f32[2,32,128]{2,1,0:T(8,128)S(1)} %pad_maximum_fusion.14), channel_id=1, source_target_pairs={{0,4},{1,5},{2,6},{3,7},{4,0},{5,1},{6,2},{7,3},{8,12},{9,13},{10,... | collective-permute-start | bytes 98312 | tf_op jit(solution)/shard_map/ppermute | solution.py:31
  45.6 5.5 %collective-permute-start.21 = (f32[2,32,128]{2,1,0:T(8,128)S(1)}, f32[2,32,128]{2,1,0:T(8,128)S(1)}, u32[]{:S(2)}, u32[]{:S(2)}) collective-permute-start(f32[2,32,128]{2,1,0:T(8,128)S(1)} %pad_maximum_fusion.15), channel_id=1, source_target_pairs={{0,3},{1,2},{2,1},{3,0},{4,7},{5,6},{6,5},{7,4},{8,11},{9,10},{10,... | collective-permute-start | bytes 98312 | tf_op jit(solution)/shard_map/ppermute | solution.py:31
  47.2 4.7 %collective-permute-start.23 = (f32[4,32,128]{2,1,0:T(8,128)S(1)}, f32[4,32,128]{2,1,0:T(8,128)S(1)}, u32[]{:S(2)}, u32[]{:S(2)}) collective-permute-start(f32[4,32,128]{2,1,0:T(8,128)S(1)} %pad_maximum_fusion.2), channel_id=1, source_target_pairs={{0,2},{1,3},{2,0},{3,1},{4,6},{5,7},{6,4},{7,5},{8,10},{9,11},{10,... | collective-permute-start | bytes 196616 | tf_op jit(solution)/shard_map/ppermute | solution.py:31
  53.3 4.6 %collective-permute-start.25 = (f32[4,32,128]{2,1,0:T(8,128)S(1)}, f32[4,32,128]{2,1,0:T(8,128)S(1)}, u32[]{:S(2)}, u32[]{:S(2)}) collective-permute-start(f32[4,32,128]{2,1,0:T(8,128)S(1)} %get-tuple-element.63), channel_id=1, source_target_pairs={{0,9},{1,8},{2,11},{3,10},{4,13},{5,12},{6,15},{7,14},{8,17},{9,16... | collective-permute-start | bytes 196616 | tf_op jit(solution)/shard_map/ppermute | solution.py:31
  55.3 6.2 %collective-permute-start.28 = (f32[4,32,128]{2,1,0:T(8,128)S(1)}, f32[4,32,128]{2,1,0:T(8,128)S(1)}, u32[]{:S(2)}, u32[]{:S(2)}) collective-permute-start(f32[4,32,128]{2,1,0:T(8,128)S(1)} %get-tuple-element.65), channel_id=1, source_target_pairs={{0,4},{1,5},{2,6},{3,7},{4,0},{5,1},{6,2},{7,3},{8,12},{9,13},{10,... | collective-permute-start | bytes 196616 | tf_op jit(solution)/shard_map/ppermute | solution.py:31
  57.9 7.1 %collective-permute-start.26 = (f32[2,32,128]{2,1,0:T(8,128)S(1)}, f32[2,32,128]{2,1,0:T(8,128)S(1)}, u32[]{:S(2)}, u32[]{:S(2)}) collective-permute-start(f32[2,32,128]{2,1,0:T(8,128)S(1)} %pad_maximum_fusion.17), channel_id=1, source_target_pairs={{0,6},{1,7},{2,4},{3,5},{4,2},{5,3},{6,0},{7,1},{8,14},{9,15},{10,... | collective-permute-start | bytes 98312 | tf_op jit(solution)/shard_map/ppermute | solution.py:31
  61.1 4.8 %collective-permute-start.27 = (f32[2,32,128]{2,1,0:T(8,128)S(1)}, f32[2,32,128]{2,1,0:T(8,128)S(1)}, u32[]{:S(2)}, u32[]{:S(2)}) collective-permute-start(f32[2,32,128]{2,1,0:T(8,128)S(1)} %pad_maximum_fusion.18), channel_id=1, source_target_pairs={{0,4},{1,5},{2,6},{3,7},{4,0},{5,1},{6,2},{7,3},{8,12},{9,13},{10,... | collective-permute-start | bytes 98312 | tf_op jit(solution)/shard_map/ppermute | solution.py:31
  61.5 5.6 %collective-permute-start.29 = (f32[2,32,128]{2,1,0:T(8,128)S(1)}, f32[2,32,128]{2,1,0:T(8,128)S(1)}, u32[]{:S(2)}, u32[]{:S(2)}) collective-permute-start(f32[2,32,128]{2,1,0:T(8,128)S(1)} %pad_maximum_fusion.19), channel_id=1, source_target_pairs={{0,3},{1,2},{2,1},{3,0},{4,7},{5,6},{6,5},{7,4},{8,11},{9,10},{10,... | collective-permute-start | bytes 98312 | tf_op jit(solution)/shard_map/ppermute | solution.py:31
  63.0 5.2 %collective-permute-start.31 = (f32[4,32,128]{2,1,0:T(8,128)S(1)}, f32[4,32,128]{2,1,0:T(8,128)S(1)}, u32[]{:S(2)}, u32[]{:S(2)}) collective-permute-start(f32[4,32,128]{2,1,0:T(8,128)S(1)} %pad_maximum_fusion.3), channel_id=1, source_target_pairs={{0,2},{1,3},{2,0},{3,1},{4,6},{5,7},{6,4},{7,5},{8,10},{9,11},{10,... | collective-permute-start | bytes 196616 | tf_op jit(solution)/shard_map/ppermute | solution.py:31
  69.5 4.6 %collective-permute-start.33 = (f32[4,32,128]{2,1,0:T(8,128)S(1)}, f32[4,32,128]{2,1,0:T(8,128)S(1)}, u32[]{:S(2)}, u32[]{:S(2)}) collective-permute-start(f32[4,32,128]{2,1,0:T(8,128)S(1)} %get-tuple-element.68), channel_id=1, source_target_pairs={{0,9},{1,8},{2,11},{3,10},{4,13},{5,12},{6,15},{7,14},{8,17},{9,16... | collective-permute-start | bytes 196616 | tf_op jit(solution)/shard_map/ppermute | solution.py:31
  71.0 6.4 %collective-permute-start.36 = (f32[4,32,128]{2,1,0:T(8,128)S(1)}, f32[4,32,128]{2,1,0:T(8,128)S(1)}, u32[]{:S(2)}, u32[]{:S(2)}) collective-permute-start(f32[4,32,128]{2,1,0:T(8,128)S(1)} %get-tuple-element.70), channel_id=1, source_target_pairs={{0,4},{1,5},{2,6},{3,7},{4,0},{5,1},{6,2},{7,3},{8,12},{9,13},{10,... | collective-permute-start | bytes 196616 | tf_op jit(solution)/shard_map/ppermute | solution.py:31
  74.2 6.8 %collective-permute-start.34 = (f32[2,32,128]{2,1,0:T(8,128)S(1)}, f32[2,32,128]{2,1,0:T(8,128)S(1)}, u32[]{:S(2)}, u32[]{:S(2)}) collective-permute-start(f32[2,32,128]{2,1,0:T(8,128)S(1)} %pad_maximum_fusion.21), channel_id=1, source_target_pairs={{0,6},{1,7},{2,4},{3,5},{4,2},{5,3},{6,0},{7,1},{8,14},{9,15},{10,... | collective-permute-start | bytes 98312 | tf_op jit(solution)/shard_map/ppermute | solution.py:31
  77.1 4.9 %collective-permute-start.35 = (f32[2,32,128]{2,1,0:T(8,128)S(1)}, f32[2,32,128]{2,1,0:T(8,128)S(1)}, u32[]{:S(2)}, u32[]{:S(2)}) collective-permute-start(f32[2,32,128]{2,1,0:T(8,128)S(1)} %pad_maximum_fusion.22), channel_id=1, source_target_pairs={{0,4},{1,5},{2,6},{3,7},{4,0},{5,1},{6,2},{7,3},{8,12},{9,13},{10,... | collective-permute-start | bytes 98312 | tf_op jit(solution)/shard_map/ppermute | solution.py:31
  77.4 5.3 %collective-permute-start.37 = (f32[2,32,128]{2,1,0:T(8,128)S(1)}, f32[2,32,128]{2,1,0:T(8,128)S(1)}, u32[]{:S(2)}, u32[]{:S(2)}) collective-permute-start(f32[2,32,128]{2,1,0:T(8,128)S(1)} %pad_maximum_fusion.23), channel_id=1, source_target_pairs={{0,3},{1,2},{2,1},{3,0},{4,7},{5,6},{6,5},{7,4},{8,11},{9,10},{10,... | collective-permute-start | bytes 98312 | tf_op jit(solution)/shard_map/ppermute | solution.py:31
  78.9 4.7 %collective-permute-start.39 = (f32[4,32,128]{2,1,0:T(8,128)S(1)}, f32[4,32,128]{2,1,0:T(8,128)S(1)}, u32[]{:S(2)}, u32[]{:S(2)}) collective-permute-start(f32[4,32,128]{2,1,0:T(8,128)S(1)} %pad_maximum_fusion.4), channel_id=1, source_target_pairs={{0,2},{1,3},{2,0},{3,1},{4,6},{5,7},{6,4},{7,5},{8,10},{9,11},{10,... | collective-permute-start | bytes 196616 | tf_op jit(solution)/shard_map/ppermute | solution.py:31
  (8 other events, 32.5 us)
where the time goes:
time: 85.9 us; the launch traced here: 85.8 us
  starting transfers between devices  58.2 us (68%)
  waiting for transfers between devices  17 us (20%)
  Pallas kernels  10.2 us (12%)
    ppermute x40, starting transfers between devices, moved(): return lax.ppermute(value, ('section', 'blk'), pairs)  58.2 us
    ppermute x40, waiting for transfers between devices, moved(): return lax.ppermute(value, ('section', 'blk'), pairs)  17 us
    pallas_call x5, Pallas kernels, shards(): pl.pallas_call(functools.partial(later_level, level, rows, columns), in_s...  7.07 us
    pallas_call x1, Pallas kernels, shards(): pl.pallas_call(functools.partial(first_level, rows, columns), in_specs=[h...  3.13 us
  transfers between devices with their start and end apart: 40, of which 21 were waited for; matrix products, arithmetic and copies ran while one was open for 0% of the time, Pallas kernels for 0%

commit v1 on v0

--- a/solution.py
+++ b/solution.py
@@ -48,17 +48,21 @@
 
 def sort_blocks(blocks, levels, plan):
     stride = blocks + 1
-    for level in range(plan.shape[0] // stride):
-        plan[level * stride + blocks] = 0
-
-    def place(block, carry):
-        first = levels[block] * stride
-        count = plan[first + blocks]
-        plan[first + count] = block
-        plan[first + blocks] = count + 1
-        return carry
-
-    lax.fori_loop(0, blocks, place, 0)
+    count = plan.shape[0] // stride
+    together = 4 if blocks % 4 == 0 else 1
+
+    def place(step, ends):
+        for i in range(together):
+            block = step * together + i
+            level = levels[block]
+            for end in ends:
+                plan[end] = block
+            ends = tuple(end + jnp.where(level == own, 1, 0) for own, end in enumerate(ends))
+        return ends
+
+    ends = lax.fori_loop(0, blocks // together, place, tuple(jnp.int32(own * stride) for own in range(count)))
+    for own, end in enumerate(ends):
+        plan[own * stride + blocks] = end - own * stride
 
 
 def solve_blocks(level, blocks, plan, inflow_of, kin, weight, pool):

time: 85.9 us -> 85.8 us (level)
  transfers between devices with their start and end apart: 40 -> 40, of which waited for: 21 -> 22; matrix products, arithmetic and copies ran while one was open for 0% -> 0% of each run, Pallas kernels for 0% -> 0%
where the time goes in v1:
time: 85.8 us; the launch traced here: 85.6 us
  starting transfers between devices  58 us (68%)
  waiting for transfers between devices  17.1 us (20%)
  Pallas kernels  10.1 us (12%)
    ppermute x40, starting transfers between devices, moved(): return lax.ppermute(value, ('section', 'blk'), pairs)  58 us
    ppermute x40, waiting for transfers between devices, moved(): return lax.ppermute(value, ('section', 'blk'), pairs)  17.1 us
    pallas_call x5, Pallas kernels, shards(): pl.pallas_call(functools.partial(later_level, level, rows, columns), in_s...  7.07 us
    pallas_call x1, Pallas kernels, shards(): pl.pallas_call(functools.partial(first_level, rows, columns), in_specs=[h...  3.01 us
  transfers between devices with their start and end apart: 40, of which 22 were waited for; matrix products, arithmetic and copies ran while one was open for 0% of the time, Pallas kernels for 0%

profile of v1, /device:TPU:0, one launch (start us, length us, event | category | flops | bytes accessed | tf_op | source)
XLA Modules:
  0.0 85.6 jit_solution(7606860997815841964)
XLA Ops:
  0.0 3.0 %first_level.1 = (f32[129,32,128]{2,1,0:T(8,128)S(1)}, f32[48,32,32]{2,1,0:T(8,128)S(1)}, s32[294]{0:T(512)S(1)}, s32[5,1,8]{2,1,0:T(1,128)S(1)}, s32[5,1,8]{2,1...) custom-call(s32[48]{0:T(128)} %refs_0_.1, ...), custom_call_target="tpu_custom_call" | custom-call | tf_op jit(solution)/shard_map/first_level/pallas_call | solution.py:190
  3.5 3.7 %collective-permute-start.1 = (f32[4,32,128]{2,1,0:T(8,128)S(1)}, f32[4,32,128]{2,1,0:T(8,128)S(1)}, u32[]{:S(2)}, u32[]{:S(2)}) collective-permute-start(f32[4,32,128]{2,1,0:T(8,128)S(1)} %get-tuple-element.48), channel_id=1, source_target_pairs={{0,9},{1,8},{2,11},{3,10},{4,13},{5,12},{6,15},{7,14},{8,17},{9,16... | collective-permute-start | bytes 196616 | tf_op jit(solution)/shard_map/ppermute | solution.py:31
  7.2 2.6 %collective-permute-start.4 = (f32[4,32,128]{2,1,0:T(8,128)S(1)}, f32[4,32,128]{2,1,0:T(8,128)S(1)}, u32[]{:S(2)}, u32[]{:S(2)}) collective-permute-start(f32[4,32,128]{2,1,0:T(8,128)S(1)} %get-tuple-element.50), channel_id=1, source_target_pairs={{0,4},{1,5},{2,6},{3,7},{4,0},{5,1},{6,2},{7,3},{8,12},{9,13},{10,... | collective-permute-start | bytes 196616 | tf_op jit(solution)/shard_map/ppermute | solution.py:31
  9.9 3.0 %collective-permute-start.2 = (f32[2,32,128]{2,1,0:T(8,128)S(1)}, f32[2,32,128]{2,1,0:T(8,128)S(1)}, u32[]{:S(2)}, u32[]{:S(2)}) collective-permute-start(f32[2,32,128]{2,1,0:T(8,128)S(1)} %pad_maximum_fusion.5), channel_id=1, source_target_pairs={{0,6},{1,7},{2,4},{3,5},{4,2},{5,3},{6,0},{7,1},{8,14},{9,15},{10,... | collective-permute-start | bytes 98312 | tf_op jit(solution)/shard_map/ppermute | solution.py:31
  14.6 1.3 %collective-permute-start.7 = (f32[4,32,128]{2,1,0:T(8,128)S(1)}, f32[4,32,128]{2,1,0:T(8,128)S(1)}, u32[]{:S(2)}, u32[]{:S(2)}) collective-permute-start(f32[4,32,128]{2,1,0:T(8,128)S(1)} %pad_maximum_fusion), channel_id=1, source_target_pairs={{0,2},{1,3},{2,0},{3,1},{4,6},{5,7},{6,4},{7,5},{8,10},{9,11},{10,... | collective-permute-start | bytes 196616 | tf_op jit(solution)/shard_map/ppermute | solution.py:31
  15.9 1.6 %collective-permute-start.6 = (f32[2,32,128]{2,1,0:T(8,128)S(1)}, f32[2,32,128]{2,1,0:T(8,128)S(1)}, u32[]{:S(2)}, u32[]{:S(2)}) collective-permute-start(f32[2,32,128]{2,1,0:T(8,128)S(1)} %pad_maximum_fusion.8), channel_id=1, source_target_pairs={{0,1},{1,0},{2,3},{3,2},{4,5},{5,4},{6,7},{7,6},{8,9},{9,8},{10,11... | collective-permute-start | bytes 98312 | tf_op jit(solution)/shard_map/ppermute | solution.py:31
  17.7 1.4 %collective-permute-done.5.refs_2_ = f32[2,32,128]{2,1,0:T(8,128)S(1)} collective-permute-done((f32[2,32,128]{2,1,0:T(8,128)S(1)}, f32[2,32,128]{2,1,0:T(8,128)S(1)}, u32[]{:S(2)}, u32[]{:S(2)}) %collective-permute-start.5) | collective-permute-done | bytes 32800 | tf_op jit(solution)/shard_map/ppermute | solution.py:31
  19.8 1.2 %later_level.5 = (f32[129,32,128]{2,1,0:T(8,128)S(1)}, f32[4,32,128]{2,1,0:T(8,128)S(1)}, f32[4,32,128]{2,1,0:T(8,128)S(1)}, f32[4,32,128]{2,1,0:T(8,128)S(1)}, f32[4,32,128]{2,1,0:T(8,128)S(1)}) custom-call(s32[294]{0:T(512)S(1)} %get-tuple-element.39.plan, s32[5,1,8]{2,1,0:T(1,128)S(1)} %get-tuple-element.40.peers, ...), custom_call_target="tpu_custom_call", output_to_operand_aliasing={{0}: (17, {})} | custom-call | tf_op jit(solution)/shard_map/later_level/pallas_call | solution.py:222
  21.2 1.8 %collective-permute-start.9 = (f32[4,32,128]{2,1,0:T(8,128)S(1)}, f32[4,32,128]{2,1,0:T(8,128)S(1)}, u32[]{:S(2)}, u32[]{:S(2)}) collective-permute-start(f32[4,32,128]{2,1,0:T(8,128)S(1)} %get-tuple-element.53), channel_id=1, source_target_pairs={{0,9},{1,8},{2,11},{3,10},{4,13},{5,12},{6,15},{7,14},{8,17},{9,16... | collective-permute-start | bytes 196616 | tf_op jit(solution)/shard_map/ppermute | solution.py:31
  22.9 2.9 %collective-permute-start.12 = (f32[4,32,128]{2,1,0:T(8,128)S(1)}, f32[4,32,128]{2,1,0:T(8,128)S(1)}, u32[]{:S(2)}, u32[]{:S(2)}) collective-permute-start(f32[4,32,128]{2,1,0:T(8,128)S(1)} %get-tuple-element.55), channel_id=1, source_target_pairs={{0,4},{1,5},{2,6},{3,7},{4,0},{5,1},{6,2},{7,3},{8,12},{9,13},{10,... | collective-permute-start | bytes 196616 | tf_op jit(solution)/shard_map/ppermute | solution.py:31
  25.9 3.8 %collective-permute-start.10 = (f32[2,32,128]{2,1,0:T(8,128)S(1)}, f32[2,32,128]{2,1,0:T(8,128)S(1)}, u32[]{:S(2)}, u32[]{:S(2)}) collective-permute-start(f32[2,32,128]{2,1,0:T(8,128)S(1)} %pad_maximum_fusion.9), channel_id=1, source_target_pairs={{0,6},{1,7},{2,4},{3,5},{4,2},{5,3},{6,0},{7,1},{8,14},{9,15},{10,... | collective-permute-start | bytes 98312 | tf_op jit(solution)/shard_map/ppermute | solution.py:31
  29.7 1.7 %collective-permute-start.13 = (f32[2,32,128]{2,1,0:T(8,128)S(1)}, f32[2,32,128]{2,1,0:T(8,128)S(1)}, u32[]{:S(2)}, u32[]{:S(2)}) collective-permute-start(f32[2,32,128]{2,1,0:T(8,128)S(1)} %pad_maximum_fusion.11), channel_id=1, source_target_pairs={{0,3},{1,2},{2,1},{3,0},{4,7},{5,6},{6,5},{7,4},{8,11},{9,10},{10,... | collective-permute-start | bytes 98312 | tf_op jit(solution)/shard_map/ppermute | solution.py:31
  33.2 1.2 %collective-permute-done.11.refs_1_ = f32[2,32,128]{2,1,0:T(8,128)S(1)} collective-permute-done((f32[2,32,128]{2,1,0:T(8,128)S(1)}, f32[2,32,128]{2,1,0:T(8,128)S(1)}, u32[]{:S(2)}, u32[]{:S(2)}) %collective-permute-start.11) | collective-permute-done | bytes 32800 | tf_op jit(solution)/shard_map/ppermute | solution.py:31
  34.8 1.5 %collective-permute-done.14.refs_3_ = f32[2,32,128]{2,1,0:T(8,128)S(1)} collective-permute-done((f32[2,32,128]{2,1,0:T(8,128)S(1)}, f32[2,32,128]{2,1,0:T(8,128)S(1)}, u32[]{:S(2)}, u32[]{:S(2)}) %collective-permute-start.14) | collective-permute-done | bytes 32800 | tf_op jit(solution)/shard_map/ppermute | solution.py:31
  36.3 1.2 %later_level.6 = (f32[129,32,128]{2,1,0:T(8,128)S(1)}, f32[4,32,128]{2,1,0:T(8,128)S(1)}, f32[4,32,128]{2,1,0:T(8,128)S(1)}, f32[4,32,128]{2,1,0:T(8,128)S(1)}, f32[4,32,128]{2,1,0:T(8,128)S(1)}) custom-call(s32[294]{0:T(512)S(1)} %get-tuple-element.39.plan, s32[5,1,8]{2,1,0:T(1,128)S(1)} %get-tuple-element.40.peers, ...), custom_call_target="tpu_custom_call", output_to_operand_aliasing={{0}: (17, {})} | custom-call | tf_op jit(solution)/shard_map/later_level/pallas_call | solution.py:222
  37.7 1.6 %collective-permute-start.17 = (f32[4,32,128]{2,1,0:T(8,128)S(1)}, f32[4,32,128]{2,1,0:T(8,128)S(1)}, u32[]{:S(2)}, u32[]{:S(2)}) collective-permute-start(f32[4,32,128]{2,1,0:T(8,128)S(1)} %get-tuple-element.58), channel_id=1, source_target_pairs={{0,9},{1,8},{2,11},{3,10},{4,13},{5,12},{6,15},{7,14},{8,17},{9,16... | collective-permute-start | bytes 196616 | tf_op jit(solution)/shard_map/ppermute | solution.py:31
  39.2 2.3 %collective-permute-start.20 = (f32[4,32,128]{2,1,0:T(8,128)S(1)}, f32[4,32,128]{2,1,0:T(8,128)S(1)}, u32[]{:S(2)}, u32[]{:S(2)}) collective-permute-start(f32[4,32,128]{2,1,0:T(8,128)S(1)} %get-tuple-element.60), channel_id=1, source_target_pairs={{0,4},{1,5},{2,6},{3,7},{4,0},{5,1},{6,2},{7,3},{8,12},{9,13},{10,... | collective-permute-start | bytes 196616 | tf_op jit(solution)/shard_map/ppermute | solution.py:31
  42.3 3.0 %collective-permute-start.18 = (f32[2,32,128]{2,1,0:T(8,128)S(1)}, f32[2,32,128]{2,1,0:T(8,128)S(1)}, u32[]{:S(2)}, u32[]{:S(2)}) collective-permute-start(f32[2,32,128]{2,1,0:T(8,128)S(1)} %pad_maximum_fusion.13), channel_id=1, source_target_pairs={{0,6},{1,7},{2,4},{3,5},{4,2},{5,3},{6,0},{7,1},{8,14},{9,15},{10,... | collective-permute-start | bytes 98312 | tf_op jit(solution)/shard_map/ppermute | solution.py:31
  45.4 1.7 %collective-permute-start.21 = (f32[2,32,128]{2,1,0:T(8,128)S(1)}, f32[2,32,128]{2,1,0:T(8,128)S(1)}, u32[]{:S(2)}, u32[]{:S(2)}) collective-permute-start(f32[2,32,128]{2,1,0:T(8,128)S(1)} %pad_maximum_fusion.15), channel_id=1, source_target_pairs={{0,3},{1,2},{2,1},{3,0},{4,7},{5,6},{6,5},{7,4},{8,11},{9,10},{10,... | collective-permute-start | bytes 98312 | tf_op jit(solution)/shard_map/ppermute | solution.py:31
  49.0 1.5 %collective-permute-done.19.refs_1_ = f32[2,32,128]{2,1,0:T(8,128)S(1)} collective-permute-done((f32[2,32,128]{2,1,0:T(8,128)S(1)}, f32[2,32,128]{2,1,0:T(8,128)S(1)}, u32[]{:S(2)}, u32[]{:S(2)}) %collective-permute-start.19) | collective-permute-done | bytes 32800 | tf_op jit(solution)/shard_map/ppermute | solution.py:31
  51.9 1.2 %later_level.7 = (f32[129,32,128]{2,1,0:T(8,128)S(1)}, f32[4,32,128]{2,1,0:T(8,128)S(1)}, f32[4,32,128]{2,1,0:T(8,128)S(1)}, f32[4,32,128]{2,1,0:T(8,128)S(1)}, f32[4,32,128]{2,1,0:T(8,128)S(1)}) custom-call(s32[294]{0:T(512)S(1)} %get-tuple-element.39.plan, s32[5,1,8]{2,1,0:T(1,128)S(1)} %get-tuple-element.40.peers, ...), custom_call_target="tpu_custom_call", output_to_operand_aliasing={{0}: (17, {})} | custom-call | tf_op jit(solution)/shard_map/later_level/pallas_call | solution.py:222
  53.2 2.0 %collective-permute-start.25 = (f32[4,32,128]{2,1,0:T(8,128)S(1)}, f32[4,32,128]{2,1,0:T(8,128)S(1)}, u32[]{:S(2)}, u32[]{:S(2)}) collective-permute-start(f32[4,32,128]{2,1,0:T(8,128)S(1)} %get-tuple-element.63), channel_id=1, source_target_pairs={{0,9},{1,8},{2,11},{3,10},{4,13},{5,12},{6,15},{7,14},{8,17},{9,16... | collective-permute-start | bytes 196616 | tf_op jit(solution)/shard_map/ppermute | solution.py:31
  55.2 2.5 %collective-permute-start.28 = (f32[4,32,128]{2,1,0:T(8,128)S(1)}, f32[4,32,128]{2,1,0:T(8,128)S(1)}, u32[]{:S(2)}, u32[]{:S(2)}) collective-permute-start(f32[4,32,128]{2,1,0:T(8,128)S(1)} %get-tuple-element.65), channel_id=1, source_target_pairs={{0,4},{1,5},{2,6},{3,7},{4,0},{5,1},{6,2},{7,3},{8,12},{9,13},{10,... | collective-permute-start | bytes 196616 | tf_op jit(solution)/shard_map/ppermute | solution.py:31
  57.8 3.1 %collective-permute-start.26 = (f32[2,32,128]{2,1,0:T(8,128)S(1)}, f32[2,32,128]{2,1,0:T(8,128)S(1)}, u32[]{:S(2)}, u32[]{:S(2)}) collective-permute-start(f32[2,32,128]{2,1,0:T(8,128)S(1)} %pad_maximum_fusion.17), channel_id=1, source_target_pairs={{0,6},{1,7},{2,4},{3,5},{4,2},{5,3},{6,0},{7,1},{8,14},{9,15},{10,... | collective-permute-start | bytes 98312 | tf_op jit(solution)/shard_map/ppermute | solution.py:31
  61.4 1.5 %collective-permute-start.29 = (f32[2,32,128]{2,1,0:T(8,128)S(1)}, f32[2,32,128]{2,1,0:T(8,128)S(1)}, u32[]{:S(2)}, u32[]{:S(2)}) collective-permute-start(f32[2,32,128]{2,1,0:T(8,128)S(1)} %pad_maximum_fusion.19), channel_id=1, source_target_pairs={{0,3},{1,2},{2,1},{3,0},{4,7},{5,6},{6,5},{7,4},{8,11},{9,10},{10,... | collective-permute-start | bytes 98312 | tf_op jit(solution)/shard_map/ppermute | solution.py:31
  62.9 1.3 %collective-permute-start.31 = (f32[4,32,128]{2,1,0:T(8,128)S(1)}, f32[4,32,128]{2,1,0:T(8,128)S(1)}, u32[]{:S(2)}, u32[]{:S(2)}) collective-permute-start(f32[4,32,128]{2,1,0:T(8,128)S(1)} %pad_maximum_fusion.3), channel_id=1, source_target_pairs={{0,2},{1,3},{2,0},{3,1},{4,6},{5,7},{6,4},{7,5},{8,10},{9,11},{10,... | collective-permute-start | bytes 196616 | tf_op jit(solution)/shard_map/ppermute | solution.py:31
  68.1 1.2 %later_level.8 = (f32[129,32,128]{2,1,0:T(8,128)S(1)}, f32[4,32,128]{2,1,0:T(8,128)S(1)}, f32[4,32,128]{2,1,0:T(8,128)S(1)}, f32[4,32,128]{2,1,0:T(8,128)S(1)}, f32[4,32,128]{2,1,0:T(8,128)S(1)}) custom-call(s32[294]{0:T(512)S(1)} %get-tuple-element.39.plan, s32[5,1,8]{2,1,0:T(1,128)S(1)} %get-tuple-element.40.peers, ...), custom_call_target="tpu_custom_call", output_to_operand_aliasing={{0}: (17, {})} | custom-call | tf_op jit(solution)/shard_map/later_level/pallas_call | solution.py:222
  69.4 1.5 %collective-permute-start.33 = (f32[4,32,128]{2,1,0:T(8,128)S(1)}, f32[4,32,128]{2,1,0:T(8,128)S(1)}, u32[]{:S(2)}, u32[]{:S(2)}) collective-permute-start(f32[4,32,128]{2,1,0:T(8,128)S(1)} %get-tuple-element.68), channel_id=1, source_target_pairs={{0,9},{1,8},{2,11},{3,10},{4,13},{5,12},{6,15},{7,14},{8,17},{9,16... | collective-permute-start | bytes 196616 | tf_op jit(solution)/shard_map/ppermute | solution.py:31
  70.9 2.8 %collective-permute-start.36 = (f32[4,32,128]{2,1,0:T(8,128)S(1)}, f32[4,32,128]{2,1,0:T(8,128)S(1)}, u32[]{:S(2)}, u32[]{:S(2)}) collective-permute-start(f32[4,32,128]{2,1,0:T(8,128)S(1)} %get-tuple-element.70), channel_id=1, source_target_pairs={{0,4},{1,5},{2,6},{3,7},{4,0},{5,1},{6,2},{7,3},{8,12},{9,13},{10,... | collective-permute-start | bytes 196616 | tf_op jit(solution)/shard_map/ppermute | solution.py:31
  74.1 2.9 %collective-permute-start.34 = (f32[2,32,128]{2,1,0:T(8,128)S(1)}, f32[2,32,128]{2,1,0:T(8,128)S(1)}, u32[]{:S(2)}, u32[]{:S(2)}) collective-permute-start(f32[2,32,128]{2,1,0:T(8,128)S(1)} %pad_maximum_fusion.21), channel_id=1, source_target_pairs={{0,6},{1,7},{2,4},{3,5},{4,2},{5,3},{6,0},{7,1},{8,14},{9,15},{10,... | collective-permute-start | bytes 98312 | tf_op jit(solution)/shard_map/ppermute | solution.py:31
  77.3 1.6 %collective-permute-start.37 = (f32[2,32,128]{2,1,0:T(8,128)S(1)}, f32[2,32,128]{2,1,0:T(8,128)S(1)}, u32[]{:S(2)}, u32[]{:S(2)}) collective-permute-start(f32[2,32,128]{2,1,0:T(8,128)S(1)} %pad_maximum_fusion.23), channel_id=1, source_target_pairs={{0,3},{1,2},{2,1},{3,0},{4,7},{5,6},{6,5},{7,4},{8,11},{9,10},{10,... | collective-permute-start | bytes 98312 | tf_op jit(solution)/shard_map/ppermute | solution.py:31
  83.5 2.1 %later_level.9 = (f32[129,32,128]{2,1,0:T(8,128)S(1)}, f32[48,32,128]{2,1,0:T(8,128)}) custom-call(s32[294]{0:T(512)S(1)} %get-tuple-element.39.plan, s32[5,1,8]{2,1,0:T(1,128)S(1)} %get-tuple-element.40.peers, s32[5,1,8]{2,1,0:T(1,128)S(1)} %get-tuple-element.41.downs, s32[4,48]{1,0:T(4,128)S(1)} %get-tuple-element.42.slots, ...), custom_call_target="tpu_custom_call", output_to_operand_aliasing={{0}: (17, {})} | custom-call | tf_op jit(solution)/shard_map/later_level/pallas_call | solution.py:222
  (99 shorter events, 19.9 us)
Async XLA Ops:
  3.0 6.8 %collective-permute-start = (f32[4,32,128]{2,1,0:T(8,128)S(1)}, f32[4,32,128]{2,1,0:T(8,128)S(1)}, u32[]{:S(2)}, u32[]{:S(2)}) collective-permute-start(f32[4,32,128]{2,1,0:T(8,128)S(1)} %get-tuple-element.47), channel_id=1, source_target_pairs={{0,8},{1,9},{2,10},{3,11},{4,12},{5,13},{6,14},{7,15},{8,16},{9,17... | collective-permute-start | bytes 196616 | tf_op jit(solution)/shard_map/ppermute | solution.py:31
  3.5 6.3 %collective-permute-start.1 = (f32[4,32,128]{2,1,0:T(8,128)S(1)}, f32[4,32,128]{2,1,0:T(8,128)S(1)}, u32[]{:S(2)}, u32[]{:S(2)}) collective-permute-start(f32[4,32,128]{2,1,0:T(8,128)S(1)} %get-tuple-element.48), channel_id=1, source_target_pairs={{0,9},{1,8},{2,11},{3,10},{4,13},{5,12},{6,15},{7,14},{8,17},{9,16... | collective-permute-start | bytes 196616 | tf_op jit(solution)/shard_map/ppermute | solution.py:31
  7.2 6.7 %collective-permute-start.4 = (f32[4,32,128]{2,1,0:T(8,128)S(1)}, f32[4,32,128]{2,1,0:T(8,128)S(1)}, u32[]{:S(2)}, u32[]{:S(2)}) collective-permute-start(f32[4,32,128]{2,1,0:T(8,128)S(1)} %get-tuple-element.50), channel_id=1, source_target_pairs={{0,4},{1,5},{2,6},{3,7},{4,0},{5,1},{6,2},{7,3},{8,12},{9,13},{10,... | collective-permute-start | bytes 196616 | tf_op jit(solution)/shard_map/ppermute | solution.py:31
  9.9 7.6 %collective-permute-start.2 = (f32[2,32,128]{2,1,0:T(8,128)S(1)}, f32[2,32,128]{2,1,0:T(8,128)S(1)}, u32[]{:S(2)}, u32[]{:S(2)}) collective-permute-start(f32[2,32,128]{2,1,0:T(8,128)S(1)} %pad_maximum_fusion.5), channel_id=1, source_target_pairs={{0,6},{1,7},{2,4},{3,5},{4,2},{5,3},{6,0},{7,1},{8,14},{9,15},{10,... | collective-permute-start | bytes 98312 | tf_op jit(solution)/shard_map/ppermute | solution.py:31
  12.8 4.8 %collective-permute-start.3 = (f32[2,32,128]{2,1,0:T(8,128)S(1)}, f32[2,32,128]{2,1,0:T(8,128)S(1)}, u32[]{:S(2)}, u32[]{:S(2)}) collective-permute-start(f32[2,32,128]{2,1,0:T(8,128)S(1)} %pad_maximum_fusion.6), channel_id=1, source_target_pairs={{0,4},{1,5},{2,6},{3,7},{4,0},{5,1},{6,2},{7,3},{8,12},{9,13},{10,... | collective-permute-start | bytes 98312 | tf_op jit(solution)/shard_map/ppermute | solution.py:31
  13.9 5.1 %collective-permute-start.5 = (f32[2,32,128]{2,1,0:T(8,128)S(1)}, f32[2,32,128]{2,1,0:T(8,128)S(1)}, u32[]{:S(2)}, u32[]{:S(2)}) collective-permute-start(f32[2,32,128]{2,1,0:T(8,128)S(1)} %pad_maximum_fusion.7), channel_id=1, source_target_pairs={{0,3},{1,2},{2,1},{3,0},{4,7},{5,6},{6,5},{7,4},{8,11},{9,10},{10,... | collective-permute-start | bytes 98312 | tf_op jit(solution)/shard_map/ppermute | solution.py:31
  14.6 5.2 %collective-permute-start.7 = (f32[4,32,128]{2,1,0:T(8,128)S(1)}, f32[4,32,128]{2,1,0:T(8,128)S(1)}, u32[]{:S(2)}, u32[]{:S(2)}) collective-permute-start(f32[4,32,128]{2,1,0:T(8,128)S(1)} %pad_maximum_fusion), channel_id=1, source_target_pairs={{0,2},{1,3},{2,0},{3,1},{4,6},{5,7},{6,4},{7,5},{8,10},{9,11},{10,... | collective-permute-start | bytes 196616 | tf_op jit(solution)/shard_map/ppermute | solution.py:31
  21.1 4.7 %collective-permute-start.8 = (f32[4,32,128]{2,1,0:T(8,128)S(1)}, f32[4,32,128]{2,1,0:T(8,128)S(1)}, u32[]{:S(2)}, u32[]{:S(2)}) collective-permute-start(f32[4,32,128]{2,1,0:T(8,128)S(1)} %get-tuple-element.52), channel_id=1, source_target_pairs={{0,8},{1,9},{2,10},{3,11},{4,12},{5,13},{6,14},{7,15},{8,16},{9,17... | collective-permute-start | bytes 196616 | tf_op jit(solution)/shard_map/ppermute | solution.py:31
  21.2 4.7 %collective-permute-start.9 = (f32[4,32,128]{2,1,0:T(8,128)S(1)}, f32[4,32,128]{2,1,0:T(8,128)S(1)}, u32[]{:S(2)}, u32[]{:S(2)}) collective-permute-start(f32[4,32,128]{2,1,0:T(8,128)S(1)} %get-tuple-element.53), channel_id=1, source_target_pairs={{0,9},{1,8},{2,11},{3,10},{4,13},{5,12},{6,15},{7,14},{8,17},{9,16... | collective-permute-start | bytes 196616 | tf_op jit(solution)/shard_map/ppermute | solution.py:31
  22.9 6.7 %collective-permute-start.12 = (f32[4,32,128]{2,1,0:T(8,128)S(1)}, f32[4,32,128]{2,1,0:T(8,128)S(1)}, u32[]{:S(2)}, u32[]{:S(2)}) collective-permute-start(f32[4,32,128]{2,1,0:T(8,128)S(1)} %get-tuple-element.55), channel_id=1, source_target_pairs={{0,4},{1,5},{2,6},{3,7},{4,0},{5,1},{6,2},{7,3},{8,12},{9,13},{10,... | collective-permute-start | bytes 196616 | tf_op jit(solution)/shard_map/ppermute | solution.py:31
  25.9 7.4 %collective-permute-start.10 = (f32[2,32,128]{2,1,0:T(8,128)S(1)}, f32[2,32,128]{2,1,0:T(8,128)S(1)}, u32[]{:S(2)}, u32[]{:S(2)}) collective-permute-start(f32[2,32,128]{2,1,0:T(8,128)S(1)} %pad_maximum_fusion.9), channel_id=1, source_target_pairs={{0,6},{1,7},{2,4},{3,5},{4,2},{5,3},{6,0},{7,1},{8,14},{9,15},{10,... | collective-permute-start | bytes 98312 | tf_op jit(solution)/shard_map/ppermute | solution.py:31
  29.6 4.8 %collective-permute-start.11 = (f32[2,32,128]{2,1,0:T(8,128)S(1)}, f32[2,32,128]{2,1,0:T(8,128)S(1)}, u32[]{:S(2)}, u32[]{:S(2)}) collective-permute-start(f32[2,32,128]{2,1,0:T(8,128)S(1)} %pad_maximum_fusion.10), channel_id=1, source_target_pairs={{0,4},{1,5},{2,6},{3,7},{4,0},{5,1},{6,2},{7,3},{8,12},{9,13},{10,... | collective-permute-start | bytes 98312 | tf_op jit(solution)/shard_map/ppermute | solution.py:31
  29.7 5.2 %collective-permute-start.13 = (f32[2,32,128]{2,1,0:T(8,128)S(1)}, f32[2,32,128]{2,1,0:T(8,128)S(1)}, u32[]{:S(2)}, u32[]{:S(2)}) collective-permute-start(f32[2,32,128]{2,1,0:T(8,128)S(1)} %pad_maximum_fusion.11), channel_id=1, source_target_pairs={{0,3},{1,2},{2,1},{3,0},{4,7},{5,6},{6,5},{7,4},{8,11},{9,10},{10,... | collective-permute-start | bytes 98312 | tf_op jit(solution)/shard_map/ppermute | solution.py:31
  31.4 5.0 %collective-permute-start.15 = (f32[4,32,128]{2,1,0:T(8,128)S(1)}, f32[4,32,128]{2,1,0:T(8,128)S(1)}, u32[]{:S(2)}, u32[]{:S(2)}) collective-permute-start(f32[4,32,128]{2,1,0:T(8,128)S(1)} %pad_maximum_fusion.1), channel_id=1, source_target_pairs={{0,2},{1,3},{2,0},{3,1},{4,6},{5,7},{6,4},{7,5},{8,10},{9,11},{10,... | collective-permute-start | bytes 196616 | tf_op jit(solution)/shard_map/ppermute | solution.py:31
  37.7 4.6 %collective-permute-start.17 = (f32[4,32,128]{2,1,0:T(8,128)S(1)}, f32[4,32,128]{2,1,0:T(8,128)S(1)}, u32[]{:S(2)}, u32[]{:S(2)}) collective-permute-start(f32[4,32,128]{2,1,0:T(8,128)S(1)} %get-tuple-element.58), channel_id=1, source_target_pairs={{0,9},{1,8},{2,11},{3,10},{4,13},{5,12},{6,15},{7,14},{8,17},{9,16... | collective-permute-start | bytes 196616 | tf_op jit(solution)/shard_map/ppermute | solution.py:31
  39.2 6.2 %collective-permute-start.20 = (f32[4,32,128]{2,1,0:T(8,128)S(1)}, f32[4,32,128]{2,1,0:T(8,128)S(1)}, u32[]{:S(2)}, u32[]{:S(2)}) collective-permute-start(f32[4,32,128]{2,1,0:T(8,128)S(1)} %get-tuple-element.60), channel_id=1, source_target_pairs={{0,4},{1,5},{2,6},{3,7},{4,0},{5,1},{6,2},{7,3},{8,12},{9,13},{10,... | collective-permute-start | bytes 196616 | tf_op jit(solution)/shard_map/ppermute | solution.py:31
  42.3 6.7 %collective-permute-start.18 = (f32[2,32,128]{2,1,0:T(8,128)S(1)}, f32[2,32,128]{2,1,0:T(8,128)S(1)}, u32[]{:S(2)}, u32[]{:S(2)}) collective-permute-start(f32[2,32,128]{2,1,0:T(8,128)S(1)} %pad_maximum_fusion.13), channel_id=1, source_target_pairs={{0,6},{1,7},{2,4},{3,5},{4,2},{5,3},{6,0},{7,1},{8,14},{9,15},{10,... | collective-permute-start | bytes 98312 | tf_op jit(solution)/shard_map/ppermute | solution.py:31
  45.3 5.3 %collective-permute-start.19 = (f32[2,32,128]{2,1,0:T(8,128)S(1)}, f32[2,32,128]{2,1,0:T(8,128)S(1)}, u32[]{:S(2)}, u32[]{:S(2)}) collective-permute-start(f32[2,32,128]{2,1,0:T(8,128)S(1)} %pad_maximum_fusion.14), channel_id=1, source_target_pairs={{0,4},{1,5},{2,6},{3,7},{4,0},{5,1},{6,2},{7,3},{8,12},{9,13},{10,... | collective-permute-start | bytes 98312 | tf_op jit(solution)/shard_map/ppermute | solution.py:31
  45.4 5.5 %collective-permute-start.21 = (f32[2,32,128]{2,1,0:T(8,128)S(1)}, f32[2,32,128]{2,1,0:T(8,128)S(1)}, u32[]{:S(2)}, u32[]{:S(2)}) collective-permute-start(f32[2,32,128]{2,1,0:T(8,128)S(1)} %pad_maximum_fusion.15), channel_id=1, source_target_pairs={{0,3},{1,2},{2,1},{3,0},{4,7},{5,6},{6,5},{7,4},{8,11},{9,10},{10,... | collective-permute-start | bytes 98312 | tf_op jit(solution)/shard_map/ppermute | solution.py:31
  47.1 4.8 %collective-permute-start.23 = (f32[4,32,128]{2,1,0:T(8,128)S(1)}, f32[4,32,128]{2,1,0:T(8,128)S(1)}, u32[]{:S(2)}, u32[]{:S(2)}) collective-permute-start(f32[4,32,128]{2,1,0:T(8,128)S(1)} %pad_maximum_fusion.2), channel_id=1, source_target_pairs={{0,2},{1,3},{2,0},{3,1},{4,6},{5,7},{6,4},{7,5},{8,10},{9,11},{10,... | collective-permute-start | bytes 196616 | tf_op jit(solution)/shard_map/ppermute | solution.py:31
  53.2 4.6 %collective-permute-start.25 = (f32[4,32,128]{2,1,0:T(8,128)S(1)}, f32[4,32,128]{2,1,0:T(8,128)S(1)}, u32[]{:S(2)}, u32[]{:S(2)}) collective-permute-start(f32[4,32,128]{2,1,0:T(8,128)S(1)} %get-tuple-element.63), channel_id=1, source_target_pairs={{0,9},{1,8},{2,11},{3,10},{4,13},{5,12},{6,15},{7,14},{8,17},{9,16... | collective-permute-start | bytes 196616 | tf_op jit(solution)/shard_map/ppermute | solution.py:31
  55.2 6.2 %collective-permute-start.28 = (f32[4,32,128]{2,1,0:T(8,128)S(1)}, f32[4,32,128]{2,1,0:T(8,128)S(1)}, u32[]{:S(2)}, u32[]{:S(2)}) collective-permute-start(f32[4,32,128]{2,1,0:T(8,128)S(1)} %get-tuple-element.65), channel_id=1, source_target_pairs={{0,4},{1,5},{2,6},{3,7},{4,0},{5,1},{6,2},{7,3},{8,12},{9,13},{10,... | collective-permute-start | bytes 196616 | tf_op jit(solution)/shard_map/ppermute | solution.py:31
  57.8 7.1 %collective-permute-start.26 = (f32[2,32,128]{2,1,0:T(8,128)S(1)}, f32[2,32,128]{2,1,0:T(8,128)S(1)}, u32[]{:S(2)}, u32[]{:S(2)}) collective-permute-start(f32[2,32,128]{2,1,0:T(8,128)S(1)} %pad_maximum_fusion.17), channel_id=1, source_target_pairs={{0,6},{1,7},{2,4},{3,5},{4,2},{5,3},{6,0},{7,1},{8,14},{9,15},{10,... | collective-permute-start | bytes 98312 | tf_op jit(solution)/shard_map/ppermute | solution.py:31
  60.9 4.8 %collective-permute-start.27 = (f32[2,32,128]{2,1,0:T(8,128)S(1)}, f32[2,32,128]{2,1,0:T(8,128)S(1)}, u32[]{:S(2)}, u32[]{:S(2)}) collective-permute-start(f32[2,32,128]{2,1,0:T(8,128)S(1)} %pad_maximum_fusion.18), channel_id=1, source_target_pairs={{0,4},{1,5},{2,6},{3,7},{4,0},{5,1},{6,2},{7,3},{8,12},{9,13},{10,... | collective-permute-start | bytes 98312 | tf_op jit(solution)/shard_map/ppermute | solution.py:31
  61.4 5.6 %collective-permute-start.29 = (f32[2,32,128]{2,1,0:T(8,128)S(1)}, f32[2,32,128]{2,1,0:T(8,128)S(1)}, u32[]{:S(2)}, u32[]{:S(2)}) collective-permute-start(f32[2,32,128]{2,1,0:T(8,128)S(1)} %pad_maximum_fusion.19), channel_id=1, source_target_pairs={{0,3},{1,2},{2,1},{3,0},{4,7},{5,6},{6,5},{7,4},{8,11},{9,10},{10,... | collective-permute-start | bytes 98312 | tf_op jit(solution)/shard_map/ppermute | solution.py:31
  62.9 5.2 %collective-permute-start.31 = (f32[4,32,128]{2,1,0:T(8,128)S(1)}, f32[4,32,128]{2,1,0:T(8,128)S(1)}, u32[]{:S(2)}, u32[]{:S(2)}) collective-permute-start(f32[4,32,128]{2,1,0:T(8,128)S(1)} %pad_maximum_fusion.3), channel_id=1, source_target_pairs={{0,2},{1,3},{2,0},{3,1},{4,6},{5,7},{6,4},{7,5},{8,10},{9,11},{10,... | collective-permute-start | bytes 196616 | tf_op jit(solution)/shard_map/ppermute | solution.py:31
  69.4 4.6 %collective-permute-start.33 = (f32[4,32,128]{2,1,0:T(8,128)S(1)}, f32[4,32,128]{2,1,0:T(8,128)S(1)}, u32[]{:S(2)}, u32[]{:S(2)}) collective-permute-start(f32[4,32,128]{2,1,0:T(8,128)S(1)} %get-tuple-element.68), channel_id=1, source_target_pairs={{0,9},{1,8},{2,11},{3,10},{4,13},{5,12},{6,15},{7,14},{8,17},{9,16... | collective-permute-start | bytes 196616 | tf_op jit(solution)/shard_map/ppermute | solution.py:31
  70.9 6.4 %collective-permute-start.36 = (f32[4,32,128]{2,1,0:T(8,128)S(1)}, f32[4,32,128]{2,1,0:T(8,128)S(1)}, u32[]{:S(2)}, u32[]{:S(2)}) collective-permute-start(f32[4,32,128]{2,1,0:T(8,128)S(1)} %get-tuple-element.70), channel_id=1, source_target_pairs={{0,4},{1,5},{2,6},{3,7},{4,0},{5,1},{6,2},{7,3},{8,12},{9,13},{10,... | collective-permute-start | bytes 196616 | tf_op jit(solution)/shard_map/ppermute | solution.py:31
  74.1 6.8 %collective-permute-start.34 = (f32[2,32,128]{2,1,0:T(8,128)S(1)}, f32[2,32,128]{2,1,0:T(8,128)S(1)}, u32[]{:S(2)}, u32[]{:S(2)}) collective-permute-start(f32[2,32,128]{2,1,0:T(8,128)S(1)} %pad_maximum_fusion.21), channel_id=1, source_target_pairs={{0,6},{1,7},{2,4},{3,5},{4,2},{5,3},{6,0},{7,1},{8,14},{9,15},{10,... | collective-permute-start | bytes 98312 | tf_op jit(solution)/shard_map/ppermute | solution.py:31
  77.0 4.9 %collective-permute-start.35 = (f32[2,32,128]{2,1,0:T(8,128)S(1)}, f32[2,32,128]{2,1,0:T(8,128)S(1)}, u32[]{:S(2)}, u32[]{:S(2)}) collective-permute-start(f32[2,32,128]{2,1,0:T(8,128)S(1)} %pad_maximum_fusion.22), channel_id=1, source_target_pairs={{0,4},{1,5},{2,6},{3,7},{4,0},{5,1},{6,2},{7,3},{8,12},{9,13},{10,... | collective-permute-start | bytes 98312 | tf_op jit(solution)/shard_map/ppermute | solution.py:31
  77.3 5.4 %collective-permute-start.37 = (f32[2,32,128]{2,1,0:T(8,128)S(1)}, f32[2,32,128]{2,1,0:T(8,128)S(1)}, u32[]{:S(2)}, u32[]{:S(2)}) collective-permute-start(f32[2,32,128]{2,1,0:T(8,128)S(1)} %pad_maximum_fusion.23), channel_id=1, source_target_pairs={{0,3},{1,2},{2,1},{3,0},{4,7},{5,6},{6,5},{7,4},{8,11},{9,10},{10,... | collective-permute-start | bytes 98312 | tf_op jit(solution)/shard_map/ppermute | solution.py:31
  78.8 4.7 %collective-permute-start.39 = (f32[4,32,128]{2,1,0:T(8,128)S(1)}, f32[4,32,128]{2,1,0:T(8,128)S(1)}, u32[]{:S(2)}, u32[]{:S(2)}) collective-permute-start(f32[4,32,128]{2,1,0:T(8,128)S(1)} %pad_maximum_fusion.4), channel_id=1, source_target_pairs={{0,2},{1,3},{2,0},{3,1},{4,6},{5,7},{6,4},{7,5},{8,10},{9,11},{10,... | collective-permute-start | bytes 196616 | tf_op jit(solution)/shard_map/ppermute | solution.py:31
  (8 other events, 32.4 us)

commit v2 on v1

--- a/solution.py
+++ b/solution.py
@@ -96,19 +96,21 @@
 def first_level(rows, columns, *refs):
     refs = list(refs)
     levels_in, kin_in, residual_in, weight_in, peers_in, downs_in, slots_in, frac_in = (refs.pop(0) for _ in range(8))
-    pool, kin, plan, peers_out, downs_out, slots_out, residual, weight, frac = (refs.pop(0) for _ in range(9))
+    pool, kin, plan_out, peers_out, downs_out, slots_out, residual, weight, frac = (refs.pop(0) for _ in range(9))
     outs = [refs.pop(0) for _ in range(columns + rows // halves_of(rows))]
-    levels, kin_here, peers, downs, sems = refs
+    plan, levels, kin_here, peers, downs, sems = refs
     pairs = [(levels_in, levels), (kin_in, kin_here), (residual_in, residual), (weight_in, weight)]
     pairs += [(peers_in, peers), (downs_in, downs)]
     pairs += [(peers_in, peers_out), (downs_in, downs_out), (slots_in, slots_out), (frac_in, frac)]
+    pairs += [(plan, plan_out)]
     copies = [pltpu.make_async_copy(source, target, sems.at[i]) for i, (source, target) in enumerate(pairs)]
-    for copy in copies:
+    for copy in copies[:-1]:
         copy.start()
     blocks = residual.shape[0]
     pool[blocks] = jnp.zeros(pool.shape[1:], pool.dtype)
     copies[0].wait()
     sort_blocks(blocks, levels, plan)
+    copies[-1].start()
     copies[1].wait()
     for i in range(kin.shape[1]):
         kin[:, i, :] = jnp.transpose(kin_here[i])
@@ -190,14 +192,15 @@
     pool, kin, *outs = pl.pallas_call(
         functools.partial(first_level, rows, columns),
         in_specs=[hbm] * len(to_first),
-        out_specs=[vmem, vmem, smem] + [vmem] * (len(held) + len(send_shapes)),
+        out_specs=[vmem] * (2 + len(held_shapes) + len(send_shapes)),
         out_shape=[pool_shape, kin_shape] + held_shapes + send_shapes,
         scratch_shapes=[
+            pltpu.SMEM(held_shapes[0].shape, jnp.int32),
             pltpu.SMEM(block_level.shape, jnp.int32),
             pltpu.VMEM(kin_turned.shape, jnp.float32),
             pltpu.SMEM(peers.shape, jnp.int32),
             pltpu.SMEM(downs.shape, jnp.int32),
-            pltpu.SemaphoreType.DMA((10,)),
+            pltpu.SemaphoreType.DMA((11,)),
         ],
         compiler_params=params,
         name="first_level",

time: 85.8 us -> 85.2 us (level)
  no operation moved by 1% of the time
where the time goes in v2:
time: 85.2 us; the launch traced here: 85.1 us
  starting transfers between devices  58.2 us (68%)
  waiting for transfers between devices  17 us (20%)
  Pallas kernels  9.47 us (11%)
    ppermute x40, starting transfers between devices, moved(): return lax.ppermute(value, ('section', 'blk'), pairs)  58.2 us
    ppermute x40, waiting for transfers between devices, moved(): return lax.ppermute(value, ('section', 'blk'), pairs)  17 us
    pallas_call x5, Pallas kernels, shards(): pl.pallas_call(functools.partial(later_level, level, rows, columns), in_s...  7.06 us
    pallas_call x1, Pallas kernels, shards(): pl.pallas_call(functools.partial(first_level, rows, columns), in_specs=[h...  2.41 us
  transfers between devices with their start and end apart: 40, of which 22 were waited for; matrix products, arithmetic and copies ran while one was open for 0% of the time, Pallas kernels for 0%

profile of v2, /device:TPU:0, one launch (start us, length us, event | category | flops | bytes accessed | tf_op | source)
XLA Modules:
  0.0 85.1 jit_solution(16815406058874779636)
XLA Ops:
  0.0 2.4 %first_level.1 = (f32[129,32,128]{2,1,0:T(8,128)S(1)}, f32[48,32,32]{2,1,0:T(8,128)S(1)}, s32[294]{0:T(512)S(1)}, s32[5,1,8]{2,1,0:T(1,128)S(1)}, s32[5,1,8]{2,1...) custom-call(s32[48]{0:T(128)} %refs_0_.1, ...), custom_call_target="tpu_custom_call" | custom-call | tf_op jit(solution)/shard_map/first_level/pallas_call | solution.py:192
  2.9 3.7 %collective-permute-start.1 = (f32[4,32,128]{2,1,0:T(8,128)S(1)}, f32[4,32,128]{2,1,0:T(8,128)S(1)}, u32[]{:S(2)}, u32[]{:S(2)}) collective-permute-start(f32[4,32,128]{2,1,0:T(8,128)S(1)} %get-tuple-element.48), channel_id=1, source_target_pairs={{0,9},{1,8},{2,11},{3,10},{4,13},{5,12},{6,15},{7,14},{8,17},{9,16... | collective-permute-start | bytes 196616 | tf_op jit(solution)/shard_map/ppermute | solution.py:31
  6.7 2.6 %collective-permute-start.4 = (f32[4,32,128]{2,1,0:T(8,128)S(1)}, f32[4,32,128]{2,1,0:T(8,128)S(1)}, u32[]{:S(2)}, u32[]{:S(2)}) collective-permute-start(f32[4,32,128]{2,1,0:T(8,128)S(1)} %get-tuple-element.50), channel_id=1, source_target_pairs={{0,4},{1,5},{2,6},{3,7},{4,0},{5,1},{6,2},{7,3},{8,12},{9,13},{10,... | collective-permute-start | bytes 196616 | tf_op jit(solution)/shard_map/ppermute | solution.py:31
  9.3 3.0 %collective-permute-start.2 = (f32[2,32,128]{2,1,0:T(8,128)S(1)}, f32[2,32,128]{2,1,0:T(8,128)S(1)}, u32[]{:S(2)}, u32[]{:S(2)}) collective-permute-start(f32[2,32,128]{2,1,0:T(8,128)S(1)} %pad_maximum_fusion.5), channel_id=1, source_target_pairs={{0,6},{1,7},{2,4},{3,5},{4,2},{5,3},{6,0},{7,1},{8,14},{9,15},{10,... | collective-permute-start | bytes 98312 | tf_op jit(solution)/shard_map/ppermute | solution.py:31
  14.1 1.3 %collective-permute-start.7 = (f32[4,32,128]{2,1,0:T(8,128)S(1)}, f32[4,32,128]{2,1,0:T(8,128)S(1)}, u32[]{:S(2)}, u32[]{:S(2)}) collective-permute-start(f32[4,32,128]{2,1,0:T(8,128)S(1)} %pad_maximum_fusion), channel_id=1, source_target_pairs={{0,2},{1,3},{2,0},{3,1},{4,6},{5,7},{6,4},{7,5},{8,10},{9,11},{10,... | collective-permute-start | bytes 196616 | tf_op jit(solution)/shard_map/ppermute | solution.py:31
  15.3 1.6 %collective-permute-start.6 = (f32[2,32,128]{2,1,0:T(8,128)S(1)}, f32[2,32,128]{2,1,0:T(8,128)S(1)}, u32[]{:S(2)}, u32[]{:S(2)}) collective-permute-start(f32[2,32,128]{2,1,0:T(8,128)S(1)} %pad_maximum_fusion.8), channel_id=1, source_target_pairs={{0,1},{1,0},{2,3},{3,2},{4,5},{5,4},{6,7},{7,6},{8,9},{9,8},{10,11... | collective-permute-start | bytes 98312 | tf_op jit(solution)/shard_map/ppermute | solution.py:31
  17.1 1.4 %collective-permute-done.5.refs_2_ = f32[2,32,128]{2,1,0:T(8,128)S(1)} collective-permute-done((f32[2,32,128]{2,1,0:T(8,128)S(1)}, f32[2,32,128]{2,1,0:T(8,128)S(1)}, u32[]{:S(2)}, u32[]{:S(2)}) %collective-permute-start.5) | collective-permute-done | bytes 32800 | tf_op jit(solution)/shard_map/ppermute | solution.py:31
  19.2 1.2 %later_level.5 = (f32[129,32,128]{2,1,0:T(8,128)S(1)}, f32[4,32,128]{2,1,0:T(8,128)S(1)}, f32[4,32,128]{2,1,0:T(8,128)S(1)}, f32[4,32,128]{2,1,0:T(8,128)S(1)}, f32[4,32,128]{2,1,0:T(8,128)S(1)}) custom-call(s32[294]{0:T(512)S(1)} %get-tuple-element.39.plan, s32[5,1,8]{2,1,0:T(1,128)S(1)} %get-tuple-element.40.peers, ...), custom_call_target="tpu_custom_call", output_to_operand_aliasing={{0}: (17, {})} | custom-call | tf_op jit(solution)/shard_map/later_level/pallas_call | solution.py:225
  20.6 1.8 %collective-permute-start.9 = (f32[4,32,128]{2,1,0:T(8,128)S(1)}, f32[4,32,128]{2,1,0:T(8,128)S(1)}, u32[]{:S(2)}, u32[]{:S(2)}) collective-permute-start(f32[4,32,128]{2,1,0:T(8,128)S(1)} %get-tuple-element.53), channel_id=1, source_target_pairs={{0,9},{1,8},{2,11},{3,10},{4,13},{5,12},{6,15},{7,14},{8,17},{9,16... | collective-permute-start | bytes 196616 | tf_op jit(solution)/shard_map/ppermute | solution.py:31
  22.3 2.9 %collective-permute-start.12 = (f32[4,32,128]{2,1,0:T(8,128)S(1)}, f32[4,32,128]{2,1,0:T(8,128)S(1)}, u32[]{:S(2)}, u32[]{:S(2)}) collective-permute-start(f32[4,32,128]{2,1,0:T(8,128)S(1)} %get-tuple-element.55), channel_id=1, source_target_pairs={{0,4},{1,5},{2,6},{3,7},{4,0},{5,1},{6,2},{7,3},{8,12},{9,13},{10,... | collective-permute-start | bytes 196616 | tf_op jit(solution)/shard_map/ppermute | solution.py:31
  25.3 3.8 %collective-permute-start.10 = (f32[2,32,128]{2,1,0:T(8,128)S(1)}, f32[2,32,128]{2,1,0:T(8,128)S(1)}, u32[]{:S(2)}, u32[]{:S(2)}) collective-permute-start(f32[2,32,128]{2,1,0:T(8,128)S(1)} %pad_maximum_fusion.9), channel_id=1, source_target_pairs={{0,6},{1,7},{2,4},{3,5},{4,2},{5,3},{6,0},{7,1},{8,14},{9,15},{10,... | collective-permute-start | bytes 98312 | tf_op jit(solution)/shard_map/ppermute | solution.py:31
  29.1 1.7 %collective-permute-start.13 = (f32[2,32,128]{2,1,0:T(8,128)S(1)}, f32[2,32,128]{2,1,0:T(8,128)S(1)}, u32[]{:S(2)}, u32[]{:S(2)}) collective-permute-start(f32[2,32,128]{2,1,0:T(8,128)S(1)} %pad_maximum_fusion.11), channel_id=1, source_target_pairs={{0,3},{1,2},{2,1},{3,0},{4,7},{5,6},{6,5},{7,4},{8,11},{9,10},{10,... | collective-permute-start | bytes 98312 | tf_op jit(solution)/shard_map/ppermute | solution.py:31
  34.3 1.5 %collective-permute-done.14.refs_3_ = f32[2,32,128]{2,1,0:T(8,128)S(1)} collective-permute-done((f32[2,32,128]{2,1,0:T(8,128)S(1)}, f32[2,32,128]{2,1,0:T(8,128)S(1)}, u32[]{:S(2)}, u32[]{:S(2)}) %collective-permute-start.14) | collective-permute-done | bytes 32800 | tf_op jit(solution)/shard_map/ppermute | solution.py:31
  35.8 1.2 %later_level.6 = (f32[129,32,128]{2,1,0:T(8,128)S(1)}, f32[4,32,128]{2,1,0:T(8,128)S(1)}, f32[4,32,128]{2,1,0:T(8,128)S(1)}, f32[4,32,128]{2,1,0:T(8,128)S(1)}, f32[4,32,128]{2,1,0:T(8,128)S(1)}) custom-call(s32[294]{0:T(512)S(1)} %get-tuple-element.39.plan, s32[5,1,8]{2,1,0:T(1,128)S(1)} %get-tuple-element.40.peers, ...), custom_call_target="tpu_custom_call", output_to_operand_aliasing={{0}: (17, {})} | custom-call | tf_op jit(solution)/shard_map/later_level/pallas_call | solution.py:225
  37.1 1.6 %collective-permute-start.17 = (f32[4,32,128]{2,1,0:T(8,128)S(1)}, f32[4,32,128]{2,1,0:T(8,128)S(1)}, u32[]{:S(2)}, u32[]{:S(2)}) collective-permute-start(f32[4,32,128]{2,1,0:T(8,128)S(1)} %get-tuple-element.58), channel_id=1, source_target_pairs={{0,9},{1,8},{2,11},{3,10},{4,13},{5,12},{6,15},{7,14},{8,17},{9,16... | collective-permute-start | bytes 196616 | tf_op jit(solution)/shard_map/ppermute | solution.py:31
  38.6 2.3 %collective-permute-start.20 = (f32[4,32,128]{2,1,0:T(8,128)S(1)}, f32[4,32,128]{2,1,0:T(8,128)S(1)}, u32[]{:S(2)}, u32[]{:S(2)}) collective-permute-start(f32[4,32,128]{2,1,0:T(8,128)S(1)} %get-tuple-element.60), channel_id=1, source_target_pairs={{0,4},{1,5},{2,6},{3,7},{4,0},{5,1},{6,2},{7,3},{8,12},{9,13},{10,... | collective-permute-start | bytes 196616 | tf_op jit(solution)/shard_map/ppermute | solution.py:31
  41.7 3.0 %collective-permute-start.18 = (f32[2,32,128]{2,1,0:T(8,128)S(1)}, f32[2,32,128]{2,1,0:T(8,128)S(1)}, u32[]{:S(2)}, u32[]{:S(2)}) collective-permute-start(f32[2,32,128]{2,1,0:T(8,128)S(1)} %pad_maximum_fusion.13), channel_id=1, source_target_pairs={{0,6},{1,7},{2,4},{3,5},{4,2},{5,3},{6,0},{7,1},{8,14},{9,15},{10,... | collective-permute-start | bytes 98312 | tf_op jit(solution)/shard_map/ppermute | solution.py:31
  44.9 1.7 %collective-permute-start.21 = (f32[2,32,128]{2,1,0:T(8,128)S(1)}, f32[2,32,128]{2,1,0:T(8,128)S(1)}, u32[]{:S(2)}, u32[]{:S(2)}) collective-permute-start(f32[2,32,128]{2,1,0:T(8,128)S(1)} %pad_maximum_fusion.15), channel_id=1, source_target_pairs={{0,3},{1,2},{2,1},{3,0},{4,7},{5,6},{6,5},{7,4},{8,11},{9,10},{10,... | collective-permute-start | bytes 98312 | tf_op jit(solution)/shard_map/ppermute | solution.py:31
  48.4 1.5 %collective-permute-done.19.refs_1_ = f32[2,32,128]{2,1,0:T(8,128)S(1)} collective-permute-done((f32[2,32,128]{2,1,0:T(8,128)S(1)}, f32[2,32,128]{2,1,0:T(8,128)S(1)}, u32[]{:S(2)}, u32[]{:S(2)}) %collective-permute-start.19) | collective-permute-done | bytes 32800 | tf_op jit(solution)/shard_map/ppermute | solution.py:31
  51.2 1.2 %later_level.7 = (f32[129,32,128]{2,1,0:T(8,128)S(1)}, f32[4,32,128]{2,1,0:T(8,128)S(1)}, f32[4,32,128]{2,1,0:T(8,128)S(1)}, f32[4,32,128]{2,1,0:T(8,128)S(1)}, f32[4,32,128]{2,1,0:T(8,128)S(1)}) custom-call(s32[294]{0:T(512)S(1)} %get-tuple-element.39.plan, s32[5,1,8]{2,1,0:T(1,128)S(1)} %get-tuple-element.40.peers, ...), custom_call_target="tpu_custom_call", output_to_operand_aliasing={{0}: (17, {})} | custom-call | tf_op jit(solution)/shard_map/later_level/pallas_call | solution.py:225
  52.6 2.0 %collective-permute-start.25 = (f32[4,32,128]{2,1,0:T(8,128)S(1)}, f32[4,32,128]{2,1,0:T(8,128)S(1)}, u32[]{:S(2)}, u32[]{:S(2)}) collective-permute-start(f32[4,32,128]{2,1,0:T(8,128)S(1)} %get-tuple-element.63), channel_id=1, source_target_pairs={{0,9},{1,8},{2,11},{3,10},{4,13},{5,12},{6,15},{7,14},{8,17},{9,16... | collective-permute-start | bytes 196616 | tf_op jit(solution)/shard_map/ppermute | solution.py:31
  54.6 2.5 %collective-permute-start.28 = (f32[4,32,128]{2,1,0:T(8,128)S(1)}, f32[4,32,128]{2,1,0:T(8,128)S(1)}, u32[]{:S(2)}, u32[]{:S(2)}) collective-permute-start(f32[4,32,128]{2,1,0:T(8,128)S(1)} %get-tuple-element.65), channel_id=1, source_target_pairs={{0,4},{1,5},{2,6},{3,7},{4,0},{5,1},{6,2},{7,3},{8,12},{9,13},{10,... | collective-permute-start | bytes 196616 | tf_op jit(solution)/shard_map/ppermute | solution.py:31
  57.2 3.1 %collective-permute-start.26 = (f32[2,32,128]{2,1,0:T(8,128)S(1)}, f32[2,32,128]{2,1,0:T(8,128)S(1)}, u32[]{:S(2)}, u32[]{:S(2)}) collective-permute-start(f32[2,32,128]{2,1,0:T(8,128)S(1)} %pad_maximum_fusion.17), channel_id=1, source_target_pairs={{0,6},{1,7},{2,4},{3,5},{4,2},{5,3},{6,0},{7,1},{8,14},{9,15},{10,... | collective-permute-start | bytes 98312 | tf_op jit(solution)/shard_map/ppermute | solution.py:31
  60.8 1.5 %collective-permute-start.29 = (f32[2,32,128]{2,1,0:T(8,128)S(1)}, f32[2,32,128]{2,1,0:T(8,128)S(1)}, u32[]{:S(2)}, u32[]{:S(2)}) collective-permute-start(f32[2,32,128]{2,1,0:T(8,128)S(1)} %pad_maximum_fusion.19), channel_id=1, source_target_pairs={{0,3},{1,2},{2,1},{3,0},{4,7},{5,6},{6,5},{7,4},{8,11},{9,10},{10,... | collective-permute-start | bytes 98312 | tf_op jit(solution)/shard_map/ppermute | solution.py:31
  62.3 1.3 %collective-permute-start.31 = (f32[4,32,128]{2,1,0:T(8,128)S(1)}, f32[4,32,128]{2,1,0:T(8,128)S(1)}, u32[]{:S(2)}, u32[]{:S(2)}) collective-permute-start(f32[4,32,128]{2,1,0:T(8,128)S(1)} %pad_maximum_fusion.3), channel_id=1, source_target_pairs={{0,2},{1,3},{2,0},{3,1},{4,6},{5,7},{6,4},{7,5},{8,10},{9,11},{10,... | collective-permute-start | bytes 196616 | tf_op jit(solution)/shard_map/ppermute | solution.py:31
  67.5 1.2 %later_level.8 = (f32[129,32,128]{2,1,0:T(8,128)S(1)}, f32[4,32,128]{2,1,0:T(8,128)S(1)}, f32[4,32,128]{2,1,0:T(8,128)S(1)}, f32[4,32,128]{2,1,0:T(8,128)S(1)}, f32[4,32,128]{2,1,0:T(8,128)S(1)}) custom-call(s32[294]{0:T(512)S(1)} %get-tuple-element.39.plan, s32[5,1,8]{2,1,0:T(1,128)S(1)} %get-tuple-element.40.peers, ...), custom_call_target="tpu_custom_call", output_to_operand_aliasing={{0}: (17, {})} | custom-call | tf_op jit(solution)/shard_map/later_level/pallas_call | solution.py:225
  68.8 1.5 %collective-permute-start.33 = (f32[4,32,128]{2,1,0:T(8,128)S(1)}, f32[4,32,128]{2,1,0:T(8,128)S(1)}, u32[]{:S(2)}, u32[]{:S(2)}) collective-permute-start(f32[4,32,128]{2,1,0:T(8,128)S(1)} %get-tuple-element.68), channel_id=1, source_target_pairs={{0,9},{1,8},{2,11},{3,10},{4,13},{5,12},{6,15},{7,14},{8,17},{9,16... | collective-permute-start | bytes 196616 | tf_op jit(solution)/shard_map/ppermute | solution.py:31
  70.3 2.8 %collective-permute-start.36 = (f32[4,32,128]{2,1,0:T(8,128)S(1)}, f32[4,32,128]{2,1,0:T(8,128)S(1)}, u32[]{:S(2)}, u32[]{:S(2)}) collective-permute-start(f32[4,32,128]{2,1,0:T(8,128)S(1)} %get-tuple-element.70), channel_id=1, source_target_pairs={{0,4},{1,5},{2,6},{3,7},{4,0},{5,1},{6,2},{7,3},{8,12},{9,13},{10,... | collective-permute-start | bytes 196616 | tf_op jit(solution)/shard_map/ppermute | solution.py:31
  73.5 2.9 %collective-permute-start.34 = (f32[2,32,128]{2,1,0:T(8,128)S(1)}, f32[2,32,128]{2,1,0:T(8,128)S(1)}, u32[]{:S(2)}, u32[]{:S(2)}) collective-permute-start(f32[2,32,128]{2,1,0:T(8,128)S(1)} %pad_maximum_fusion.21), channel_id=1, source_target_pairs={{0,6},{1,7},{2,4},{3,5},{4,2},{5,3},{6,0},{7,1},{8,14},{9,15},{10,... | collective-permute-start | bytes 98312 | tf_op jit(solution)/shard_map/ppermute | solution.py:31
  76.7 1.5 %collective-permute-start.37 = (f32[2,32,128]{2,1,0:T(8,128)S(1)}, f32[2,32,128]{2,1,0:T(8,128)S(1)}, u32[]{:S(2)}, u32[]{:S(2)}) collective-permute-start(f32[2,32,128]{2,1,0:T(8,128)S(1)} %pad_maximum_fusion.23), channel_id=1, source_target_pairs={{0,3},{1,2},{2,1},{3,0},{4,7},{5,6},{6,5},{7,4},{8,11},{9,10},{10,... | collective-permute-start | bytes 98312 | tf_op jit(solution)/shard_map/ppermute | solution.py:31
  79.0 1.2 %collective-permute-start.38 = (f32[2,32,128]{2,1,0:T(8,128)S(1)}, f32[2,32,128]{2,1,0:T(8,128)S(1)}, u32[]{:S(2)}, u32[]{:S(2)}) collective-permute-start(f32[2,32,128]{2,1,0:T(8,128)S(1)} %pad_maximum_fusion.24), channel_id=1, source_target_pairs={{0,1},{1,0},{2,3},{3,2},{4,5},{5,4},{6,7},{7,6},{8,9},{9,8},{10,11... | collective-permute-start | bytes 98312 | tf_op jit(solution)/shard_map/ppermute | solution.py:31
  83.0 2.1 %later_level.9 = (f32[129,32,128]{2,1,0:T(8,128)S(1)}, f32[48,32,128]{2,1,0:T(8,128)}) custom-call(s32[294]{0:T(512)S(1)} %get-tuple-element.39.plan, s32[5,1,8]{2,1,0:T(1,128)S(1)} %get-tuple-element.40.peers, s32[5,1,8]{2,1,0:T(1,128)S(1)} %get-tuple-element.41.downs, s32[4,48]{1,0:T(4,128)S(1)} %get-tuple-element.42.slots, ...), custom_call_target="tpu_custom_call", output_to_operand_aliasing={{0}: (17, {})} | custom-call | tf_op jit(solution)/shard_map/later_level/pallas_call | solution.py:225
  (99 shorter events, 19.8 us)
Async XLA Ops:
  2.4 6.8 %collective-permute-start = (f32[4,32,128]{2,1,0:T(8,128)S(1)}, f32[4,32,128]{2,1,0:T(8,128)S(1)}, u32[]{:S(2)}, u32[]{:S(2)}) collective-permute-start(f32[4,32,128]{2,1,0:T(8,128)S(1)} %get-tuple-element.47), channel_id=1, source_target_pairs={{0,8},{1,9},{2,10},{3,11},{4,12},{5,13},{6,14},{7,15},{8,16},{9,17... | collective-permute-start | bytes 196616 | tf_op jit(solution)/shard_map/ppermute | solution.py:31
  2.9 6.3 %collective-permute-start.1 = (f32[4,32,128]{2,1,0:T(8,128)S(1)}, f32[4,32,128]{2,1,0:T(8,128)S(1)}, u32[]{:S(2)}, u32[]{:S(2)}) collective-permute-start(f32[4,32,128]{2,1,0:T(8,128)S(1)} %get-tuple-element.48), channel_id=1, source_target_pairs={{0,9},{1,8},{2,11},{3,10},{4,13},{5,12},{6,15},{7,14},{8,17},{9,16... | collective-permute-start | bytes 196616 | tf_op jit(solution)/shard_map/ppermute | solution.py:31
  6.7 6.7 %collective-permute-start.4 = (f32[4,32,128]{2,1,0:T(8,128)S(1)}, f32[4,32,128]{2,1,0:T(8,128)S(1)}, u32[]{:S(2)}, u32[]{:S(2)}) collective-permute-start(f32[4,32,128]{2,1,0:T(8,128)S(1)} %get-tuple-element.50), channel_id=1, source_target_pairs={{0,4},{1,5},{2,6},{3,7},{4,0},{5,1},{6,2},{7,3},{8,12},{9,13},{10,... | collective-permute-start | bytes 196616 | tf_op jit(solution)/shard_map/ppermute | solution.py:31
  9.3 7.6 %collective-permute-start.2 = (f32[2,32,128]{2,1,0:T(8,128)S(1)}, f32[2,32,128]{2,1,0:T(8,128)S(1)}, u32[]{:S(2)}, u32[]{:S(2)}) collective-permute-start(f32[2,32,128]{2,1,0:T(8,128)S(1)} %pad_maximum_fusion.5), channel_id=1, source_target_pairs={{0,6},{1,7},{2,4},{3,5},{4,2},{5,3},{6,0},{7,1},{8,14},{9,15},{10,... | collective-permute-start | bytes 98312 | tf_op jit(solution)/shard_map/ppermute | solution.py:31
  12.3 4.8 %collective-permute-start.3 = (f32[2,32,128]{2,1,0:T(8,128)S(1)}, f32[2,32,128]{2,1,0:T(8,128)S(1)}, u32[]{:S(2)}, u32[]{:S(2)}) collective-permute-start(f32[2,32,128]{2,1,0:T(8,128)S(1)} %pad_maximum_fusion.6), channel_id=1, source_target_pairs={{0,4},{1,5},{2,6},{3,7},{4,0},{5,1},{6,2},{7,3},{8,12},{9,13},{10,... | collective-permute-start | bytes 98312 | tf_op jit(solution)/shard_map/ppermute | solution.py:31
  13.3 5.1 %collective-permute-start.5 = (f32[2,32,128]{2,1,0:T(8,128)S(1)}, f32[2,32,128]{2,1,0:T(8,128)S(1)}, u32[]{:S(2)}, u32[]{:S(2)}) collective-permute-start(f32[2,32,128]{2,1,0:T(8,128)S(1)} %pad_maximum_fusion.7), channel_id=1, source_target_pairs={{0,3},{1,2},{2,1},{3,0},{4,7},{5,6},{6,5},{7,4},{8,11},{9,10},{10,... | collective-permute-start | bytes 98312 | tf_op jit(solution)/shard_map/ppermute | solution.py:31
  14.1 5.2 %collective-permute-start.7 = (f32[4,32,128]{2,1,0:T(8,128)S(1)}, f32[4,32,128]{2,1,0:T(8,128)S(1)}, u32[]{:S(2)}, u32[]{:S(2)}) collective-permute-start(f32[4,32,128]{2,1,0:T(8,128)S(1)} %pad_maximum_fusion), channel_id=1, source_target_pairs={{0,2},{1,3},{2,0},{3,1},{4,6},{5,7},{6,4},{7,5},{8,10},{9,11},{10,... | collective-permute-start | bytes 196616 | tf_op jit(solution)/shard_map/ppermute | solution.py:31
  20.5 4.7 %collective-permute-start.8 = (f32[4,32,128]{2,1,0:T(8,128)S(1)}, f32[4,32,128]{2,1,0:T(8,128)S(1)}, u32[]{:S(2)}, u32[]{:S(2)}) collective-permute-start(f32[4,32,128]{2,1,0:T(8,128)S(1)} %get-tuple-element.52), channel_id=1, source_target_pairs={{0,8},{1,9},{2,10},{3,11},{4,12},{5,13},{6,14},{7,15},{8,16},{9,17... | collective-permute-start | bytes 196616 | tf_op jit(solution)/shard_map/ppermute | solution.py:31
  20.6 4.7 %collective-permute-start.9 = (f32[4,32,128]{2,1,0:T(8,128)S(1)}, f32[4,32,128]{2,1,0:T(8,128)S(1)}, u32[]{:S(2)}, u32[]{:S(2)}) collective-permute-start(f32[4,32,128]{2,1,0:T(8,128)S(1)} %get-tuple-element.53), channel_id=1, source_target_pairs={{0,9},{1,8},{2,11},{3,10},{4,13},{5,12},{6,15},{7,14},{8,17},{9,16... | collective-permute-start | bytes 196616 | tf_op jit(solution)/shard_map/ppermute | solution.py:31
  22.3 6.7 %collective-permute-start.12 = (f32[4,32,128]{2,1,0:T(8,128)S(1)}, f32[4,32,128]{2,1,0:T(8,128)S(1)}, u32[]{:S(2)}, u32[]{:S(2)}) collective-permute-start(f32[4,32,128]{2,1,0:T(8,128)S(1)} %get-tuple-element.55), channel_id=1, source_target_pairs={{0,4},{1,5},{2,6},{3,7},{4,0},{5,1},{6,2},{7,3},{8,12},{9,13},{10,... | collective-permute-start | bytes 196616 | tf_op jit(solution)/shard_map/ppermute | solution.py:31
  25.3 7.4 %collective-permute-start.10 = (f32[2,32,128]{2,1,0:T(8,128)S(1)}, f32[2,32,128]{2,1,0:T(8,128)S(1)}, u32[]{:S(2)}, u32[]{:S(2)}) collective-permute-start(f32[2,32,128]{2,1,0:T(8,128)S(1)} %pad_maximum_fusion.9), channel_id=1, source_target_pairs={{0,6},{1,7},{2,4},{3,5},{4,2},{5,3},{6,0},{7,1},{8,14},{9,15},{10,... | collective-permute-start | bytes 98312 | tf_op jit(solution)/shard_map/ppermute | solution.py:31
  29.1 4.8 %collective-permute-start.11 = (f32[2,32,128]{2,1,0:T(8,128)S(1)}, f32[2,32,128]{2,1,0:T(8,128)S(1)}, u32[]{:S(2)}, u32[]{:S(2)}) collective-permute-start(f32[2,32,128]{2,1,0:T(8,128)S(1)} %pad_maximum_fusion.10), channel_id=1, source_target_pairs={{0,4},{1,5},{2,6},{3,7},{4,0},{5,1},{6,2},{7,3},{8,12},{9,13},{10,... | collective-permute-start | bytes 98312 | tf_op jit(solution)/shard_map/ppermute | solution.py:31
  29.1 5.2 %collective-permute-start.13 = (f32[2,32,128]{2,1,0:T(8,128)S(1)}, f32[2,32,128]{2,1,0:T(8,128)S(1)}, u32[]{:S(2)}, u32[]{:S(2)}) collective-permute-start(f32[2,32,128]{2,1,0:T(8,128)S(1)} %pad_maximum_fusion.11), channel_id=1, source_target_pairs={{0,3},{1,2},{2,1},{3,0},{4,7},{5,6},{6,5},{7,4},{8,11},{9,10},{10,... | collective-permute-start | bytes 98312 | tf_op jit(solution)/shard_map/ppermute | solution.py:31
  30.8 5.0 %collective-permute-start.15 = (f32[4,32,128]{2,1,0:T(8,128)S(1)}, f32[4,32,128]{2,1,0:T(8,128)S(1)}, u32[]{:S(2)}, u32[]{:S(2)}) collective-permute-start(f32[4,32,128]{2,1,0:T(8,128)S(1)} %pad_maximum_fusion.1), channel_id=1, source_target_pairs={{0,2},{1,3},{2,0},{3,1},{4,6},{5,7},{6,4},{7,5},{8,10},{9,11},{10,... | collective-permute-start | bytes 196616 | tf_op jit(solution)/shard_map/ppermute | solution.py:31
  37.1 4.6 %collective-permute-start.17 = (f32[4,32,128]{2,1,0:T(8,128)S(1)}, f32[4,32,128]{2,1,0:T(8,128)S(1)}, u32[]{:S(2)}, u32[]{:S(2)}) collective-permute-start(f32[4,32,128]{2,1,0:T(8,128)S(1)} %get-tuple-element.58), channel_id=1, source_target_pairs={{0,9},{1,8},{2,11},{3,10},{4,13},{5,12},{6,15},{7,14},{8,17},{9,16... | collective-permute-start | bytes 196616 | tf_op jit(solution)/shard_map/ppermute | solution.py:31
  38.6 6.2 %collective-permute-start.20 = (f32[4,32,128]{2,1,0:T(8,128)S(1)}, f32[4,32,128]{2,1,0:T(8,128)S(1)}, u32[]{:S(2)}, u32[]{:S(2)}) collective-permute-start(f32[4,32,128]{2,1,0:T(8,128)S(1)} %get-tuple-element.60), channel_id=1, source_target_pairs={{0,4},{1,5},{2,6},{3,7},{4,0},{5,1},{6,2},{7,3},{8,12},{9,13},{10,... | collective-permute-start | bytes 196616 | tf_op jit(solution)/shard_map/ppermute | solution.py:31
  41.7 6.7 %collective-permute-start.18 = (f32[2,32,128]{2,1,0:T(8,128)S(1)}, f32[2,32,128]{2,1,0:T(8,128)S(1)}, u32[]{:S(2)}, u32[]{:S(2)}) collective-permute-start(f32[2,32,128]{2,1,0:T(8,128)S(1)} %pad_maximum_fusion.13), channel_id=1, source_target_pairs={{0,6},{1,7},{2,4},{3,5},{4,2},{5,3},{6,0},{7,1},{8,14},{9,15},{10,... | collective-permute-start | bytes 98312 | tf_op jit(solution)/shard_map/ppermute | solution.py:31
  44.7 5.2 %collective-permute-start.19 = (f32[2,32,128]{2,1,0:T(8,128)S(1)}, f32[2,32,128]{2,1,0:T(8,128)S(1)}, u32[]{:S(2)}, u32[]{:S(2)}) collective-permute-start(f32[2,32,128]{2,1,0:T(8,128)S(1)} %pad_maximum_fusion.14), channel_id=1, source_target_pairs={{0,4},{1,5},{2,6},{3,7},{4,0},{5,1},{6,2},{7,3},{8,12},{9,13},{10,... | collective-permute-start | bytes 98312 | tf_op jit(solution)/shard_map/ppermute | solution.py:31
  44.9 5.5 %collective-permute-start.21 = (f32[2,32,128]{2,1,0:T(8,128)S(1)}, f32[2,32,128]{2,1,0:T(8,128)S(1)}, u32[]{:S(2)}, u32[]{:S(2)}) collective-permute-start(f32[2,32,128]{2,1,0:T(8,128)S(1)} %pad_maximum_fusion.15), channel_id=1, source_target_pairs={{0,3},{1,2},{2,1},{3,0},{4,7},{5,6},{6,5},{7,4},{8,11},{9,10},{10,... | collective-permute-start | bytes 98312 | tf_op jit(solution)/shard_map/ppermute | solution.py:31
  46.5 4.7 %collective-permute-start.23 = (f32[4,32,128]{2,1,0:T(8,128)S(1)}, f32[4,32,128]{2,1,0:T(8,128)S(1)}, u32[]{:S(2)}, u32[]{:S(2)}) collective-permute-start(f32[4,32,128]{2,1,0:T(8,128)S(1)} %pad_maximum_fusion.2), channel_id=1, source_target_pairs={{0,2},{1,3},{2,0},{3,1},{4,6},{5,7},{6,4},{7,5},{8,10},{9,11},{10,... | collective-permute-start | bytes 196616 | tf_op jit(solution)/shard_map/ppermute | solution.py:31
  52.6 4.6 %collective-permute-start.25 = (f32[4,32,128]{2,1,0:T(8,128)S(1)}, f32[4,32,128]{2,1,0:T(8,128)S(1)}, u32[]{:S(2)}, u32[]{:S(2)}) collective-permute-start(f32[4,32,128]{2,1,0:T(8,128)S(1)} %get-tuple-element.63), channel_id=1, source_target_pairs={{0,9},{1,8},{2,11},{3,10},{4,13},{5,12},{6,15},{7,14},{8,17},{9,16... | collective-permute-start | bytes 196616 | tf_op jit(solution)/shard_map/ppermute | solution.py:31
  54.6 6.2 %collective-permute-start.28 = (f32[4,32,128]{2,1,0:T(8,128)S(1)}, f32[4,32,128]{2,1,0:T(8,128)S(1)}, u32[]{:S(2)}, u32[]{:S(2)}) collective-permute-start(f32[4,32,128]{2,1,0:T(8,128)S(1)} %get-tuple-element.65), channel_id=1, source_target_pairs={{0,4},{1,5},{2,6},{3,7},{4,0},{5,1},{6,2},{7,3},{8,12},{9,13},{10,... | collective-permute-start | bytes 196616 | tf_op jit(solution)/shard_map/ppermute | solution.py:31
  57.2 7.1 %collective-permute-start.26 = (f32[2,32,128]{2,1,0:T(8,128)S(1)}, f32[2,32,128]{2,1,0:T(8,128)S(1)}, u32[]{:S(2)}, u32[]{:S(2)}) collective-permute-start(f32[2,32,128]{2,1,0:T(8,128)S(1)} %pad_maximum_fusion.17), channel_id=1, source_target_pairs={{0,6},{1,7},{2,4},{3,5},{4,2},{5,3},{6,0},{7,1},{8,14},{9,15},{10,... | collective-permute-start | bytes 98312 | tf_op jit(solution)/shard_map/ppermute | solution.py:31
  60.4 4.8 %collective-permute-start.27 = (f32[2,32,128]{2,1,0:T(8,128)S(1)}, f32[2,32,128]{2,1,0:T(8,128)S(1)}, u32[]{:S(2)}, u32[]{:S(2)}) collective-permute-start(f32[2,32,128]{2,1,0:T(8,128)S(1)} %pad_maximum_fusion.18), channel_id=1, source_target_pairs={{0,4},{1,5},{2,6},{3,7},{4,0},{5,1},{6,2},{7,3},{8,12},{9,13},{10,... | collective-permute-start | bytes 98312 | tf_op jit(solution)/shard_map/ppermute | solution.py:31
  60.8 5.6 %collective-permute-start.29 = (f32[2,32,128]{2,1,0:T(8,128)S(1)}, f32[2,32,128]{2,1,0:T(8,128)S(1)}, u32[]{:S(2)}, u32[]{:S(2)}) collective-permute-start(f32[2,32,128]{2,1,0:T(8,128)S(1)} %pad_maximum_fusion.19), channel_id=1, source_target_pairs={{0,3},{1,2},{2,1},{3,0},{4,7},{5,6},{6,5},{7,4},{8,11},{9,10},{10,... | collective-permute-start | bytes 98312 | tf_op jit(solution)/shard_map/ppermute | solution.py:31
  62.3 5.2 %collective-permute-start.31 = (f32[4,32,128]{2,1,0:T(8,128)S(1)}, f32[4,32,128]{2,1,0:T(8,128)S(1)}, u32[]{:S(2)}, u32[]{:S(2)}) collective-permute-start(f32[4,32,128]{2,1,0:T(8,128)S(1)} %pad_maximum_fusion.3), channel_id=1, source_target_pairs={{0,2},{1,3},{2,0},{3,1},{4,6},{5,7},{6,4},{7,5},{8,10},{9,11},{10,... | collective-permute-start | bytes 196616 | tf_op jit(solution)/shard_map/ppermute | solution.py:31
  68.8 4.6 %collective-permute-start.33 = (f32[4,32,128]{2,1,0:T(8,128)S(1)}, f32[4,32,128]{2,1,0:T(8,128)S(1)}, u32[]{:S(2)}, u32[]{:S(2)}) collective-permute-start(f32[4,32,128]{2,1,0:T(8,128)S(1)} %get-tuple-element.68), channel_id=1, source_target_pairs={{0,9},{1,8},{2,11},{3,10},{4,13},{5,12},{6,15},{7,14},{8,17},{9,16... | collective-permute-start | bytes 196616 | tf_op jit(solution)/shard_map/ppermute | solution.py:31
  70.3 6.4 %collective-permute-start.36 = (f32[4,32,128]{2,1,0:T(8,128)S(1)}, f32[4,32,128]{2,1,0:T(8,128)S(1)}, u32[]{:S(2)}, u32[]{:S(2)}) collective-permute-start(f32[4,32,128]{2,1,0:T(8,128)S(1)} %get-tuple-element.70), channel_id=1, source_target_pairs={{0,4},{1,5},{2,6},{3,7},{4,0},{5,1},{6,2},{7,3},{8,12},{9,13},{10,... | collective-permute-start | bytes 196616 | tf_op jit(solution)/shard_map/ppermute | solution.py:31
  73.5 6.8 %collective-permute-start.34 = (f32[2,32,128]{2,1,0:T(8,128)S(1)}, f32[2,32,128]{2,1,0:T(8,128)S(1)}, u32[]{:S(2)}, u32[]{:S(2)}) collective-permute-start(f32[2,32,128]{2,1,0:T(8,128)S(1)} %pad_maximum_fusion.21), channel_id=1, source_target_pairs={{0,6},{1,7},{2,4},{3,5},{4,2},{5,3},{6,0},{7,1},{8,14},{9,15},{10,... | collective-permute-start | bytes 98312 | tf_op jit(solution)/shard_map/ppermute | solution.py:31
  76.4 4.9 %collective-permute-start.35 = (f32[2,32,128]{2,1,0:T(8,128)S(1)}, f32[2,32,128]{2,1,0:T(8,128)S(1)}, u32[]{:S(2)}, u32[]{:S(2)}) collective-permute-start(f32[2,32,128]{2,1,0:T(8,128)S(1)} %pad_maximum_fusion.22), channel_id=1, source_target_pairs={{0,4},{1,5},{2,6},{3,7},{4,0},{5,1},{6,2},{7,3},{8,12},{9,13},{10,... | collective-permute-start | bytes 98312 | tf_op jit(solution)/shard_map/ppermute | solution.py:31
  76.7 5.3 %collective-permute-start.37 = (f32[2,32,128]{2,1,0:T(8,128)S(1)}, f32[2,32,128]{2,1,0:T(8,128)S(1)}, u32[]{:S(2)}, u32[]{:S(2)}) collective-permute-start(f32[2,32,128]{2,1,0:T(8,128)S(1)} %pad_maximum_fusion.23), channel_id=1, source_target_pairs={{0,3},{1,2},{2,1},{3,0},{4,7},{5,6},{6,5},{7,4},{8,11},{9,10},{10,... | collective-permute-start | bytes 98312 | tf_op jit(solution)/shard_map/ppermute | solution.py:31
  78.2 4.7 %collective-permute-start.39 = (f32[4,32,128]{2,1,0:T(8,128)S(1)}, f32[4,32,128]{2,1,0:T(8,128)S(1)}, u32[]{:S(2)}, u32[]{:S(2)}) collective-permute-start(f32[4,32,128]{2,1,0:T(8,128)S(1)} %pad_maximum_fusion.4), channel_id=1, source_target_pairs={{0,2},{1,3},{2,0},{3,1},{4,6},{5,7},{6,4},{7,5},{8,10},{9,11},{10,... | collective-permute-start | bytes 196616 | tf_op jit(solution)/shard_map/ppermute | solution.py:31
  (8 other events, 32.5 us)

commit v3 on v2

--- a/solution.py
+++ b/solution.py
@@ -49,18 +49,12 @@
 def sort_blocks(blocks, levels, plan):
     stride = blocks + 1
     count = plan.shape[0] // stride
-    together = 4 if blocks % 4 == 0 else 1
-
-    def place(step, ends):
-        for i in range(together):
-            block = step * together + i
-            level = levels[block]
-            for end in ends:
-                plan[end] = block
-            ends = tuple(end + jnp.where(level == own, 1, 0) for own, end in enumerate(ends))
-        return ends
-
-    ends = lax.fori_loop(0, blocks // together, place, tuple(jnp.int32(own * stride) for own in range(count)))
+    ends = [jnp.int32(own * stride) for own in range(count)]
+    for block in range(blocks):
+        level = levels[block]
+        for end in ends:
+            plan[end] = block
+        ends = [end + jnp.where(level == own, 1, 0) for own, end in enumerate(ends)]
     for own, end in enumerate(ends):
         plan[own * stride + blocks] = end - own * stride
 
@@ -75,8 +69,10 @@
             kin[block], inflow_of(block), precision=lax.Precision.HIGHEST, preferred_element_type=jnp.float32
         )
         solved.append(weight[pl.ds(block, 1), :] * mixed)
-    for block, value in zip(ids, solved):
-        pool[block] = value
+    if pool is not None:
+        for block, value in zip(ids, solved):
+            pool[block] = value
+    return count, ids, solved
 
 
 def fill_sends(level, rows, columns, blocks, peers, downs, pool, outs):
@@ -108,15 +104,12 @@
         copy.start()
     blocks = residual.shape[0]
     pool[blocks] = jnp.zeros(pool.shape[1:], pool.dtype)
-    copies[0].wait()
+    for copy in copies[:6]:
+        copy.wait()
     sort_blocks(blocks, levels, plan)
-    copies[-1].start()
-    copies[1].wait()
     for i in range(kin.shape[1]):
         kin[:, i, :] = jnp.transpose(kin_here[i])
-    for copy in copies[2:6]:
-        copy.wait()
-
+    copies[-1].start()
     solve_blocks(0, blocks, plan, lambda block: residual[block], kin, weight, pool)
     fill_sends(0, rows, columns, blocks, peers, downs, pool, outs)
     for copy in copies[6:]:
@@ -134,6 +127,10 @@
     outs = refs
     blocks, upw = residual.shape[0], slots.shape[0]
     rounds, groups = peers.shape[0], rows * columns
+    if level == rounds:
+        out, last, sems = refs
+        earlier = pltpu.make_async_copy(pool.at[pl.ds(0, blocks)], out, sems.at[last.shape[0]])
+        earlier.start()
     here = lax.axis_index("blk")
     row, column = here // columns, lax.rem(here, columns)
     peers_first = blocks + 1 + (level - 1) * groups
@@ -158,11 +155,19 @@
             inflow = inflow + parts[k : k + 1, :] * pool[slots[k, block]]
         return inflow
 
-    solve_blocks(level, blocks, plan, inflow_of, kin, weight, pool)
     if level < rounds:
+        solve_blocks(level, blocks, plan, inflow_of, kin, weight, pool)
         fill_sends(level, rows, columns, blocks, peers, downs, pool, outs)
-    else:
-        outs[0][...] = pool[pl.ds(0, blocks)]
+        return
+    count, ids, solved = solve_blocks(level, blocks, plan, inflow_of, kin, weight, None)
+    for i, value in enumerate(solved):
+        last[i] = value
+    copies = [pltpu.make_async_copy(last.at[i], out.at[block], sems.at[i]) for i, block in enumerate(ids)]
+    earlier.wait()
+    for i, copy in enumerate(copies):
+        pl.when(i < count)(copy.start)
+    for i, copy in enumerate(copies):
+        pl.when(i < count)(copy.wait)
 
 
 def shards(
@@ -222,11 +227,15 @@
         else:
             out_shapes = [jax.ShapeDtypeStruct(residual.shape, residual.dtype)]
         operands = held + [kin] + arrived + from_above + from_halves + [pool]
+        own = blocks * 8 // 24
         pool, *outs = pl.pallas_call(
             functools.partial(later_level, level, rows, columns),
             in_specs=[smem] * 4 + [vmem] * (len(operands) - 4),
-            out_specs=[vmem] * (1 + len(out_shapes)),
+            out_specs=[vmem] + [vmem if level < rounds else hbm] * len(out_shapes),
             out_shape=[pool_shape] + out_shapes,
+            scratch_shapes=[]
+            if level < rounds
+            else [pltpu.VMEM((own, species, cells), jnp.float32), pltpu.SemaphoreType.DMA((own + 1,))],
             input_output_aliases={len(operands) - 1: 0},
             compiler_params=params,
             name="later_level",

time: 85.2 us -> 86.3 us (1.013)
  Pallas kernels: 9.47 us -> 10.6 us
    pallas_call x1, Pallas kernels: 2.41 us -> 3.3 us  [shards(): pl.pallas_call(functools.partial(first_level, rows, columns), in_specs=[h...]
where the time goes in v3:
time: 86.3 us; the launch traced here: 86.2 us
  starting transfers between devices  58.1 us (67%)
  waiting for transfers between devices  17.1 us (20%)
  Pallas kernels  10.6 us (12%)
    ppermute x40, starting transfers between devices, moved(): return lax.ppermute(value, ('section', 'blk'), pairs)  58.1 us
    ppermute x40, waiting for transfers between devices, moved(): return lax.ppermute(value, ('section', 'blk'), pairs)  17.1 us
    pallas_call x5, Pallas kernels, shards(): pl.pallas_call(functools.partial(later_level, level, rows, columns), in_s...  7.3 us
    pallas_call x1, Pallas kernels, shards(): pl.pallas_call(functools.partial(first_level, rows, columns), in_specs=[h...  3.3 us
  transfers between devices with their start and end apart: 40, of which 22 were waited for; matrix products, arithmetic and copies ran while one was open for 0% of the time, Pallas kernels for 0%

profile of v3, /device:TPU:0, one launch (start us, length us, event | category | flops | bytes accessed | tf_op | source)
XLA Modules:
  0.0 86.2 jit_solution(8434496514199067770)
XLA Ops:
  0.0 3.3 %first_level.1 = (f32[129,32,128]{2,1,0:T(8,128)S(1)}, f32[48,32,32]{2,1,0:T(8,128)S(1)}, s32[294]{0:T(512)S(1)}, s32[5,1,8]{2,1,0:T(1,128)S(1)}, s32[5,1,8]{2,1...) custom-call(s32[48]{0:T(128)} %refs_0_.1, ...), custom_call_target="tpu_custom_call" | custom-call | tf_op jit(solution)/shard_map/first_level/pallas_call | solution.py:197
  3.8 3.7 %collective-permute-start.1 = (f32[4,32,128]{2,1,0:T(8,128)S(1)}, f32[4,32,128]{2,1,0:T(8,128)S(1)}, u32[]{:S(2)}, u32[]{:S(2)}) collective-permute-start(f32[4,32,128]{2,1,0:T(8,128)S(1)} %get-tuple-element.48), channel_id=1, source_target_pairs={{0,9},{1,8},{2,11},{3,10},{4,13},{5,12},{6,15},{7,14},{8,17},{9,16... | collective-permute-start | bytes 196616 | tf_op jit(solution)/shard_map/ppermute | solution.py:31
  7.5 2.6 %collective-permute-start.4 = (f32[4,32,128]{2,1,0:T(8,128)S(1)}, f32[4,32,128]{2,1,0:T(8,128)S(1)}, u32[]{:S(2)}, u32[]{:S(2)}) collective-permute-start(f32[4,32,128]{2,1,0:T(8,128)S(1)} %get-tuple-element.50), channel_id=1, source_target_pairs={{0,4},{1,5},{2,6},{3,7},{4,0},{5,1},{6,2},{7,3},{8,12},{9,13},{10,... | collective-permute-start | bytes 196616 | tf_op jit(solution)/shard_map/ppermute | solution.py:31
  10.2 3.0 %collective-permute-start.2 = (f32[2,32,128]{2,1,0:T(8,128)S(1)}, f32[2,32,128]{2,1,0:T(8,128)S(1)}, u32[]{:S(2)}, u32[]{:S(2)}) collective-permute-start(f32[2,32,128]{2,1,0:T(8,128)S(1)} %pad_maximum_fusion.5), channel_id=1, source_target_pairs={{0,6},{1,7},{2,4},{3,5},{4,2},{5,3},{6,0},{7,1},{8,14},{9,15},{10,... | collective-permute-start | bytes 98312 | tf_op jit(solution)/shard_map/ppermute | solution.py:31
  15.0 1.3 %collective-permute-start.7 = (f32[4,32,128]{2,1,0:T(8,128)S(1)}, f32[4,32,128]{2,1,0:T(8,128)S(1)}, u32[]{:S(2)}, u32[]{:S(2)}) collective-permute-start(f32[4,32,128]{2,1,0:T(8,128)S(1)} %pad_maximum_fusion), channel_id=1, source_target_pairs={{0,2},{1,3},{2,0},{3,1},{4,6},{5,7},{6,4},{7,5},{8,10},{9,11},{10,... | collective-permute-start | bytes 196616 | tf_op jit(solution)/shard_map/ppermute | solution.py:31
  16.2 1.5 %collective-permute-start.6 = (f32[2,32,128]{2,1,0:T(8,128)S(1)}, f32[2,32,128]{2,1,0:T(8,128)S(1)}, u32[]{:S(2)}, u32[]{:S(2)}) collective-permute-start(f32[2,32,128]{2,1,0:T(8,128)S(1)} %pad_maximum_fusion.8), channel_id=1, source_target_pairs={{0,1},{1,0},{2,3},{3,2},{4,5},{5,4},{6,7},{7,6},{8,9},{9,8},{10,11... | collective-permute-start | bytes 98312 | tf_op jit(solution)/shard_map/ppermute | solution.py:31
  18.0 1.3 %collective-permute-done.5.refs_2_ = f32[2,32,128]{2,1,0:T(8,128)S(1)} collective-permute-done((f32[2,32,128]{2,1,0:T(8,128)S(1)}, f32[2,32,128]{2,1,0:T(8,128)S(1)}, u32[]{:S(2)}, u32[]{:S(2)}) %collective-permute-start.5) | collective-permute-done | bytes 32800 | tf_op jit(solution)/shard_map/ppermute | solution.py:31
  20.2 1.2 %later_level.5 = (f32[129,32,128]{2,1,0:T(8,128)S(1)}, f32[4,32,128]{2,1,0:T(8,128)S(1)}, f32[4,32,128]{2,1,0:T(8,128)S(1)}, f32[4,32,128]{2,1,0:T(8,128)S(1)}, f32[4,32,128]{2,1,0:T(8,128)S(1)}) custom-call(s32[294]{0:T(512)S(1)} %get-tuple-element.39.plan, s32[5,1,8]{2,1,0:T(1,128)S(1)} %get-tuple-element.40.peers, ...), custom_call_target="tpu_custom_call", output_to_operand_aliasing={{0}: (17, {})} | custom-call | tf_op jit(solution)/shard_map/later_level/pallas_call | solution.py:231
  21.5 1.7 %collective-permute-start.9 = (f32[4,32,128]{2,1,0:T(8,128)S(1)}, f32[4,32,128]{2,1,0:T(8,128)S(1)}, u32[]{:S(2)}, u32[]{:S(2)}) collective-permute-start(f32[4,32,128]{2,1,0:T(8,128)S(1)} %get-tuple-element.53), channel_id=1, source_target_pairs={{0,9},{1,8},{2,11},{3,10},{4,13},{5,12},{6,15},{7,14},{8,17},{9,16... | collective-permute-start | bytes 196616 | tf_op jit(solution)/shard_map/ppermute | solution.py:31
  23.2 2.9 %collective-permute-start.12 = (f32[4,32,128]{2,1,0:T(8,128)S(1)}, f32[4,32,128]{2,1,0:T(8,128)S(1)}, u32[]{:S(2)}, u32[]{:S(2)}) collective-permute-start(f32[4,32,128]{2,1,0:T(8,128)S(1)} %get-tuple-element.55), channel_id=1, source_target_pairs={{0,4},{1,5},{2,6},{3,7},{4,0},{5,1},{6,2},{7,3},{8,12},{9,13},{10,... | collective-permute-start | bytes 196616 | tf_op jit(solution)/shard_map/ppermute | solution.py:31
  26.2 3.8 %collective-permute-start.10 = (f32[2,32,128]{2,1,0:T(8,128)S(1)}, f32[2,32,128]{2,1,0:T(8,128)S(1)}, u32[]{:S(2)}, u32[]{:S(2)}) collective-permute-start(f32[2,32,128]{2,1,0:T(8,128)S(1)} %pad_maximum_fusion.9), channel_id=1, source_target_pairs={{0,6},{1,7},{2,4},{3,5},{4,2},{5,3},{6,0},{7,1},{8,14},{9,15},{10,... | collective-permute-start | bytes 98312 | tf_op jit(solution)/shard_map/ppermute | solution.py:31
  30.0 1.7 %collective-permute-start.13 = (f32[2,32,128]{2,1,0:T(8,128)S(1)}, f32[2,32,128]{2,1,0:T(8,128)S(1)}, u32[]{:S(2)}, u32[]{:S(2)}) collective-permute-start(f32[2,32,128]{2,1,0:T(8,128)S(1)} %pad_maximum_fusion.11), channel_id=1, source_target_pairs={{0,3},{1,2},{2,1},{3,0},{4,7},{5,6},{6,5},{7,4},{8,11},{9,10},{10,... | collective-permute-start | bytes 98312 | tf_op jit(solution)/shard_map/ppermute | solution.py:31
  35.1 1.5 %collective-permute-done.14.refs_3_ = f32[2,32,128]{2,1,0:T(8,128)S(1)} collective-permute-done((f32[2,32,128]{2,1,0:T(8,128)S(1)}, f32[2,32,128]{2,1,0:T(8,128)S(1)}, u32[]{:S(2)}, u32[]{:S(2)}) %collective-permute-start.14) | collective-permute-done | bytes 32800 | tf_op jit(solution)/shard_map/ppermute | solution.py:31
  36.6 1.2 %later_level.6 = (f32[129,32,128]{2,1,0:T(8,128)S(1)}, f32[4,32,128]{2,1,0:T(8,128)S(1)}, f32[4,32,128]{2,1,0:T(8,128)S(1)}, f32[4,32,128]{2,1,0:T(8,128)S(1)}, f32[4,32,128]{2,1,0:T(8,128)S(1)}) custom-call(s32[294]{0:T(512)S(1)} %get-tuple-element.39.plan, s32[5,1,8]{2,1,0:T(1,128)S(1)} %get-tuple-element.40.peers, ...), custom_call_target="tpu_custom_call", output_to_operand_aliasing={{0}: (17, {})} | custom-call | tf_op jit(solution)/shard_map/later_level/pallas_call | solution.py:231
  38.0 1.6 %collective-permute-start.17 = (f32[4,32,128]{2,1,0:T(8,128)S(1)}, f32[4,32,128]{2,1,0:T(8,128)S(1)}, u32[]{:S(2)}, u32[]{:S(2)}) collective-permute-start(f32[4,32,128]{2,1,0:T(8,128)S(1)} %get-tuple-element.58), channel_id=1, source_target_pairs={{0,9},{1,8},{2,11},{3,10},{4,13},{5,12},{6,15},{7,14},{8,17},{9,16... | collective-permute-start | bytes 196616 | tf_op jit(solution)/shard_map/ppermute | solution.py:31
  39.5 2.3 %collective-permute-start.20 = (f32[4,32,128]{2,1,0:T(8,128)S(1)}, f32[4,32,128]{2,1,0:T(8,128)S(1)}, u32[]{:S(2)}, u32[]{:S(2)}) collective-permute-start(f32[4,32,128]{2,1,0:T(8,128)S(1)} %get-tuple-element.60), channel_id=1, source_target_pairs={{0,4},{1,5},{2,6},{3,7},{4,0},{5,1},{6,2},{7,3},{8,12},{9,13},{10,... | collective-permute-start | bytes 196616 | tf_op jit(solution)/shard_map/ppermute | solution.py:31
  42.6 3.0 %collective-permute-start.18 = (f32[2,32,128]{2,1,0:T(8,128)S(1)}, f32[2,32,128]{2,1,0:T(8,128)S(1)}, u32[]{:S(2)}, u32[]{:S(2)}) collective-permute-start(f32[2,32,128]{2,1,0:T(8,128)S(1)} %pad_maximum_fusion.13), channel_id=1, source_target_pairs={{0,6},{1,7},{2,4},{3,5},{4,2},{5,3},{6,0},{7,1},{8,14},{9,15},{10,... | collective-permute-start | bytes 98312 | tf_op jit(solution)/shard_map/ppermute | solution.py:31
  45.7 1.7 %collective-permute-start.21 = (f32[2,32,128]{2,1,0:T(8,128)S(1)}, f32[2,32,128]{2,1,0:T(8,128)S(1)}, u32[]{:S(2)}, u32[]{:S(2)}) collective-permute-start(f32[2,32,128]{2,1,0:T(8,128)S(1)} %pad_maximum_fusion.15), channel_id=1, source_target_pairs={{0,3},{1,2},{2,1},{3,0},{4,7},{5,6},{6,5},{7,4},{8,11},{9,10},{10,... | collective-permute-start | bytes 98312 | tf_op jit(solution)/shard_map/ppermute | solution.py:31
  49.3 1.5 %collective-permute-done.19.refs_1_ = f32[2,32,128]{2,1,0:T(8,128)S(1)} collective-permute-done((f32[2,32,128]{2,1,0:T(8,128)S(1)}, f32[2,32,128]{2,1,0:T(8,128)S(1)}, u32[]{:S(2)}, u32[]{:S(2)}) %collective-permute-start.19) | collective-permute-done | bytes 32800 | tf_op jit(solution)/shard_map/ppermute | solution.py:31
  52.1 1.2 %later_level.7 = (f32[129,32,128]{2,1,0:T(8,128)S(1)}, f32[4,32,128]{2,1,0:T(8,128)S(1)}, f32[4,32,128]{2,1,0:T(8,128)S(1)}, f32[4,32,128]{2,1,0:T(8,128)S(1)}, f32[4,32,128]{2,1,0:T(8,128)S(1)}) custom-call(s32[294]{0:T(512)S(1)} %get-tuple-element.39.plan, s32[5,1,8]{2,1,0:T(1,128)S(1)} %get-tuple-element.40.peers, ...), custom_call_target="tpu_custom_call", output_to_operand_aliasing={{0}: (17, {})} | custom-call | tf_op jit(solution)/shard_map/later_level/pallas_call | solution.py:231
  53.4 2.0 %collective-permute-start.25 = (f32[4,32,128]{2,1,0:T(8,128)S(1)}, f32[4,32,128]{2,1,0:T(8,128)S(1)}, u32[]{:S(2)}, u32[]{:S(2)}) collective-permute-start(f32[4,32,128]{2,1,0:T(8,128)S(1)} %get-tuple-element.63), channel_id=1, source_target_pairs={{0,9},{1,8},{2,11},{3,10},{4,13},{5,12},{6,15},{7,14},{8,17},{9,16... | collective-permute-start | bytes 196616 | tf_op jit(solution)/shard_map/ppermute | solution.py:31
  55.5 2.5 %collective-permute-start.28 = (f32[4,32,128]{2,1,0:T(8,128)S(1)}, f32[4,32,128]{2,1,0:T(8,128)S(1)}, u32[]{:S(2)}, u32[]{:S(2)}) collective-permute-start(f32[4,32,128]{2,1,0:T(8,128)S(1)} %get-tuple-element.65), channel_id=1, source_target_pairs={{0,4},{1,5},{2,6},{3,7},{4,0},{5,1},{6,2},{7,3},{8,12},{9,13},{10,... | collective-permute-start | bytes 196616 | tf_op jit(solution)/shard_map/ppermute | solution.py:31
  58.1 3.1 %collective-permute-start.26 = (f32[2,32,128]{2,1,0:T(8,128)S(1)}, f32[2,32,128]{2,1,0:T(8,128)S(1)}, u32[]{:S(2)}, u32[]{:S(2)}) collective-permute-start(f32[2,32,128]{2,1,0:T(8,128)S(1)} %pad_maximum_fusion.17), channel_id=1, source_target_pairs={{0,6},{1,7},{2,4},{3,5},{4,2},{5,3},{6,0},{7,1},{8,14},{9,15},{10,... | collective-permute-start | bytes 98312 | tf_op jit(solution)/shard_map/ppermute | solution.py:31
  61.7 1.5 %collective-permute-start.29 = (f32[2,32,128]{2,1,0:T(8,128)S(1)}, f32[2,32,128]{2,1,0:T(8,128)S(1)}, u32[]{:S(2)}, u32[]{:S(2)}) collective-permute-start(f32[2,32,128]{2,1,0:T(8,128)S(1)} %pad_maximum_fusion.19), channel_id=1, source_target_pairs={{0,3},{1,2},{2,1},{3,0},{4,7},{5,6},{6,5},{7,4},{8,11},{9,10},{10,... | collective-permute-start | bytes 98312 | tf_op jit(solution)/shard_map/ppermute | solution.py:31
  63.2 1.3 %collective-permute-start.31 = (f32[4,32,128]{2,1,0:T(8,128)S(1)}, f32[4,32,128]{2,1,0:T(8,128)S(1)}, u32[]{:S(2)}, u32[]{:S(2)}) collective-permute-start(f32[4,32,128]{2,1,0:T(8,128)S(1)} %pad_maximum_fusion.3), channel_id=1, source_target_pairs={{0,2},{1,3},{2,0},{3,1},{4,6},{5,7},{6,4},{7,5},{8,10},{9,11},{10,... | collective-permute-start | bytes 196616 | tf_op jit(solution)/shard_map/ppermute | solution.py:31
  68.4 1.2 %later_level.8 = (f32[129,32,128]{2,1,0:T(8,128)S(1)}, f32[4,32,128]{2,1,0:T(8,128)S(1)}, f32[4,32,128]{2,1,0:T(8,128)S(1)}, f32[4,32,128]{2,1,0:T(8,128)S(1)}, f32[4,32,128]{2,1,0:T(8,128)S(1)}) custom-call(s32[294]{0:T(512)S(1)} %get-tuple-element.39.plan, s32[5,1,8]{2,1,0:T(1,128)S(1)} %get-tuple-element.40.peers, ...), custom_call_target="tpu_custom_call", output_to_operand_aliasing={{0}: (17, {})} | custom-call | tf_op jit(solution)/shard_map/later_level/pallas_call | solution.py:231
  69.7 1.4 %collective-permute-start.33 = (f32[4,32,128]{2,1,0:T(8,128)S(1)}, f32[4,32,128]{2,1,0:T(8,128)S(1)}, u32[]{:S(2)}, u32[]{:S(2)}) collective-permute-start(f32[4,32,128]{2,1,0:T(8,128)S(1)} %get-tuple-element.68), channel_id=1, source_target_pairs={{0,9},{1,8},{2,11},{3,10},{4,13},{5,12},{6,15},{7,14},{8,17},{9,16... | collective-permute-start | bytes 196616 | tf_op jit(solution)/shard_map/ppermute | solution.py:31
  71.2 2.8 %collective-permute-start.36 = (f32[4,32,128]{2,1,0:T(8,128)S(1)}, f32[4,32,128]{2,1,0:T(8,128)S(1)}, u32[]{:S(2)}, u32[]{:S(2)}) collective-permute-start(f32[4,32,128]{2,1,0:T(8,128)S(1)} %get-tuple-element.70), channel_id=1, source_target_pairs={{0,4},{1,5},{2,6},{3,7},{4,0},{5,1},{6,2},{7,3},{8,12},{9,13},{10,... | collective-permute-start | bytes 196616 | tf_op jit(solution)/shard_map/ppermute | solution.py:31
  74.4 2.9 %collective-permute-start.34 = (f32[2,32,128]{2,1,0:T(8,128)S(1)}, f32[2,32,128]{2,1,0:T(8,128)S(1)}, u32[]{:S(2)}, u32[]{:S(2)}) collective-permute-start(f32[2,32,128]{2,1,0:T(8,128)S(1)} %pad_maximum_fusion.21), channel_id=1, source_target_pairs={{0,6},{1,7},{2,4},{3,5},{4,2},{5,3},{6,0},{7,1},{8,14},{9,15},{10,... | collective-permute-start | bytes 98312 | tf_op jit(solution)/shard_map/ppermute | solution.py:31
  77.6 1.5 %collective-permute-start.37 = (f32[2,32,128]{2,1,0:T(8,128)S(1)}, f32[2,32,128]{2,1,0:T(8,128)S(1)}, u32[]{:S(2)}, u32[]{:S(2)}) collective-permute-start(f32[2,32,128]{2,1,0:T(8,128)S(1)} %pad_maximum_fusion.23), channel_id=1, source_target_pairs={{0,3},{1,2},{2,1},{3,0},{4,7},{5,6},{6,5},{7,4},{8,11},{9,10},{10,... | collective-permute-start | bytes 98312 | tf_op jit(solution)/shard_map/ppermute | solution.py:31
  79.9 1.2 %collective-permute-start.38 = (f32[2,32,128]{2,1,0:T(8,128)S(1)}, f32[2,32,128]{2,1,0:T(8,128)S(1)}, u32[]{:S(2)}, u32[]{:S(2)}) collective-permute-start(f32[2,32,128]{2,1,0:T(8,128)S(1)} %pad_maximum_fusion.24), channel_id=1, source_target_pairs={{0,1},{1,0},{2,3},{3,2},{4,5},{5,4},{6,7},{7,6},{8,9},{9,8},{10,11... | collective-permute-start | bytes 98312 | tf_op jit(solution)/shard_map/ppermute | solution.py:31
  83.8 2.3 %later_level.9 = (f32[129,32,128]{2,1,0:T(8,128)S(1)}, f32[48,32,128]{2,1,0:T(8,128)}) custom-call(s32[294]{0:T(512)S(1)} %get-tuple-element.39.plan, s32[5,1,8]{2,1,0:T(1,128)S(1)} %get-tuple-element.40.peers, s32[5,1,8]{2,1,0:T(1,128)S(1)} %get-tuple-element.41.downs, s32[4,48]{1,0:T(4,128)S(1)} %get-tuple-element.42.slots, ...), custom_call_target="tpu_custom_call", output_to_operand_aliasing={{0}: (17, {})} | custom-call | tf_op jit(solution)/shard_map/later_level/pallas_call | solution.py:231
  (99 shorter events, 19.9 us)
Async XLA Ops:
  3.3 6.8 %collective-permute-start = (f32[4,32,128]{2,1,0:T(8,128)S(1)}, f32[4,32,128]{2,1,0:T(8,128)S(1)}, u32[]{:S(2)}, u32[]{:S(2)}) collective-permute-start(f32[4,32,128]{2,1,0:T(8,128)S(1)} %get-tuple-element.47), channel_id=1, source_target_pairs={{0,8},{1,9},{2,10},{3,11},{4,12},{5,13},{6,14},{7,15},{8,16},{9,17... | collective-permute-start | bytes 196616 | tf_op jit(solution)/shard_map/ppermute | solution.py:31
  3.8 6.3 %collective-permute-start.1 = (f32[4,32,128]{2,1,0:T(8,128)S(1)}, f32[4,32,128]{2,1,0:T(8,128)S(1)}, u32[]{:S(2)}, u32[]{:S(2)}) collective-permute-start(f32[4,32,128]{2,1,0:T(8,128)S(1)} %get-tuple-element.48), channel_id=1, source_target_pairs={{0,9},{1,8},{2,11},{3,10},{4,13},{5,12},{6,15},{7,14},{8,17},{9,16... | collective-permute-start | bytes 196616 | tf_op jit(solution)/shard_map/ppermute | solution.py:31
  7.5 6.7 %collective-permute-start.4 = (f32[4,32,128]{2,1,0:T(8,128)S(1)}, f32[4,32,128]{2,1,0:T(8,128)S(1)}, u32[]{:S(2)}, u32[]{:S(2)}) collective-permute-start(f32[4,32,128]{2,1,0:T(8,128)S(1)} %get-tuple-element.50), channel_id=1, source_target_pairs={{0,4},{1,5},{2,6},{3,7},{4,0},{5,1},{6,2},{7,3},{8,12},{9,13},{10,... | collective-permute-start | bytes 196616 | tf_op jit(solution)/shard_map/ppermute | solution.py:31
  10.2 7.6 %collective-permute-start.2 = (f32[2,32,128]{2,1,0:T(8,128)S(1)}, f32[2,32,128]{2,1,0:T(8,128)S(1)}, u32[]{:S(2)}, u32[]{:S(2)}) collective-permute-start(f32[2,32,128]{2,1,0:T(8,128)S(1)} %pad_maximum_fusion.5), channel_id=1, source_target_pairs={{0,6},{1,7},{2,4},{3,5},{4,2},{5,3},{6,0},{7,1},{8,14},{9,15},{10,... | collective-permute-start | bytes 98312 | tf_op jit(solution)/shard_map/ppermute | solution.py:31
  13.2 4.8 %collective-permute-start.3 = (f32[2,32,128]{2,1,0:T(8,128)S(1)}, f32[2,32,128]{2,1,0:T(8,128)S(1)}, u32[]{:S(2)}, u32[]{:S(2)}) collective-permute-start(f32[2,32,128]{2,1,0:T(8,128)S(1)} %pad_maximum_fusion.6), channel_id=1, source_target_pairs={{0,4},{1,5},{2,6},{3,7},{4,0},{5,1},{6,2},{7,3},{8,12},{9,13},{10,... | collective-permute-start | bytes 98312 | tf_op jit(solution)/shard_map/ppermute | solution.py:31
  14.2 5.1 %collective-permute-start.5 = (f32[2,32,128]{2,1,0:T(8,128)S(1)}, f32[2,32,128]{2,1,0:T(8,128)S(1)}, u32[]{:S(2)}, u32[]{:S(2)}) collective-permute-start(f32[2,32,128]{2,1,0:T(8,128)S(1)} %pad_maximum_fusion.7), channel_id=1, source_target_pairs={{0,3},{1,2},{2,1},{3,0},{4,7},{5,6},{6,5},{7,4},{8,11},{9,10},{10,... | collective-permute-start | bytes 98312 | tf_op jit(solution)/shard_map/ppermute | solution.py:31
  15.0 5.2 %collective-permute-start.7 = (f32[4,32,128]{2,1,0:T(8,128)S(1)}, f32[4,32,128]{2,1,0:T(8,128)S(1)}, u32[]{:S(2)}, u32[]{:S(2)}) collective-permute-start(f32[4,32,128]{2,1,0:T(8,128)S(1)} %pad_maximum_fusion), channel_id=1, source_target_pairs={{0,2},{1,3},{2,0},{3,1},{4,6},{5,7},{6,4},{7,5},{8,10},{9,11},{10,... | collective-permute-start | bytes 196616 | tf_op jit(solution)/shard_map/ppermute | solution.py:31
  21.4 4.7 %collective-permute-start.8 = (f32[4,32,128]{2,1,0:T(8,128)S(1)}, f32[4,32,128]{2,1,0:T(8,128)S(1)}, u32[]{:S(2)}, u32[]{:S(2)}) collective-permute-start(f32[4,32,128]{2,1,0:T(8,128)S(1)} %get-tuple-element.52), channel_id=1, source_target_pairs={{0,8},{1,9},{2,10},{3,11},{4,12},{5,13},{6,14},{7,15},{8,16},{9,17... | collective-permute-start | bytes 196616 | tf_op jit(solution)/shard_map/ppermute | solution.py:31
  21.5 4.6 %collective-permute-start.9 = (f32[4,32,128]{2,1,0:T(8,128)S(1)}, f32[4,32,128]{2,1,0:T(8,128)S(1)}, u32[]{:S(2)}, u32[]{:S(2)}) collective-permute-start(f32[4,32,128]{2,1,0:T(8,128)S(1)} %get-tuple-element.53), channel_id=1, source_target_pairs={{0,9},{1,8},{2,11},{3,10},{4,13},{5,12},{6,15},{7,14},{8,17},{9,16... | collective-permute-start | bytes 196616 | tf_op jit(solution)/shard_map/ppermute | solution.py:31
  23.2 6.7 %collective-permute-start.12 = (f32[4,32,128]{2,1,0:T(8,128)S(1)}, f32[4,32,128]{2,1,0:T(8,128)S(1)}, u32[]{:S(2)}, u32[]{:S(2)}) collective-permute-start(f32[4,32,128]{2,1,0:T(8,128)S(1)} %get-tuple-element.55), channel_id=1, source_target_pairs={{0,4},{1,5},{2,6},{3,7},{4,0},{5,1},{6,2},{7,3},{8,12},{9,13},{10,... | collective-permute-start | bytes 196616 | tf_op jit(solution)/shard_map/ppermute | solution.py:31
  26.2 7.4 %collective-permute-start.10 = (f32[2,32,128]{2,1,0:T(8,128)S(1)}, f32[2,32,128]{2,1,0:T(8,128)S(1)}, u32[]{:S(2)}, u32[]{:S(2)}) collective-permute-start(f32[2,32,128]{2,1,0:T(8,128)S(1)} %pad_maximum_fusion.9), channel_id=1, source_target_pairs={{0,6},{1,7},{2,4},{3,5},{4,2},{5,3},{6,0},{7,1},{8,14},{9,15},{10,... | collective-permute-start | bytes 98312 | tf_op jit(solution)/shard_map/ppermute | solution.py:31
  29.9 4.8 %collective-permute-start.11 = (f32[2,32,128]{2,1,0:T(8,128)S(1)}, f32[2,32,128]{2,1,0:T(8,128)S(1)}, u32[]{:S(2)}, u32[]{:S(2)}) collective-permute-start(f32[2,32,128]{2,1,0:T(8,128)S(1)} %pad_maximum_fusion.10), channel_id=1, source_target_pairs={{0,4},{1,5},{2,6},{3,7},{4,0},{5,1},{6,2},{7,3},{8,12},{9,13},{10,... | collective-permute-start | bytes 98312 | tf_op jit(solution)/shard_map/ppermute | solution.py:31
  30.0 5.2 %collective-permute-start.13 = (f32[2,32,128]{2,1,0:T(8,128)S(1)}, f32[2,32,128]{2,1,0:T(8,128)S(1)}, u32[]{:S(2)}, u32[]{:S(2)}) collective-permute-start(f32[2,32,128]{2,1,0:T(8,128)S(1)} %pad_maximum_fusion.11), channel_id=1, source_target_pairs={{0,3},{1,2},{2,1},{3,0},{4,7},{5,6},{6,5},{7,4},{8,11},{9,10},{10,... | collective-permute-start | bytes 98312 | tf_op jit(solution)/shard_map/ppermute | solution.py:31
  31.7 5.0 %collective-permute-start.15 = (f32[4,32,128]{2,1,0:T(8,128)S(1)}, f32[4,32,128]{2,1,0:T(8,128)S(1)}, u32[]{:S(2)}, u32[]{:S(2)}) collective-permute-start(f32[4,32,128]{2,1,0:T(8,128)S(1)} %pad_maximum_fusion.1), channel_id=1, source_target_pairs={{0,2},{1,3},{2,0},{3,1},{4,6},{5,7},{6,4},{7,5},{8,10},{9,11},{10,... | collective-permute-start | bytes 196616 | tf_op jit(solution)/shard_map/ppermute | solution.py:31
  38.0 4.6 %collective-permute-start.17 = (f32[4,32,128]{2,1,0:T(8,128)S(1)}, f32[4,32,128]{2,1,0:T(8,128)S(1)}, u32[]{:S(2)}, u32[]{:S(2)}) collective-permute-start(f32[4,32,128]{2,1,0:T(8,128)S(1)} %get-tuple-element.58), channel_id=1, source_target_pairs={{0,9},{1,8},{2,11},{3,10},{4,13},{5,12},{6,15},{7,14},{8,17},{9,16... | collective-permute-start | bytes 196616 | tf_op jit(solution)/shard_map/ppermute | solution.py:31
  39.5 6.2 %collective-permute-start.20 = (f32[4,32,128]{2,1,0:T(8,128)S(1)}, f32[4,32,128]{2,1,0:T(8,128)S(1)}, u32[]{:S(2)}, u32[]{:S(2)}) collective-permute-start(f32[4,32,128]{2,1,0:T(8,128)S(1)} %get-tuple-element.60), channel_id=1, source_target_pairs={{0,4},{1,5},{2,6},{3,7},{4,0},{5,1},{6,2},{7,3},{8,12},{9,13},{10,... | collective-permute-start | bytes 196616 | tf_op jit(solution)/shard_map/ppermute | solution.py:31
  42.6 6.7 %collective-permute-start.18 = (f32[2,32,128]{2,1,0:T(8,128)S(1)}, f32[2,32,128]{2,1,0:T(8,128)S(1)}, u32[]{:S(2)}, u32[]{:S(2)}) collective-permute-start(f32[2,32,128]{2,1,0:T(8,128)S(1)} %pad_maximum_fusion.13), channel_id=1, source_target_pairs={{0,6},{1,7},{2,4},{3,5},{4,2},{5,3},{6,0},{7,1},{8,14},{9,15},{10,... | collective-permute-start | bytes 98312 | tf_op jit(solution)/shard_map/ppermute | solution.py:31
  45.6 5.2 %collective-permute-start.19 = (f32[2,32,128]{2,1,0:T(8,128)S(1)}, f32[2,32,128]{2,1,0:T(8,128)S(1)}, u32[]{:S(2)}, u32[]{:S(2)}) collective-permute-start(f32[2,32,128]{2,1,0:T(8,128)S(1)} %pad_maximum_fusion.14), channel_id=1, source_target_pairs={{0,4},{1,5},{2,6},{3,7},{4,0},{5,1},{6,2},{7,3},{8,12},{9,13},{10,... | collective-permute-start | bytes 98312 | tf_op jit(solution)/shard_map/ppermute | solution.py:31
  45.7 5.5 %collective-permute-start.21 = (f32[2,32,128]{2,1,0:T(8,128)S(1)}, f32[2,32,128]{2,1,0:T(8,128)S(1)}, u32[]{:S(2)}, u32[]{:S(2)}) collective-permute-start(f32[2,32,128]{2,1,0:T(8,128)S(1)} %pad_maximum_fusion.15), channel_id=1, source_target_pairs={{0,3},{1,2},{2,1},{3,0},{4,7},{5,6},{6,5},{7,4},{8,11},{9,10},{10,... | collective-permute-start | bytes 98312 | tf_op jit(solution)/shard_map/ppermute | solution.py:31
  47.4 4.7 %collective-permute-start.23 = (f32[4,32,128]{2,1,0:T(8,128)S(1)}, f32[4,32,128]{2,1,0:T(8,128)S(1)}, u32[]{:S(2)}, u32[]{:S(2)}) collective-permute-start(f32[4,32,128]{2,1,0:T(8,128)S(1)} %pad_maximum_fusion.2), channel_id=1, source_target_pairs={{0,2},{1,3},{2,0},{3,1},{4,6},{5,7},{6,4},{7,5},{8,10},{9,11},{10,... | collective-permute-start | bytes 196616 | tf_op jit(solution)/shard_map/ppermute | solution.py:31
  53.4 4.6 %collective-permute-start.25 = (f32[4,32,128]{2,1,0:T(8,128)S(1)}, f32[4,32,128]{2,1,0:T(8,128)S(1)}, u32[]{:S(2)}, u32[]{:S(2)}) collective-permute-start(f32[4,32,128]{2,1,0:T(8,128)S(1)} %get-tuple-element.63), channel_id=1, source_target_pairs={{0,9},{1,8},{2,11},{3,10},{4,13},{5,12},{6,15},{7,14},{8,17},{9,16... | collective-permute-start | bytes 196616 | tf_op jit(solution)/shard_map/ppermute | solution.py:31
  55.5 6.2 %collective-permute-start.28 = (f32[4,32,128]{2,1,0:T(8,128)S(1)}, f32[4,32,128]{2,1,0:T(8,128)S(1)}, u32[]{:S(2)}, u32[]{:S(2)}) collective-permute-start(f32[4,32,128]{2,1,0:T(8,128)S(1)} %get-tuple-element.65), channel_id=1, source_target_pairs={{0,4},{1,5},{2,6},{3,7},{4,0},{5,1},{6,2},{7,3},{8,12},{9,13},{10,... | collective-permute-start | bytes 196616 | tf_op jit(solution)/shard_map/ppermute | solution.py:31
  58.1 7.1 %collective-permute-start.26 = (f32[2,32,128]{2,1,0:T(8,128)S(1)}, f32[2,32,128]{2,1,0:T(8,128)S(1)}, u32[]{:S(2)}, u32[]{:S(2)}) collective-permute-start(f32[2,32,128]{2,1,0:T(8,128)S(1)} %pad_maximum_fusion.17), channel_id=1, source_target_pairs={{0,6},{1,7},{2,4},{3,5},{4,2},{5,3},{6,0},{7,1},{8,14},{9,15},{10,... | collective-permute-start | bytes 98312 | tf_op jit(solution)/shard_map/ppermute | solution.py:31
  61.2 4.8 %collective-permute-start.27 = (f32[2,32,128]{2,1,0:T(8,128)S(1)}, f32[2,32,128]{2,1,0:T(8,128)S(1)}, u32[]{:S(2)}, u32[]{:S(2)}) collective-permute-start(f32[2,32,128]{2,1,0:T(8,128)S(1)} %pad_maximum_fusion.18), channel_id=1, source_target_pairs={{0,4},{1,5},{2,6},{3,7},{4,0},{5,1},{6,2},{7,3},{8,12},{9,13},{10,... | collective-permute-start | bytes 98312 | tf_op jit(solution)/shard_map/ppermute | solution.py:31
  61.7 5.6 %collective-permute-start.29 = (f32[2,32,128]{2,1,0:T(8,128)S(1)}, f32[2,32,128]{2,1,0:T(8,128)S(1)}, u32[]{:S(2)}, u32[]{:S(2)}) collective-permute-start(f32[2,32,128]{2,1,0:T(8,128)S(1)} %pad_maximum_fusion.19), channel_id=1, source_target_pairs={{0,3},{1,2},{2,1},{3,0},{4,7},{5,6},{6,5},{7,4},{8,11},{9,10},{10,... | collective-permute-start | bytes 98312 | tf_op jit(solution)/shard_map/ppermute | solution.py:31
  63.2 5.2 %collective-permute-start.31 = (f32[4,32,128]{2,1,0:T(8,128)S(1)}, f32[4,32,128]{2,1,0:T(8,128)S(1)}, u32[]{:S(2)}, u32[]{:S(2)}) collective-permute-start(f32[4,32,128]{2,1,0:T(8,128)S(1)} %pad_maximum_fusion.3), channel_id=1, source_target_pairs={{0,2},{1,3},{2,0},{3,1},{4,6},{5,7},{6,4},{7,5},{8,10},{9,11},{10,... | collective-permute-start | bytes 196616 | tf_op jit(solution)/shard_map/ppermute | solution.py:31
  69.7 4.6 %collective-permute-start.33 = (f32[4,32,128]{2,1,0:T(8,128)S(1)}, f32[4,32,128]{2,1,0:T(8,128)S(1)}, u32[]{:S(2)}, u32[]{:S(2)}) collective-permute-start(f32[4,32,128]{2,1,0:T(8,128)S(1)} %get-tuple-element.68), channel_id=1, source_target_pairs={{0,9},{1,8},{2,11},{3,10},{4,13},{5,12},{6,15},{7,14},{8,17},{9,16... | collective-permute-start | bytes 196616 | tf_op jit(solution)/shard_map/ppermute | solution.py:31
  71.2 6.4 %collective-permute-start.36 = (f32[4,32,128]{2,1,0:T(8,128)S(1)}, f32[4,32,128]{2,1,0:T(8,128)S(1)}, u32[]{:S(2)}, u32[]{:S(2)}) collective-permute-start(f32[4,32,128]{2,1,0:T(8,128)S(1)} %get-tuple-element.70), channel_id=1, source_target_pairs={{0,4},{1,5},{2,6},{3,7},{4,0},{5,1},{6,2},{7,3},{8,12},{9,13},{10,... | collective-permute-start | bytes 196616 | tf_op jit(solution)/shard_map/ppermute | solution.py:31
  74.4 6.8 %collective-permute-start.34 = (f32[2,32,128]{2,1,0:T(8,128)S(1)}, f32[2,32,128]{2,1,0:T(8,128)S(1)}, u32[]{:S(2)}, u32[]{:S(2)}) collective-permute-start(f32[2,32,128]{2,1,0:T(8,128)S(1)} %pad_maximum_fusion.21), channel_id=1, source_target_pairs={{0,6},{1,7},{2,4},{3,5},{4,2},{5,3},{6,0},{7,1},{8,14},{9,15},{10,... | collective-permute-start | bytes 98312 | tf_op jit(solution)/shard_map/ppermute | solution.py:31
  77.3 4.9 %collective-permute-start.35 = (f32[2,32,128]{2,1,0:T(8,128)S(1)}, f32[2,32,128]{2,1,0:T(8,128)S(1)}, u32[]{:S(2)}, u32[]{:S(2)}) collective-permute-start(f32[2,32,128]{2,1,0:T(8,128)S(1)} %pad_maximum_fusion.22), channel_id=1, source_target_pairs={{0,4},{1,5},{2,6},{3,7},{4,0},{5,1},{6,2},{7,3},{8,12},{9,13},{10,... | collective-permute-start | bytes 98312 | tf_op jit(solution)/shard_map/ppermute | solution.py:31
  77.6 5.4 %collective-permute-start.37 = (f32[2,32,128]{2,1,0:T(8,128)S(1)}, f32[2,32,128]{2,1,0:T(8,128)S(1)}, u32[]{:S(2)}, u32[]{:S(2)}) collective-permute-start(f32[2,32,128]{2,1,0:T(8,128)S(1)} %pad_maximum_fusion.23), channel_id=1, source_target_pairs={{0,3},{1,2},{2,1},{3,0},{4,7},{5,6},{6,5},{7,4},{8,11},{9,10},{10,... | collective-permute-start | bytes 98312 | tf_op jit(solution)/shard_map/ppermute | solution.py:31
  79.1 4.7 %collective-permute-start.39 = (f32[4,32,128]{2,1,0:T(8,128)S(1)}, f32[4,32,128]{2,1,0:T(8,128)S(1)}, u32[]{:S(2)}, u32[]{:S(2)}) collective-permute-start(f32[4,32,128]{2,1,0:T(8,128)S(1)} %pad_maximum_fusion.4), channel_id=1, source_target_pairs={{0,2},{1,3},{2,0},{3,1},{4,6},{5,7},{6,4},{7,5},{8,10},{9,11},{10,... | collective-permute-start | bytes 196616 | tf_op jit(solution)/shard_map/ppermute | solution.py:31
  (8 other events, 32.5 us)

commit v4 on v2

--- a/solution.py
+++ b/solution.py
@@ -72,7 +72,7 @@
     solved = []
     for block in ids:
         mixed = jnp.dot(
-            kin[block], inflow_of(block), precision=lax.Precision.HIGHEST, preferred_element_type=jnp.float32
+            kin[block], inflow_of(block), precision=lax.Precision.HIGH, preferred_element_type=jnp.float32
         )
         solved.append(weight[pl.ds(block, 1), :] * mixed)
     for block, value in zip(ids, solved):

time: 85.2 us -> 84.3 us (0.989)
  Pallas kernels: 9.47 us -> 8.55 us
where the time goes in v4:
time: 84.3 us; the launch traced here: 84.1 us
  starting transfers between devices  58.2 us (69%)
  waiting for transfers between devices  17 us (20%)
  Pallas kernels  8.55 us (10%)
    ppermute x40, starting transfers between devices, moved(): return lax.ppermute(value, ('section', 'blk'), pairs)  58.2 us
    ppermute x40, waiting for transfers between devices, moved(): return lax.ppermute(value, ('section', 'blk'), pairs)  17 us
    pallas_call x5, Pallas kernels, shards(): pl.pallas_call(functools.partial(later_level, level, rows, columns), in_s...  6.3 us
    pallas_call x1, Pallas kernels, shards(): pl.pallas_call(functools.partial(first_level, rows, columns), in_specs=[h...  2.25 us
  transfers between devices with their start and end apart: 40, of which 22 were waited for; matrix products, arithmetic and copies ran while one was open for 0% of the time, Pallas kernels for 0%

profile of v4, /device:TPU:0, one launch (start us, length us, event | category | flops | bytes accessed | tf_op | source)
XLA Modules:
  0.0 84.1 jit_solution(1765883857800784209)
XLA Ops:
  0.0 2.3 %first_level.1 = (f32[129,32,128]{2,1,0:T(8,128)S(1)}, f32[48,32,32]{2,1,0:T(8,128)S(1)}, s32[294]{0:T(512)S(1)}, s32[5,1,8]{2,1,0:T(1,128)S(1)}, s32[5,1,8]{2,1...) custom-call(s32[48]{0:T(128)} %refs_0_.1, ...), custom_call_target="tpu_custom_call" | custom-call | tf_op jit(solution)/shard_map/first_level/pallas_call | solution.py:192
  2.8 3.7 %collective-permute-start.1 = (f32[4,32,128]{2,1,0:T(8,128)S(1)}, f32[4,32,128]{2,1,0:T(8,128)S(1)}, u32[]{:S(2)}, u32[]{:S(2)}) collective-permute-start(f32[4,32,128]{2,1,0:T(8,128)S(1)} %get-tuple-element.48), channel_id=1, source_target_pairs={{0,9},{1,8},{2,11},{3,10},{4,13},{5,12},{6,15},{7,14},{8,17},{9,16... | collective-permute-start | bytes 196616 | tf_op jit(solution)/shard_map/ppermute | solution.py:31
  6.5 2.6 %collective-permute-start.4 = (f32[4,32,128]{2,1,0:T(8,128)S(1)}, f32[4,32,128]{2,1,0:T(8,128)S(1)}, u32[]{:S(2)}, u32[]{:S(2)}) collective-permute-start(f32[4,32,128]{2,1,0:T(8,128)S(1)} %get-tuple-element.50), channel_id=1, source_target_pairs={{0,4},{1,5},{2,6},{3,7},{4,0},{5,1},{6,2},{7,3},{8,12},{9,13},{10,... | collective-permute-start | bytes 196616 | tf_op jit(solution)/shard_map/ppermute | solution.py:31
  9.1 3.0 %collective-permute-start.2 = (f32[2,32,128]{2,1,0:T(8,128)S(1)}, f32[2,32,128]{2,1,0:T(8,128)S(1)}, u32[]{:S(2)}, u32[]{:S(2)}) collective-permute-start(f32[2,32,128]{2,1,0:T(8,128)S(1)} %pad_maximum_fusion.5), channel_id=1, source_target_pairs={{0,6},{1,7},{2,4},{3,5},{4,2},{5,3},{6,0},{7,1},{8,14},{9,15},{10,... | collective-permute-start | bytes 98312 | tf_op jit(solution)/shard_map/ppermute | solution.py:31
  13.9 1.3 %collective-permute-start.7 = (f32[4,32,128]{2,1,0:T(8,128)S(1)}, f32[4,32,128]{2,1,0:T(8,128)S(1)}, u32[]{:S(2)}, u32[]{:S(2)}) collective-permute-start(f32[4,32,128]{2,1,0:T(8,128)S(1)} %pad_maximum_fusion), channel_id=1, source_target_pairs={{0,2},{1,3},{2,0},{3,1},{4,6},{5,7},{6,4},{7,5},{8,10},{9,11},{10,... | collective-permute-start | bytes 196616 | tf_op jit(solution)/shard_map/ppermute | solution.py:31
  15.2 1.6 %collective-permute-start.6 = (f32[2,32,128]{2,1,0:T(8,128)S(1)}, f32[2,32,128]{2,1,0:T(8,128)S(1)}, u32[]{:S(2)}, u32[]{:S(2)}) collective-permute-start(f32[2,32,128]{2,1,0:T(8,128)S(1)} %pad_maximum_fusion.8), channel_id=1, source_target_pairs={{0,1},{1,0},{2,3},{3,2},{4,5},{5,4},{6,7},{7,6},{8,9},{9,8},{10,11... | collective-permute-start | bytes 98312 | tf_op jit(solution)/shard_map/ppermute | solution.py:31
  16.9 1.3 %collective-permute-done.5.refs_2_ = f32[2,32,128]{2,1,0:T(8,128)S(1)} collective-permute-done((f32[2,32,128]{2,1,0:T(8,128)S(1)}, f32[2,32,128]{2,1,0:T(8,128)S(1)}, u32[]{:S(2)}, u32[]{:S(2)}) %collective-permute-start.5) | collective-permute-done | bytes 32800 | tf_op jit(solution)/shard_map/ppermute | solution.py:31
  20.3 1.7 %collective-permute-start.9 = (f32[4,32,128]{2,1,0:T(8,128)S(1)}, f32[4,32,128]{2,1,0:T(8,128)S(1)}, u32[]{:S(2)}, u32[]{:S(2)}) collective-permute-start(f32[4,32,128]{2,1,0:T(8,128)S(1)} %get-tuple-element.53), channel_id=1, source_target_pairs={{0,9},{1,8},{2,11},{3,10},{4,13},{5,12},{6,15},{7,14},{8,17},{9,16... | collective-permute-start | bytes 196616 | tf_op jit(solution)/shard_map/ppermute | solution.py:31
  22.0 2.9 %collective-permute-start.12 = (f32[4,32,128]{2,1,0:T(8,128)S(1)}, f32[4,32,128]{2,1,0:T(8,128)S(1)}, u32[]{:S(2)}, u32[]{:S(2)}) collective-permute-start(f32[4,32,128]{2,1,0:T(8,128)S(1)} %get-tuple-element.55), channel_id=1, source_target_pairs={{0,4},{1,5},{2,6},{3,7},{4,0},{5,1},{6,2},{7,3},{8,12},{9,13},{10,... | collective-permute-start | bytes 196616 | tf_op jit(solution)/shard_map/ppermute | solution.py:31
  25.0 3.8 %collective-permute-start.10 = (f32[2,32,128]{2,1,0:T(8,128)S(1)}, f32[2,32,128]{2,1,0:T(8,128)S(1)}, u32[]{:S(2)}, u32[]{:S(2)}) collective-permute-start(f32[2,32,128]{2,1,0:T(8,128)S(1)} %pad_maximum_fusion.9), channel_id=1, source_target_pairs={{0,6},{1,7},{2,4},{3,5},{4,2},{5,3},{6,0},{7,1},{8,14},{9,15},{10,... | collective-permute-start | bytes 98312 | tf_op jit(solution)/shard_map/ppermute | solution.py:31
  28.8 1.7 %collective-permute-start.13 = (f32[2,32,128]{2,1,0:T(8,128)S(1)}, f32[2,32,128]{2,1,0:T(8,128)S(1)}, u32[]{:S(2)}, u32[]{:S(2)}) collective-permute-start(f32[2,32,128]{2,1,0:T(8,128)S(1)} %pad_maximum_fusion.11), channel_id=1, source_target_pairs={{0,3},{1,2},{2,1},{3,0},{4,7},{5,6},{6,5},{7,4},{8,11},{9,10},{10,... | collective-permute-start | bytes 98312 | tf_op jit(solution)/shard_map/ppermute | solution.py:31
  32.3 1.2 %collective-permute-done.11.refs_1_ = f32[2,32,128]{2,1,0:T(8,128)S(1)} collective-permute-done((f32[2,32,128]{2,1,0:T(8,128)S(1)}, f32[2,32,128]{2,1,0:T(8,128)S(1)}, u32[]{:S(2)}, u32[]{:S(2)}) %collective-permute-start.11) | collective-permute-done | bytes 32800 | tf_op jit(solution)/shard_map/ppermute | solution.py:31
  33.9 1.5 %collective-permute-done.14.refs_3_ = f32[2,32,128]{2,1,0:T(8,128)S(1)} collective-permute-done((f32[2,32,128]{2,1,0:T(8,128)S(1)}, f32[2,32,128]{2,1,0:T(8,128)S(1)}, u32[]{:S(2)}, u32[]{:S(2)}) %collective-permute-start.14) | collective-permute-done | bytes 32800 | tf_op jit(solution)/shard_map/ppermute | solution.py:31
  36.6 1.6 %collective-permute-start.17 = (f32[4,32,128]{2,1,0:T(8,128)S(1)}, f32[4,32,128]{2,1,0:T(8,128)S(1)}, u32[]{:S(2)}, u32[]{:S(2)}) collective-permute-start(f32[4,32,128]{2,1,0:T(8,128)S(1)} %get-tuple-element.58), channel_id=1, source_target_pairs={{0,9},{1,8},{2,11},{3,10},{4,13},{5,12},{6,15},{7,14},{8,17},{9,16... | collective-permute-start | bytes 196616 | tf_op jit(solution)/shard_map/ppermute | solution.py:31
  38.2 2.3 %collective-permute-start.20 = (f32[4,32,128]{2,1,0:T(8,128)S(1)}, f32[4,32,128]{2,1,0:T(8,128)S(1)}, u32[]{:S(2)}, u32[]{:S(2)}) collective-permute-start(f32[4,32,128]{2,1,0:T(8,128)S(1)} %get-tuple-element.60), channel_id=1, source_target_pairs={{0,4},{1,5},{2,6},{3,7},{4,0},{5,1},{6,2},{7,3},{8,12},{9,13},{10,... | collective-permute-start | bytes 196616 | tf_op jit(solution)/shard_map/ppermute | solution.py:31
  41.2 3.0 %collective-permute-start.18 = (f32[2,32,128]{2,1,0:T(8,128)S(1)}, f32[2,32,128]{2,1,0:T(8,128)S(1)}, u32[]{:S(2)}, u32[]{:S(2)}) collective-permute-start(f32[2,32,128]{2,1,0:T(8,128)S(1)} %pad_maximum_fusion.13), channel_id=1, source_target_pairs={{0,6},{1,7},{2,4},{3,5},{4,2},{5,3},{6,0},{7,1},{8,14},{9,15},{10,... | collective-permute-start | bytes 98312 | tf_op jit(solution)/shard_map/ppermute | solution.py:31
  44.4 1.7 %collective-permute-start.21 = (f32[2,32,128]{2,1,0:T(8,128)S(1)}, f32[2,32,128]{2,1,0:T(8,128)S(1)}, u32[]{:S(2)}, u32[]{:S(2)}) collective-permute-start(f32[2,32,128]{2,1,0:T(8,128)S(1)} %pad_maximum_fusion.15), channel_id=1, source_target_pairs={{0,3},{1,2},{2,1},{3,0},{4,7},{5,6},{6,5},{7,4},{8,11},{9,10},{10,... | collective-permute-start | bytes 98312 | tf_op jit(solution)/shard_map/ppermute | solution.py:31
  46.8 1.1 %collective-permute-start.22 = (f32[2,32,128]{2,1,0:T(8,128)S(1)}, f32[2,32,128]{2,1,0:T(8,128)S(1)}, u32[]{:S(2)}, u32[]{:S(2)}) collective-permute-start(f32[2,32,128]{2,1,0:T(8,128)S(1)} %pad_maximum_fusion.16), channel_id=1, source_target_pairs={{0,1},{1,0},{2,3},{3,2},{4,5},{5,4},{6,7},{7,6},{8,9},{9,8},{10,11... | collective-permute-start | bytes 98312 | tf_op jit(solution)/shard_map/ppermute | solution.py:31
  48.0 1.4 %collective-permute-done.19.refs_1_ = f32[2,32,128]{2,1,0:T(8,128)S(1)} collective-permute-done((f32[2,32,128]{2,1,0:T(8,128)S(1)}, f32[2,32,128]{2,1,0:T(8,128)S(1)}, u32[]{:S(2)}, u32[]{:S(2)}) %collective-permute-start.19) | collective-permute-done | bytes 32800 | tf_op jit(solution)/shard_map/ppermute | solution.py:31
  51.9 2.0 %collective-permute-start.25 = (f32[4,32,128]{2,1,0:T(8,128)S(1)}, f32[4,32,128]{2,1,0:T(8,128)S(1)}, u32[]{:S(2)}, u32[]{:S(2)}) collective-permute-start(f32[4,32,128]{2,1,0:T(8,128)S(1)} %get-tuple-element.63), channel_id=1, source_target_pairs={{0,9},{1,8},{2,11},{3,10},{4,13},{5,12},{6,15},{7,14},{8,17},{9,16... | collective-permute-start | bytes 196616 | tf_op jit(solution)/shard_map/ppermute | solution.py:31
  53.9 2.5 %collective-permute-start.28 = (f32[4,32,128]{2,1,0:T(8,128)S(1)}, f32[4,32,128]{2,1,0:T(8,128)S(1)}, u32[]{:S(2)}, u32[]{:S(2)}) collective-permute-start(f32[4,32,128]{2,1,0:T(8,128)S(1)} %get-tuple-element.65), channel_id=1, source_target_pairs={{0,4},{1,5},{2,6},{3,7},{4,0},{5,1},{6,2},{7,3},{8,12},{9,13},{10,... | collective-permute-start | bytes 196616 | tf_op jit(solution)/shard_map/ppermute | solution.py:31
  56.6 3.2 %collective-permute-start.26 = (f32[2,32,128]{2,1,0:T(8,128)S(1)}, f32[2,32,128]{2,1,0:T(8,128)S(1)}, u32[]{:S(2)}, u32[]{:S(2)}) collective-permute-start(f32[2,32,128]{2,1,0:T(8,128)S(1)} %pad_maximum_fusion.17), channel_id=1, source_target_pairs={{0,6},{1,7},{2,4},{3,5},{4,2},{5,3},{6,0},{7,1},{8,14},{9,15},{10,... | collective-permute-start | bytes 98312 | tf_op jit(solution)/shard_map/ppermute | solution.py:31
  60.1 1.5 %collective-permute-start.29 = (f32[2,32,128]{2,1,0:T(8,128)S(1)}, f32[2,32,128]{2,1,0:T(8,128)S(1)}, u32[]{:S(2)}, u32[]{:S(2)}) collective-permute-start(f32[2,32,128]{2,1,0:T(8,128)S(1)} %pad_maximum_fusion.19), channel_id=1, source_target_pairs={{0,3},{1,2},{2,1},{3,0},{4,7},{5,6},{6,5},{7,4},{8,11},{9,10},{10,... | collective-permute-start | bytes 98312 | tf_op jit(solution)/shard_map/ppermute | solution.py:31
  61.7 1.3 %collective-permute-start.31 = (f32[4,32,128]{2,1,0:T(8,128)S(1)}, f32[4,32,128]{2,1,0:T(8,128)S(1)}, u32[]{:S(2)}, u32[]{:S(2)}) collective-permute-start(f32[4,32,128]{2,1,0:T(8,128)S(1)} %pad_maximum_fusion.3), channel_id=1, source_target_pairs={{0,2},{1,3},{2,0},{3,1},{4,6},{5,7},{6,4},{7,5},{8,10},{9,11},{10,... | collective-permute-start | bytes 196616 | tf_op jit(solution)/shard_map/ppermute | solution.py:31
  64.6 1.1 %collective-permute-done.29.refs_2_ = f32[2,32,128]{2,1,0:T(8,128)S(1)} collective-permute-done((f32[2,32,128]{2,1,0:T(8,128)S(1)}, f32[2,32,128]{2,1,0:T(8,128)S(1)}, u32[]{:S(2)}, u32[]{:S(2)}) %collective-permute-start.29) | collective-permute-done | bytes 32800 | tf_op jit(solution)/shard_map/ppermute | solution.py:31
  65.7 1.1 %collective-permute-done.30.refs_3_ = f32[2,32,128]{2,1,0:T(8,128)S(1)} collective-permute-done((f32[2,32,128]{2,1,0:T(8,128)S(1)}, f32[2,32,128]{2,1,0:T(8,128)S(1)}, u32[]{:S(2)}, u32[]{:S(2)}) %collective-permute-start.30) | collective-permute-done | bytes 32800 | tf_op jit(solution)/shard_map/ppermute | solution.py:31
  68.0 1.4 %collective-permute-start.33 = (f32[4,32,128]{2,1,0:T(8,128)S(1)}, f32[4,32,128]{2,1,0:T(8,128)S(1)}, u32[]{:S(2)}, u32[]{:S(2)}) collective-permute-start(f32[4,32,128]{2,1,0:T(8,128)S(1)} %get-tuple-element.68), channel_id=1, source_target_pairs={{0,9},{1,8},{2,11},{3,10},{4,13},{5,12},{6,15},{7,14},{8,17},{9,16... | collective-permute-start | bytes 196616 | tf_op jit(solution)/shard_map/ppermute | solution.py:31
  69.5 2.8 %collective-permute-start.36 = (f32[4,32,128]{2,1,0:T(8,128)S(1)}, f32[4,32,128]{2,1,0:T(8,128)S(1)}, u32[]{:S(2)}, u32[]{:S(2)}) collective-permute-start(f32[4,32,128]{2,1,0:T(8,128)S(1)} %get-tuple-element.70), channel_id=1, source_target_pairs={{0,4},{1,5},{2,6},{3,7},{4,0},{5,1},{6,2},{7,3},{8,12},{9,13},{10,... | collective-permute-start | bytes 196616 | tf_op jit(solution)/shard_map/ppermute | solution.py:31
  72.7 2.9 %collective-permute-start.34 = (f32[2,32,128]{2,1,0:T(8,128)S(1)}, f32[2,32,128]{2,1,0:T(8,128)S(1)}, u32[]{:S(2)}, u32[]{:S(2)}) collective-permute-start(f32[2,32,128]{2,1,0:T(8,128)S(1)} %pad_maximum_fusion.21), channel_id=1, source_target_pairs={{0,6},{1,7},{2,4},{3,5},{4,2},{5,3},{6,0},{7,1},{8,14},{9,15},{10,... | collective-permute-start | bytes 98312 | tf_op jit(solution)/shard_map/ppermute | solution.py:31
  75.9 1.5 %collective-permute-start.37 = (f32[2,32,128]{2,1,0:T(8,128)S(1)}, f32[2,32,128]{2,1,0:T(8,128)S(1)}, u32[]{:S(2)}, u32[]{:S(2)}) collective-permute-start(f32[2,32,128]{2,1,0:T(8,128)S(1)} %pad_maximum_fusion.23), channel_id=1, source_target_pairs={{0,3},{1,2},{2,1},{3,0},{4,7},{5,6},{6,5},{7,4},{8,11},{9,10},{10,... | collective-permute-start | bytes 98312 | tf_op jit(solution)/shard_map/ppermute | solution.py:31
  78.2 1.2 %collective-permute-start.38 = (f32[2,32,128]{2,1,0:T(8,128)S(1)}, f32[2,32,128]{2,1,0:T(8,128)S(1)}, u32[]{:S(2)}, u32[]{:S(2)}) collective-permute-start(f32[2,32,128]{2,1,0:T(8,128)S(1)} %pad_maximum_fusion.24), channel_id=1, source_target_pairs={{0,1},{1,0},{2,3},{3,2},{4,5},{5,4},{6,7},{7,6},{8,9},{9,8},{10,11... | collective-permute-start | bytes 98312 | tf_op jit(solution)/shard_map/ppermute | solution.py:31
  82.2 2.0 %later_level.9 = (f32[129,32,128]{2,1,0:T(8,128)S(1)}, f32[48,32,128]{2,1,0:T(8,128)}) custom-call(s32[294]{0:T(512)S(1)} %get-tuple-element.39.plan, s32[5,1,8]{2,1,0:T(1,128)S(1)} %get-tuple-element.40.peers, s32[5,1,8]{2,1,0:T(1,128)S(1)} %get-tuple-element.41.downs, s32[4,48]{1,0:T(4,128)S(1)} %get-tuple-element.42.slots, ...), custom_call_target="tpu_custom_call", output_to_operand_aliasing={{0}: (17, {})} | custom-call | tf_op jit(solution)/shard_map/later_level/pallas_call | solution.py:225
  (99 shorter events, 19.7 us)
Async XLA Ops:
  2.3 6.8 %collective-permute-start = (f32[4,32,128]{2,1,0:T(8,128)S(1)}, f32[4,32,128]{2,1,0:T(8,128)S(1)}, u32[]{:S(2)}, u32[]{:S(2)}) collective-permute-start(f32[4,32,128]{2,1,0:T(8,128)S(1)} %get-tuple-element.47), channel_id=1, source_target_pairs={{0,8},{1,9},{2,10},{3,11},{4,12},{5,13},{6,14},{7,15},{8,16},{9,17... | collective-permute-start | bytes 196616 | tf_op jit(solution)/shard_map/ppermute | solution.py:31
  2.8 6.3 %collective-permute-start.1 = (f32[4,32,128]{2,1,0:T(8,128)S(1)}, f32[4,32,128]{2,1,0:T(8,128)S(1)}, u32[]{:S(2)}, u32[]{:S(2)}) collective-permute-start(f32[4,32,128]{2,1,0:T(8,128)S(1)} %get-tuple-element.48), channel_id=1, source_target_pairs={{0,9},{1,8},{2,11},{3,10},{4,13},{5,12},{6,15},{7,14},{8,17},{9,16... | collective-permute-start | bytes 196616 | tf_op jit(solution)/shard_map/ppermute | solution.py:31
  6.5 6.7 %collective-permute-start.4 = (f32[4,32,128]{2,1,0:T(8,128)S(1)}, f32[4,32,128]{2,1,0:T(8,128)S(1)}, u32[]{:S(2)}, u32[]{:S(2)}) collective-permute-start(f32[4,32,128]{2,1,0:T(8,128)S(1)} %get-tuple-element.50), channel_id=1, source_target_pairs={{0,4},{1,5},{2,6},{3,7},{4,0},{5,1},{6,2},{7,3},{8,12},{9,13},{10,... | collective-permute-start | bytes 196616 | tf_op jit(solution)/shard_map/ppermute | solution.py:31
  9.1 7.6 %collective-permute-start.2 = (f32[2,32,128]{2,1,0:T(8,128)S(1)}, f32[2,32,128]{2,1,0:T(8,128)S(1)}, u32[]{:S(2)}, u32[]{:S(2)}) collective-permute-start(f32[2,32,128]{2,1,0:T(8,128)S(1)} %pad_maximum_fusion.5), channel_id=1, source_target_pairs={{0,6},{1,7},{2,4},{3,5},{4,2},{5,3},{6,0},{7,1},{8,14},{9,15},{10,... | collective-permute-start | bytes 98312 | tf_op jit(solution)/shard_map/ppermute | solution.py:31
  12.1 4.8 %collective-permute-start.3 = (f32[2,32,128]{2,1,0:T(8,128)S(1)}, f32[2,32,128]{2,1,0:T(8,128)S(1)}, u32[]{:S(2)}, u32[]{:S(2)}) collective-permute-start(f32[2,32,128]{2,1,0:T(8,128)S(1)} %pad_maximum_fusion.6), channel_id=1, source_target_pairs={{0,4},{1,5},{2,6},{3,7},{4,0},{5,1},{6,2},{7,3},{8,12},{9,13},{10,... | collective-permute-start | bytes 98312 | tf_op jit(solution)/shard_map/ppermute | solution.py:31
  13.2 5.1 %collective-permute-start.5 = (f32[2,32,128]{2,1,0:T(8,128)S(1)}, f32[2,32,128]{2,1,0:T(8,128)S(1)}, u32[]{:S(2)}, u32[]{:S(2)}) collective-permute-start(f32[2,32,128]{2,1,0:T(8,128)S(1)} %pad_maximum_fusion.7), channel_id=1, source_target_pairs={{0,3},{1,2},{2,1},{3,0},{4,7},{5,6},{6,5},{7,4},{8,11},{9,10},{10,... | collective-permute-start | bytes 98312 | tf_op jit(solution)/shard_map/ppermute | solution.py:31
  13.9 5.2 %collective-permute-start.7 = (f32[4,32,128]{2,1,0:T(8,128)S(1)}, f32[4,32,128]{2,1,0:T(8,128)S(1)}, u32[]{:S(2)}, u32[]{:S(2)}) collective-permute-start(f32[4,32,128]{2,1,0:T(8,128)S(1)} %pad_maximum_fusion), channel_id=1, source_target_pairs={{0,2},{1,3},{2,0},{3,1},{4,6},{5,7},{6,4},{7,5},{8,10},{9,11},{10,... | collective-permute-start | bytes 196616 | tf_op jit(solution)/shard_map/ppermute | solution.py:31
  20.2 4.7 %collective-permute-start.8 = (f32[4,32,128]{2,1,0:T(8,128)S(1)}, f32[4,32,128]{2,1,0:T(8,128)S(1)}, u32[]{:S(2)}, u32[]{:S(2)}) collective-permute-start(f32[4,32,128]{2,1,0:T(8,128)S(1)} %get-tuple-element.52), channel_id=1, source_target_pairs={{0,8},{1,9},{2,10},{3,11},{4,12},{5,13},{6,14},{7,15},{8,16},{9,17... | collective-permute-start | bytes 196616 | tf_op jit(solution)/shard_map/ppermute | solution.py:31
  20.3 4.7 %collective-permute-start.9 = (f32[4,32,128]{2,1,0:T(8,128)S(1)}, f32[4,32,128]{2,1,0:T(8,128)S(1)}, u32[]{:S(2)}, u32[]{:S(2)}) collective-permute-start(f32[4,32,128]{2,1,0:T(8,128)S(1)} %get-tuple-element.53), channel_id=1, source_target_pairs={{0,9},{1,8},{2,11},{3,10},{4,13},{5,12},{6,15},{7,14},{8,17},{9,16... | collective-permute-start | bytes 196616 | tf_op jit(solution)/shard_map/ppermute | solution.py:31
  22.0 6.7 %collective-permute-start.12 = (f32[4,32,128]{2,1,0:T(8,128)S(1)}, f32[4,32,128]{2,1,0:T(8,128)S(1)}, u32[]{:S(2)}, u32[]{:S(2)}) collective-permute-start(f32[4,32,128]{2,1,0:T(8,128)S(1)} %get-tuple-element.55), channel_id=1, source_target_pairs={{0,4},{1,5},{2,6},{3,7},{4,0},{5,1},{6,2},{7,3},{8,12},{9,13},{10,... | collective-permute-start | bytes 196616 | tf_op jit(solution)/shard_map/ppermute | solution.py:31
  25.0 7.4 %collective-permute-start.10 = (f32[2,32,128]{2,1,0:T(8,128)S(1)}, f32[2,32,128]{2,1,0:T(8,128)S(1)}, u32[]{:S(2)}, u32[]{:S(2)}) collective-permute-start(f32[2,32,128]{2,1,0:T(8,128)S(1)} %pad_maximum_fusion.9), channel_id=1, source_target_pairs={{0,6},{1,7},{2,4},{3,5},{4,2},{5,3},{6,0},{7,1},{8,14},{9,15},{10,... | collective-permute-start | bytes 98312 | tf_op jit(solution)/shard_map/ppermute | solution.py:31
  28.7 4.8 %collective-permute-start.11 = (f32[2,32,128]{2,1,0:T(8,128)S(1)}, f32[2,32,128]{2,1,0:T(8,128)S(1)}, u32[]{:S(2)}, u32[]{:S(2)}) collective-permute-start(f32[2,32,128]{2,1,0:T(8,128)S(1)} %pad_maximum_fusion.10), channel_id=1, source_target_pairs={{0,4},{1,5},{2,6},{3,7},{4,0},{5,1},{6,2},{7,3},{8,12},{9,13},{10,... | collective-permute-start | bytes 98312 | tf_op jit(solution)/shard_map/ppermute | solution.py:31
  28.8 5.2 %collective-permute-start.13 = (f32[2,32,128]{2,1,0:T(8,128)S(1)}, f32[2,32,128]{2,1,0:T(8,128)S(1)}, u32[]{:S(2)}, u32[]{:S(2)}) collective-permute-start(f32[2,32,128]{2,1,0:T(8,128)S(1)} %pad_maximum_fusion.11), channel_id=1, source_target_pairs={{0,3},{1,2},{2,1},{3,0},{4,7},{5,6},{6,5},{7,4},{8,11},{9,10},{10,... | collective-permute-start | bytes 98312 | tf_op jit(solution)/shard_map/ppermute | solution.py:31
  30.5 5.0 %collective-permute-start.15 = (f32[4,32,128]{2,1,0:T(8,128)S(1)}, f32[4,32,128]{2,1,0:T(8,128)S(1)}, u32[]{:S(2)}, u32[]{:S(2)}) collective-permute-start(f32[4,32,128]{2,1,0:T(8,128)S(1)} %pad_maximum_fusion.1), channel_id=1, source_target_pairs={{0,2},{1,3},{2,0},{3,1},{4,6},{5,7},{6,4},{7,5},{8,10},{9,11},{10,... | collective-permute-start | bytes 196616 | tf_op jit(solution)/shard_map/ppermute | solution.py:31
  36.6 4.6 %collective-permute-start.17 = (f32[4,32,128]{2,1,0:T(8,128)S(1)}, f32[4,32,128]{2,1,0:T(8,128)S(1)}, u32[]{:S(2)}, u32[]{:S(2)}) collective-permute-start(f32[4,32,128]{2,1,0:T(8,128)S(1)} %get-tuple-element.58), channel_id=1, source_target_pairs={{0,9},{1,8},{2,11},{3,10},{4,13},{5,12},{6,15},{7,14},{8,17},{9,16... | collective-permute-start | bytes 196616 | tf_op jit(solution)/shard_map/ppermute | solution.py:31
  38.2 6.2 %collective-permute-start.20 = (f32[4,32,128]{2,1,0:T(8,128)S(1)}, f32[4,32,128]{2,1,0:T(8,128)S(1)}, u32[]{:S(2)}, u32[]{:S(2)}) collective-permute-start(f32[4,32,128]{2,1,0:T(8,128)S(1)} %get-tuple-element.60), channel_id=1, source_target_pairs={{0,4},{1,5},{2,6},{3,7},{4,0},{5,1},{6,2},{7,3},{8,12},{9,13},{10,... | collective-permute-start | bytes 196616 | tf_op jit(solution)/shard_map/ppermute | solution.py:31
  41.2 6.7 %collective-permute-start.18 = (f32[2,32,128]{2,1,0:T(8,128)S(1)}, f32[2,32,128]{2,1,0:T(8,128)S(1)}, u32[]{:S(2)}, u32[]{:S(2)}) collective-permute-start(f32[2,32,128]{2,1,0:T(8,128)S(1)} %pad_maximum_fusion.13), channel_id=1, source_target_pairs={{0,6},{1,7},{2,4},{3,5},{4,2},{5,3},{6,0},{7,1},{8,14},{9,15},{10,... | collective-permute-start | bytes 98312 | tf_op jit(solution)/shard_map/ppermute | solution.py:31
  44.2 5.2 %collective-permute-start.19 = (f32[2,32,128]{2,1,0:T(8,128)S(1)}, f32[2,32,128]{2,1,0:T(8,128)S(1)}, u32[]{:S(2)}, u32[]{:S(2)}) collective-permute-start(f32[2,32,128]{2,1,0:T(8,128)S(1)} %pad_maximum_fusion.14), channel_id=1, source_target_pairs={{0,4},{1,5},{2,6},{3,7},{4,0},{5,1},{6,2},{7,3},{8,12},{9,13},{10,... | collective-permute-start | bytes 98312 | tf_op jit(solution)/shard_map/ppermute | solution.py:31
  44.4 5.5 %collective-permute-start.21 = (f32[2,32,128]{2,1,0:T(8,128)S(1)}, f32[2,32,128]{2,1,0:T(8,128)S(1)}, u32[]{:S(2)}, u32[]{:S(2)}) collective-permute-start(f32[2,32,128]{2,1,0:T(8,128)S(1)} %pad_maximum_fusion.15), channel_id=1, source_target_pairs={{0,3},{1,2},{2,1},{3,0},{4,7},{5,6},{6,5},{7,4},{8,11},{9,10},{10,... | collective-permute-start | bytes 98312 | tf_op jit(solution)/shard_map/ppermute | solution.py:31
  46.0 4.7 %collective-permute-start.23 = (f32[4,32,128]{2,1,0:T(8,128)S(1)}, f32[4,32,128]{2,1,0:T(8,128)S(1)}, u32[]{:S(2)}, u32[]{:S(2)}) collective-permute-start(f32[4,32,128]{2,1,0:T(8,128)S(1)} %pad_maximum_fusion.2), channel_id=1, source_target_pairs={{0,2},{1,3},{2,0},{3,1},{4,6},{5,7},{6,4},{7,5},{8,10},{9,11},{10,... | collective-permute-start | bytes 196616 | tf_op jit(solution)/shard_map/ppermute | solution.py:31
  51.9 4.6 %collective-permute-start.25 = (f32[4,32,128]{2,1,0:T(8,128)S(1)}, f32[4,32,128]{2,1,0:T(8,128)S(1)}, u32[]{:S(2)}, u32[]{:S(2)}) collective-permute-start(f32[4,32,128]{2,1,0:T(8,128)S(1)} %get-tuple-element.63), channel_id=1, source_target_pairs={{0,9},{1,8},{2,11},{3,10},{4,13},{5,12},{6,15},{7,14},{8,17},{9,16... | collective-permute-start | bytes 196616 | tf_op jit(solution)/shard_map/ppermute | solution.py:31
  53.9 6.2 %collective-permute-start.28 = (f32[4,32,128]{2,1,0:T(8,128)S(1)}, f32[4,32,128]{2,1,0:T(8,128)S(1)}, u32[]{:S(2)}, u32[]{:S(2)}) collective-permute-start(f32[4,32,128]{2,1,0:T(8,128)S(1)} %get-tuple-element.65), channel_id=1, source_target_pairs={{0,4},{1,5},{2,6},{3,7},{4,0},{5,1},{6,2},{7,3},{8,12},{9,13},{10,... | collective-permute-start | bytes 196616 | tf_op jit(solution)/shard_map/ppermute | solution.py:31
  56.6 7.1 %collective-permute-start.26 = (f32[2,32,128]{2,1,0:T(8,128)S(1)}, f32[2,32,128]{2,1,0:T(8,128)S(1)}, u32[]{:S(2)}, u32[]{:S(2)}) collective-permute-start(f32[2,32,128]{2,1,0:T(8,128)S(1)} %pad_maximum_fusion.17), channel_id=1, source_target_pairs={{0,6},{1,7},{2,4},{3,5},{4,2},{5,3},{6,0},{7,1},{8,14},{9,15},{10,... | collective-permute-start | bytes 98312 | tf_op jit(solution)/shard_map/ppermute | solution.py:31
  59.7 4.8 %collective-permute-start.27 = (f32[2,32,128]{2,1,0:T(8,128)S(1)}, f32[2,32,128]{2,1,0:T(8,128)S(1)}, u32[]{:S(2)}, u32[]{:S(2)}) collective-permute-start(f32[2,32,128]{2,1,0:T(8,128)S(1)} %pad_maximum_fusion.18), channel_id=1, source_target_pairs={{0,4},{1,5},{2,6},{3,7},{4,0},{5,1},{6,2},{7,3},{8,12},{9,13},{10,... | collective-permute-start | bytes 98312 | tf_op jit(solution)/shard_map/ppermute | solution.py:31
  60.1 5.6 %collective-permute-start.29 = (f32[2,32,128]{2,1,0:T(8,128)S(1)}, f32[2,32,128]{2,1,0:T(8,128)S(1)}, u32[]{:S(2)}, u32[]{:S(2)}) collective-permute-start(f32[2,32,128]{2,1,0:T(8,128)S(1)} %pad_maximum_fusion.19), channel_id=1, source_target_pairs={{0,3},{1,2},{2,1},{3,0},{4,7},{5,6},{6,5},{7,4},{8,11},{9,10},{10,... | collective-permute-start | bytes 98312 | tf_op jit(solution)/shard_map/ppermute | solution.py:31
  61.7 5.2 %collective-permute-start.31 = (f32[4,32,128]{2,1,0:T(8,128)S(1)}, f32[4,32,128]{2,1,0:T(8,128)S(1)}, u32[]{:S(2)}, u32[]{:S(2)}) collective-permute-start(f32[4,32,128]{2,1,0:T(8,128)S(1)} %pad_maximum_fusion.3), channel_id=1, source_target_pairs={{0,2},{1,3},{2,0},{3,1},{4,6},{5,7},{6,4},{7,5},{8,10},{9,11},{10,... | collective-permute-start | bytes 196616 | tf_op jit(solution)/shard_map/ppermute | solution.py:31
  68.0 4.6 %collective-permute-start.33 = (f32[4,32,128]{2,1,0:T(8,128)S(1)}, f32[4,32,128]{2,1,0:T(8,128)S(1)}, u32[]{:S(2)}, u32[]{:S(2)}) collective-permute-start(f32[4,32,128]{2,1,0:T(8,128)S(1)} %get-tuple-element.68), channel_id=1, source_target_pairs={{0,9},{1,8},{2,11},{3,10},{4,13},{5,12},{6,15},{7,14},{8,17},{9,16... | collective-permute-start | bytes 196616 | tf_op jit(solution)/shard_map/ppermute | solution.py:31
  69.5 6.4 %collective-permute-start.36 = (f32[4,32,128]{2,1,0:T(8,128)S(1)}, f32[4,32,128]{2,1,0:T(8,128)S(1)}, u32[]{:S(2)}, u32[]{:S(2)}) collective-permute-start(f32[4,32,128]{2,1,0:T(8,128)S(1)} %get-tuple-element.70), channel_id=1, source_target_pairs={{0,4},{1,5},{2,6},{3,7},{4,0},{5,1},{6,2},{7,3},{8,12},{9,13},{10,... | collective-permute-start | bytes 196616 | tf_op jit(solution)/shard_map/ppermute | solution.py:31
  72.7 6.8 %collective-permute-start.34 = (f32[2,32,128]{2,1,0:T(8,128)S(1)}, f32[2,32,128]{2,1,0:T(8,128)S(1)}, u32[]{:S(2)}, u32[]{:S(2)}) collective-permute-start(f32[2,32,128]{2,1,0:T(8,128)S(1)} %pad_maximum_fusion.21), channel_id=1, source_target_pairs={{0,6},{1,7},{2,4},{3,5},{4,2},{5,3},{6,0},{7,1},{8,14},{9,15},{10,... | collective-permute-start | bytes 98312 | tf_op jit(solution)/shard_map/ppermute | solution.py:31
  75.6 4.9 %collective-permute-start.35 = (f32[2,32,128]{2,1,0:T(8,128)S(1)}, f32[2,32,128]{2,1,0:T(8,128)S(1)}, u32[]{:S(2)}, u32[]{:S(2)}) collective-permute-start(f32[2,32,128]{2,1,0:T(8,128)S(1)} %pad_maximum_fusion.22), channel_id=1, source_target_pairs={{0,4},{1,5},{2,6},{3,7},{4,0},{5,1},{6,2},{7,3},{8,12},{9,13},{10,... | collective-permute-start | bytes 98312 | tf_op jit(solution)/shard_map/ppermute | solution.py:31
  75.9 5.4 %collective-permute-start.37 = (f32[2,32,128]{2,1,0:T(8,128)S(1)}, f32[2,32,128]{2,1,0:T(8,128)S(1)}, u32[]{:S(2)}, u32[]{:S(2)}) collective-permute-start(f32[2,32,128]{2,1,0:T(8,128)S(1)} %pad_maximum_fusion.23), channel_id=1, source_target_pairs={{0,3},{1,2},{2,1},{3,0},{4,7},{5,6},{6,5},{7,4},{8,11},{9,10},{10,... | collective-permute-start | bytes 98312 | tf_op jit(solution)/shard_map/ppermute | solution.py:31
  77.4 4.7 %collective-permute-start.39 = (f32[4,32,128]{2,1,0:T(8,128)S(1)}, f32[4,32,128]{2,1,0:T(8,128)S(1)}, u32[]{:S(2)}, u32[]{:S(2)}) collective-permute-start(f32[4,32,128]{2,1,0:T(8,128)S(1)} %pad_maximum_fusion.4), channel_id=1, source_target_pairs={{0,2},{1,3},{2,0},{3,1},{4,6},{5,7},{6,4},{7,5},{8,10},{9,11},{10,... | collective-permute-start | bytes 196616 | tf_op jit(solution)/shard_map/ppermute | solution.py:31
  (8 other events, 32.5 us)
